TPU v7x, 32 devices: a whole 2x2x4 slice. The times are simulated.
32 devices in a mesh: dp: 16 (over z, y, core), opt: 2 (over x).
Axes of the slice: x: 2, y: 2, z: 4, core: 2. Of those that a mesh axis runs over, the one named last changes fastest.
Arguments:
- tokens: bfloat16 [16384, 384], P(('dp', 'opt')), may hold values from -6 to 6
- segment: int32 [16384], P(('dp', 'opt')), may hold values from -1 to 3, as said below
- cotangent: bfloat16 [16384, 384], P(('dp', 'opt')), may hold values from -6 to 6
- w_attn: float32 [384, 1536], P('opt'), may hold values from -0.4375 to 0.4375
- m_attn: float32 [384, 1536], P('opt'), may hold values from -28 to 28
- v_attn: float32 [384, 1536], P('opt'), may hold values from 81.92 to 327.68
- w_mlp: float32 [384, 3072], P('opt'), may hold values from -0.3125 to 0.3125
- m_mlp: float32 [384, 3072], P('opt'), may hold values from -32 to 32
- v_mlp: float32 [384, 3072], P('opt'), may hold values from 106.496 to 425.984
- vectors: float32 [4608], P('opt'), may hold values from -0.5 to 1.5, as said below
- m_vec: float32 [4608], P('opt'), may hold values from -32 to 32
- v_vec: float32 [4608], P('opt'), may hold values from 131.072 to 524.288
Outputs:
- activations: bfloat16 [16384, 384], P(('dp', 'opt'))
- input_grad: float32 [16384, 384], P(('dp', 'opt'))
- new_attn: float32 [384, 1536], P('opt')
- first_attn: float32 [384, 1536], P('opt')
- second_attn: float32 [384, 1536], P('opt')
- new_mlp: float32 [384, 3072], P('opt')
- first_mlp: float32 [384, 3072], P('opt')
- second_mlp: float32 [384, 3072], P('opt')
- new_vec: float32 [4608], P('opt')
- first_vec: float32 [4608], P('opt')
- second_vec: float32 [4608], P('opt')
Inputs may be any that keep to these rules, and one draw needn't show every extreme that they name: `segment`: each device's 512 slots hold documents in order, numbered 0, 1, 2 and so on within the device, followed by empty slots marked -1; at least 128 slots of a device are live, and some device has all live. A document has 128 to 512 slots (the last live one of a device may have fewer), and some document has exactly 512. `vectors`: the entries of g1 and g2 lie in 0.5 to 1.5, all other entries in -0.5 to 0.5.
All inputs are finite; a program needn't handle non-finite values.
Results may differ from a plain program's by a relative error of at most 0.0095.
The roundings to bfloat16 on the way count: a program that leaves them out, or rounds other values in their place, can miss the bound.
Values may be sent and summed in bfloat16 or wider, within the bound.
No kernel may reach another device: no remote copies, remote signals or barrier semaphores. Data moves between devices by JAX's collectives and lax.ppermute only.
A program may use at most 128 MiB of HBM per device.

v0:
```python
import jax
import jax.numpy as jnp
from jax import lax
from jax.sharding import PartitionSpec as P

D = 384
HEADS = 6
HEAD_DIM = 64
FF = 1536
MAXLEN = 512
STEP = 10


norm_eps = 1e-05
beta_one = 0.9
beta_two = 0.95
adam_eps = 1e-08
matrix_rate = 0.15
vector_rate = 0.6
matrix_decay = 0.1
neg_large = -1e30


def normalize(values, gain_vec, shift_vec):
    row_mean = jnp.mean(values, axis=-1, keepdims=True)
    centred = values - row_mean
    variance = jnp.mean(centred * centred, axis=-1, keepdims=True)
    return centred * lax.rsqrt(variance + norm_eps) * gain_vec + shift_vec


def gelu_tanh(values):
    return jax.nn.gelu(values, approximate=True)


def contract_rows(left_arr, right_arr):
    return lax.dot_general(
        left_arr, right_arr, (((0,), (0,)), ((), ())), preferred_element_type=jnp.float32
    )


def contract_cols(left_arr, right_arr):
    return lax.dot_general(
        left_arr, right_arr, (((1,), (1,)), ((), ())), preferred_element_type=jnp.float32
    )


def permitted(seg_query, seg_key, pos_query, pos_key):
    same_doc = seg_query[:, None] == seg_key[None, :]
    causal = pos_key[None, :] <= pos_query[:, None]
    self_only = (seg_query[:, None] >= 0) | (pos_key[None, :] == pos_query[:, None])
    return same_doc & causal & self_only


def block_scores(query_blk, key_win, allowed, scale_qk):
    scores = (
        jnp.einsum("qhd,khd->hqk", query_blk, key_win, preferred_element_type=jnp.float32)
        * scale_qk
    )
    return jnp.where(allowed[None], scores, neg_large)


def adamw_update(weight, first_moment, second, gradient, step_rate, decay_rate):
    first_moment = beta_one * first_moment + (1.0 - beta_one) * gradient
    second = beta_two * second + (1.0 - beta_two) * gradient * gradient
    first_hat = first_moment / (1.0 - beta_one**STEP)
    second_hat = second / (1.0 - beta_two**STEP)
    weight = weight - step_rate * (
        first_hat / (jnp.sqrt(second_hat) + adam_eps) + decay_rate * weight
    )
    return (weight, first_moment, second)


def spread_matrix(gradient, groups, owners):
    row_count, col_count = gradient.shape
    shaped = gradient.reshape(owners, row_count // owners, groups, col_count // groups)
    return jnp.transpose(shaped, (2, 0, 1, 3)).reshape(groups * row_count, col_count // groups)


def spread_vector(gradient, groups, owners):
    piece_len = gradient.shape[0] // (groups * owners)
    shaped = gradient.reshape(owners, groups, piece_len)
    return jnp.transpose(shaped, (1, 0, 2)).reshape(groups * owners, piece_len)


def body(
    tokens, segment, cotangent, w_attn, m_attn, v_attn, w_mlp, m_mlp, v_mlp, vectors, m_vec, v_vec
):
    attn_full, vec_low = (
        lax.all_gather(w_attn.astype(jnp.bfloat16), "opt", axis=0, tiled=True),
        lax.all_gather(vectors.astype(jnp.bfloat16), "opt", axis=0, tiled=True),
    )
    mlp_full = lax.all_gather(w_mlp.astype(jnp.bfloat16), "opt", axis=0, tiled=True)
    groups = lax.axis_size("dp")
    owners = lax.axis_size("opt")
    row_count = tokens.shape[0]
    model_width = D
    hidden_width = FF
    head_shape = (row_count, HEADS, HEAD_DIM)
    scale_qk = HEAD_DIM ** (-0.5)
    vec_full = vec_low.astype(jnp.float32)
    pieces = [vec_full[number * model_width : (number + 1) * model_width] for number in range(8)]
    gain_one, shift_one, bias_query, bias_value, bias_out, gain_two, shift_two, bias_down = pieces
    bias_up = vec_full[8 * model_width :]
    hidden = tokens.astype(jnp.float32)
    normed_one, back_one = jax.vjp(normalize, hidden, gain_one, shift_one)
    first_in = normed_one.astype(jnp.bfloat16)
    qkv_weight = attn_full[:, : 3 * model_width]
    out_weight = attn_full[:, 3 * model_width :]
    projected = jnp.dot(first_in, qkv_weight, preferred_element_type=jnp.float32)
    query_heads = (projected[:, :model_width] + bias_query).astype(jnp.bfloat16).reshape(head_shape)
    key_heads = projected[:, model_width : 2 * model_width].astype(jnp.bfloat16).reshape(head_shape)
    value_heads = (
        (projected[:, 2 * model_width :] + bias_value).astype(jnp.bfloat16).reshape(head_shape)
    )
    block_rows = 512
    positions = jnp.arange(row_count)
    blk_start = 0
    windows = [(blk_start, max(0, blk_start - MAXLEN), blk_start + block_rows)]

    def window_masked():
        allowed = permitted(segment, segment, positions, positions)
        return block_scores(query_heads, key_heads, allowed, scale_qk)

    blk_start, key_low, blk_stop = windows[0]
    masked = window_masked()
    row_max = jnp.max(masked, axis=-1, keepdims=True)
    log_total = row_max + jnp.log(jnp.sum(jnp.exp(masked - row_max), axis=-1, keepdims=True))
    attn_probs = jnp.exp(masked - log_total).astype(jnp.bfloat16)
    mixed_parts = jnp.einsum(
        "hqk,khd->qhd", attn_probs, value_heads, preferred_element_type=jnp.float32
    )
    log_totals = [log_total]
    mixed_rows = mixed_parts.reshape(row_count, model_width).astype(jnp.bfloat16)
    residual = hidden + (
        jnp.dot(mixed_rows, out_weight, preferred_element_type=jnp.float32) + bias_out
    )
    normed_two, back_two = jax.vjp(normalize, residual, gain_two, shift_two)
    second_in = normed_two.astype(jnp.bfloat16)
    up_weight = mlp_full[:, :hidden_width]
    down_weight = mlp_full[:, hidden_width:]
    pre_act = jnp.dot(second_in, up_weight, preferred_element_type=jnp.float32) + bias_up
    activated, gelu_back = jax.vjp(gelu_tanh, pre_act)
    act_low = activated.astype(jnp.bfloat16)
    output = (residual + contract_cols(act_low, down_weight) + bias_down).astype(jnp.bfloat16)
    grad_out = jnp.where((segment >= 0)[:, None], cotangent.astype(jnp.float32), 0.0)
    grad_low = grad_out.astype(jnp.bfloat16)
    grad_bias_down = jnp.sum(grad_out, axis=0)
    grad_down = contract_rows(grad_low, act_low)
    grad_act = jnp.dot(grad_low, down_weight, preferred_element_type=jnp.float32)
    grad_pre = gelu_back(grad_act)[0].astype(jnp.bfloat16)
    grad_bias_up = jnp.sum(grad_pre.astype(jnp.float32), axis=0)
    grad_up = contract_rows(second_in, grad_pre)
    grad_normed_two = contract_cols(grad_pre, up_weight)
    resid_part, grad_gain_two, grad_shift_two = back_two(grad_normed_two)
    grad_resid = grad_out + resid_part
    flat_up, flat_down = (
        lax.psum_scatter(
            spread_matrix(grad_up, groups, owners), ("dp", "opt"), scatter_dimension=0, tiled=True
        ),
        lax.psum_scatter(
            spread_matrix(grad_down, groups, owners), ("dp", "opt"), scatter_dimension=0, tiled=True
        ),
    )
    shard_up, shard_down = (
        lax.all_gather(flat_up, "dp", axis=1, tiled=True),
        lax.all_gather(flat_down, "dp", axis=1, tiled=True),
    )
    branch_grad = grad_resid.astype(jnp.bfloat16)
    grad_bias_out = jnp.sum(branch_grad.astype(jnp.float32), axis=0)
    grad_outw = contract_rows(mixed_rows, branch_grad)
    grad_mixed = contract_cols(branch_grad, out_weight).astype(jnp.bfloat16).reshape(head_shape)
    query_grads = []
    key_total = jnp.zeros(head_shape, jnp.float32)
    value_total = jnp.zeros(head_shape, jnp.float32)
    for (blk_start, key_low, blk_stop), log_total in zip(windows, log_totals):
        masked = window_masked()
        attn_probs = jnp.exp(masked - log_total)
        probs_low = attn_probs.astype(jnp.bfloat16)
        grad_probs = jnp.einsum(
            "qhd,khd->hqk", grad_mixed, value_heads, preferred_element_type=jnp.float32
        )
        row_dot = jnp.sum(attn_probs * grad_probs, axis=-1, keepdims=True)
        grad_scores = (attn_probs * (grad_probs - row_dot)).astype(jnp.bfloat16)
        query_grads.append(
            jnp.einsum("hqk,khd->qhd", grad_scores, key_heads, preferred_element_type=jnp.float32)
            * scale_qk
        )
        key_part = (
            jnp.einsum("hqk,qhd->khd", grad_scores, query_heads, preferred_element_type=jnp.float32)
            * scale_qk
        )
        value_part = jnp.einsum(
            "hqk,qhd->khd", probs_low, grad_mixed, preferred_element_type=jnp.float32
        )
        key_total = key_total.at[key_low:blk_stop].add(key_part)
        value_total = value_total.at[key_low:blk_stop].add(value_part)
    grad_query = query_grads[0].reshape(row_count, model_width).astype(jnp.bfloat16)
    grad_key = key_total.reshape(row_count, model_width).astype(jnp.bfloat16)
    grad_value = value_total.reshape(row_count, model_width).astype(jnp.bfloat16)
    grad_bias_query = jnp.sum(grad_query.astype(jnp.float32), axis=0)
    grad_bias_value = jnp.sum(grad_value.astype(jnp.float32), axis=0)
    grad_proj = jnp.concatenate([grad_query, grad_key, grad_value], axis=1)
    grad_qkv = contract_rows(first_in, grad_proj)
    grad_normed_one = contract_cols(grad_proj, qkv_weight)
    hidden_part, grad_gain_one, grad_shift_one = back_one(grad_normed_one)
    input_grad = grad_resid + hidden_part
    grad_vec = jnp.concatenate(
        [
            grad_gain_one,
            grad_shift_one,
            grad_bias_query,
            grad_bias_value,
            grad_bias_out,
            grad_gain_two,
            grad_shift_two,
            grad_bias_down,
            grad_bias_up,
        ]
    )
    flat_qkv, flat_outw, flat_vec = (
        lax.psum_scatter(
            spread_matrix(grad_qkv, groups, owners), ("dp", "opt"), scatter_dimension=0, tiled=True
        ),
        lax.psum_scatter(
            spread_matrix(grad_outw, groups, owners), ("dp", "opt"), scatter_dimension=0, tiled=True
        ),
        lax.psum_scatter(
            spread_vector(grad_vec, groups, owners), ("dp", "opt"), scatter_dimension=0, tiled=True
        ),
    )
    shard_qkv, shard_outw, shard_vec = (
        lax.all_gather(flat_qkv, "dp", axis=1, tiled=True),
        lax.all_gather(flat_outw, "dp", axis=1, tiled=True),
        lax.all_gather(flat_vec, "dp", axis=1, tiled=True),
    )
    shard_vec = shard_vec.reshape(-1)
    grad_attn = jnp.concatenate([shard_qkv, shard_outw], axis=1)
    grad_mlp = jnp.concatenate([shard_up, shard_down], axis=1)
    new_attn, first_attn, second_attn = adamw_update(
        w_attn, m_attn, v_attn, grad_attn, matrix_rate, matrix_decay
    )
    new_mlp, first_mlp, second_mlp = adamw_update(
        w_mlp, m_mlp, v_mlp, grad_mlp, matrix_rate, matrix_decay
    )
    new_vec, first_vec, second_vec = adamw_update(
        vectors, m_vec, v_vec, shard_vec, vector_rate, 0.0
    )
    return (
        output,
        input_grad,
        new_attn,
        first_attn,
        second_attn,
        new_mlp,
        first_mlp,
        second_mlp,
        new_vec,
        first_vec,
        second_vec,
    )


def solution(mesh):
    in_specs = (
        P(("dp", "opt"), None),
        P(("dp", "opt")),
        P(("dp", "opt"), None),
        P("opt", None),
        P("opt", None),
        P("opt", None),
        P("opt", None),
        P("opt", None),
        P("opt", None),
        P("opt"),
        P("opt"),
        P("opt"),
    )
    out_specs = (
        P(("dp", "opt"), None),
        P(("dp", "opt"), None),
        P("opt", None),
        P("opt", None),
        P("opt", None),
        P("opt", None),
        P("opt", None),
        P("opt", None),
        P("opt"),
        P("opt"),
        P("opt"),
    )
    return jax.shard_map(body, mesh=mesh, in_specs=in_specs, out_specs=out_specs, check_vma=False)
```

profile of v0, /device:TPU:0, one launch (start us, length us, event | category | flops | bytes accessed | tf_op | source)
XLA Modules:
  0.0 610.4 jit_solution(3303970298493624857)
XLA Ops:
  7.2 2.3 convert_element_type.116
  9.6 1.2 convert_element_type.124
  10.9 5.4 all-gather
  16.4 0.6 fusion.68
  18.0 17.6 %all-gather.6.cloned.1.call-done = bf16[384,1536]{1,0:T(8,128)(2,1)} async-done(((bf16[192,1536]{1,0:T(8,128)(2,1)}), bf16[384,1536]{1,0:T(8,128)(2,1)}) %all-gather.6.cloned.1.call-update) | async-done | bytes 1179664 | tf_op jit(solution)/shard_map/all_gather | solution.py:89
  35.7 2.1 fusion.41
  38.7 1.2 fusion
  39.9 1.3 exponential_reduce_fusion
  41.3 1.3 copy-done
  42.6 1.8 convolution_convert_fusion.1
  44.4 0.7 copy-done.18
  45.1 1.4 fusion.69
  46.7 27.2 %all-gather.8.cloned.1.call-done = bf16[384,3072]{1,0:T(8,128)(2,1)} async-done(((bf16[192,3072]{1,0:T(8,128)(2,1)}), bf16[384,3072]{1,0:T(8,128)(2,1)}) %all-gather.8.cloned.1.call-update) | async-done | bytes 2359312 | tf_op jit(solution)/shard_map/all_gather | solution.py:92
  73.9 2.4 convolution_add_fusion
  76.3 1.7 copy-done.77
  78.0 2.8 fusion.45
  80.8 4.1 reshape.298
  84.9 4.6 copy.223
  89.8 5.3 convert_reduce_fusion
  95.1 1.1 copy-done.16
  96.2 0.8 fusion.62
  97.1 2.3 reshape.296
  99.4 4.8 copy.222
  104.2 1.6 multiply_reduce_fusion.1
  106.2 0.8 copy-done.3
  107.1 0.8 convert_reduce_fusion.2
  108.3 2.3 copy.221
  110.6 1.3 convolution_convert_fusion.2
  112.0 5.3 multiply_reduce_fusion
  117.3 2.0 multiply_convert_fusion
  119.3 1.8 fusion.13
  121.1 1.3 convert_reduce_fusion.4
  122.8 0.8 copy-done.23
  123.6 5.3 convert_reduce_fusion.3
  128.8 0.7 copy-done.75
  129.6 2.1 fusion.43
  131.8 3.4 reshape.293
  135.1 2.8 copy.220
  138.0 0.6 copy-done.76
  138.6 0.6 dynamic-slice.10
  139.8 51.4 %reduce-scatter.19.cloned.1.call-done = f32[192,96]{1,0:T(8,128)} async-done(((f32[6144,96]{1,0:T(8,128)}), f32[192,96]{1,0:T(8,128)}) %reduce-scatter.19.cloned.1.call-update) | async-done | bytes 73744
  191.2 1.6 copy.219
  193.0 3.7 fusion.14
  196.7 0.9 copy.203
  197.6 2.0 fusion.70
  200.9 0.4 fusion.37
  201.4 1.1 copy.204
  202.7 94.3 %reduce-scatter.17.cloned.1.call-done = f32[192,96]{1,0:T(8,128)} async-done(((f32[6144,96]{1,0:T(8,128)}), f32[192,96]{1,0:T(8,128)}) %reduce-scatter.17.cloned.1.call-update) | async-done | bytes 73744
  297.0 1.6 copy.217
  298.9 40.0 %all-reduce.1 = f32[32,144]{1,0:T(8,128)S(1)} all-reduce(f32[32,144]{1,0:T(8,128)S(1)} %reshape.301), channel_id=6, replica_groups=mesh['dp'=16,'opt'=2] {'dp','opt'}, use_global_device_ids=true, to_apply=%region_24.25.clone | all-reduce | flops 4608 | bytes 36864
  339.3 58.9 %all-reduce = f32[2304]{0:T(1024)S(1)} all-reduce(f32[2304]{0:T(1024)S(1)} %dynamic-update-slice.4), channel_id=1, replica_groups=mesh['dp'=16,'opt'=2] {'dp'}, use_global_device_ids=true, to_apply=%add | all-reduce | flops 2304 | bytes 18432 | tf_op jit(solution)/shard_map/reshape | solution.py:236
  398.2 0.6 multiply_subtract_fusion.2
  398.8 4.1 reduce-scatter.15.cloned.1.call-done
  403.0 1.0 copy.215
  403.9 21.2 %all_gather.28 = f32[192,384]{0,1:T(8,128)S(1)} all-gather(f32[192,24]{0,1:T(8,128)S(1)} %copy.215), channel_id=1, replica_groups=mesh['dp'=16,'opt'=2] {'dp'}, dimensions={1}, use_global_device_ids=true | all-gather | bytes 313344 | tf_op jit(solution)/shard_map/all_gather | solution.py:233
  425.3 83.5 %reduce-scatter.13.cloned.1.call-done = f32[192,72]{1,0:T(8,128)} async-done(((f32[6144,72]{1,0:T(8,128)}), f32[192,72]{1,0:T(8,128)}) %reduce-scatter.13.cloned.1.call-update) | async-done | bytes 55312
  508.8 1.0 copy.213
  509.8 24.2 %all_gather.27 = f32[192,1152]{0,1:T(8,128)S(1)} all-gather(f32[192,72]{0,1:T(8,128)S(1)} %copy.213), channel_id=1, replica_groups=mesh['dp'=16,'opt'=2] {'dp'}, dimensions={1}, use_global_device_ids=true | all-gather | bytes 940032 | tf_op jit(solution)/shard_map/all_gather | solution.py:232
  534.4 4.0 multiply_subtract_fusion.1
  538.4 13.4 %all-gather.12.cloned.1.call-done = f32[192,1536]{0,1:T(8,128)} async-done(((f32[192,96]{0,1:T(8,128)}), f32[192,1536]{0,1:T(8,128)}) %all-gather.12.cloned.1.call-update) | async-done | bytes 1179664 | tf_op jit(solution)/shard_map/all_gather | solution.py:166
  551.8 1.9 copy.200
  553.6 39.6 %all-gather.10.cloned.1.call-done = f32[192,1536]{0,1:T(8,128)} async-done(((f32[192,96]{0,1:T(8,128)}), f32[192,1536]{0,1:T(8,128)}) %all-gather.10.cloned.1.call-update) | async-done | bytes 1179664 | tf_op jit(solution)/shard_map/all_gather | solution.py:165
  593.2 2.9 copy.199
  596.1 7.0 %multiply_subtract_fusion = (f32[192,3072]{1,0:T(8,128)}, f32[192,3072]{1,0:T(8,128)}, f32[192,3072]{1,0:T(8,128)}) fusion(f32[192,3072]{1,0:T(8,128)S(1)} %copy-done.2, f32[192,1536]{1,0:T(8,128)S(1)} %copy.200, f32[192,1536]{1,0:T(8,128)} %copy.199, f32[192,3072]{1,0:T(8,128)} %param.27, f32[192,3072]{1,0:T(8,128)} %param.28), kind=kLoop, calls=%fused_computation.22 | loop fusion | flops 9437184 | bytes 16515072 | tf_op jit(solution)/shard_map/sub | solution.py:67
  (221 shorter events, 6.0 us)
Async XLA Ops:
  7.2 2.5 copy-start.1
  7.2 28.5 %all-gather.6.cloned.1.call-start = ((), (), s32[]{:S(2)}) async-start(), calls=%async_computation.4 | async-start | bytes 1769472 | tf_op jit(solution)/shard_map/all_gather | solution.py:89
  9.6 7.5 %copy-start.26 = (bf16[512,384]{1,0:T(8,128)(2,1)S(1)}, bf16[512,384]{1,0:T(8,128)(2,1)}, u32[]{:S(2)}) copy-start(bf16[512,384]{1,0:T(8,128)(2,1)} %param.20) | copy-start | bytes 1179652
  9.6 64.3 %all-gather.8.cloned.1.call-start = ((), (), s32[]{:S(2)}) async-start(), calls=%async_computation.5 | async-start | bytes 3538944 | tf_op jit(solution)/shard_map/all_gather | solution.py:92
  10.8 6.7 %copy-start.53 = (s32[512]{0:T(512)S(1)}, s32[512]{0:T(512)}, u32[]{:S(2)}) copy-start(s32[512]{0:T(512)} %param.21) | copy-start | bytes 6148
  10.8 7.0 %copy-start.27 = (bf16[512,384]{1,0:T(8,128)(2,1)S(1)}, bf16[512,384]{1,0:T(8,128)(2,1)}, u32[]{:S(2)}) copy-start(bf16[512,384]{1,0:T(8,128)(2,1)} %param.22) | copy-start | bytes 1179652
  10.8 180.4 %reduce-scatter.19.cloned.1.call-start = ((), (), s32[]{:S(2)}) async-start(), calls=%async_computation.11 | async-start | bytes 3244032
  16.4 21.4 %copy-start.29 = (f32[4608]{0:T(1024)}, f32[4608]{0:T(1024)S(1)}, u32[]{:S(2)}) copy-start(f32[4608]{0:T(1024)S(1)} %reshape.308) | copy-start | bytes 55300
  17.0 20.8 %copy-start.36 = (f32[384]{0:T(512)}, f32[384]{0:T(512)S(1)}, u32[]{:S(2)}) copy-start(f32[384]{0:T(512)S(1)} %get-tuple-element.157) | copy-start | bytes 4612
  17.0 20.8 %copy-start.63 = (f32[384]{0:T(512)}, f32[384]{0:T(512)S(1)}, u32[]{:S(2)}) copy-start(f32[384]{0:T(512)S(1)} %get-tuple-element.156) | copy-start | bytes 4612
  17.0 56.9 %copy-start.33 = (f32[384]{0:T(512)}, f32[384]{0:T(512)S(1)}, u32[]{:S(2)}) copy-start(f32[384]{0:T(512)S(1)} %get-tuple-element.150) | copy-start | bytes 4612
  17.0 56.9 %copy-start.39 = (f32[384]{0:T(512)}, f32[384]{0:T(512)S(1)}, u32[]{:S(2)}) copy-start(f32[384]{0:T(512)S(1)} %get-tuple-element.152) | copy-start | bytes 4612
  17.3 20.5 %copy-start.30 = (f32[512]{0:T(512)}, f32[512]{0:T(512)S(1)}, u32[]{:S(2)}) copy-start(f32[512]{0:T(512)S(1)} %broadcast_multiply_fusion.1) | copy-start | bytes 6148
  17.5 20.4 %copy-start.56 = (f32[512]{0:T(512)}, f32[512]{0:T(512)S(1)}, u32[]{:S(2)}) copy-start(f32[512]{0:T(512)S(1)} %fusion.33) | copy-start | bytes 6148
  17.5 20.4 %copy-start.46 = (f32[512]{0:T(512)}, f32[512]{0:T(512)S(1)}, u32[]{:S(2)}) copy-start(f32[512]{0:T(512)S(1)} %fusion.52) | copy-start | bytes 6148
  17.5 72.2 %copy-start.65 = (pred[512]{0:T(512)(128)(4,1)}, pred[512]{0:T(512)(128)(4,1)S(1)}, u32[]{:S(2)}) copy-start(pred[512]{0:T(512)(128)(4,1)S(1)} %broadcast_compare_fusion) | copy-start | bytes 1540
  17.8 23.4 %copy-start.5 = (pred[512,512]{0,1:T(8,128)(4,1)}, pred[512,512]{0,1:T(8,128)(4,1)S(1)}, u32[]{:S(2)}) copy-start(pred[512,512]{0,1:T(8,128)(4,1)S(1)} %fusion.21) | copy-start | bytes 786436
  18.0 71.7 %copy-start.12 = (bf16[512,384]{0,1:T(8,128)(2,1)}, bf16[512,384]{0,1:T(8,128)(2,1)S(1)}, u32[]{:S(2)}) copy-start(bf16[512,384]{0,1:T(8,128)(2,1)S(1)} %copy.187) | copy-start | bytes 1179652
  38.3 3.0 copy-start.20
  39.9 2.7 copy-start
  44.4 29.5 %slice-start.2 = ((f32[4608]{0:T(1024)}), f32[1536]{0:T(1024)S(1)}, s32[]{:S(2)}) async-start(f32[4608]{0:T(1024)} %copy-done.29), calls=%async_computation.14 | async-start | bytes 16384 | tf_op jit(solution)/shard_map/slice | solution.py:103
  46.6 29.7 %copy-start.41 = (f32[512]{0:T(512)}, f32[512]{0:T(512)S(1)}, u32[]{:S(2)}) copy-start(f32[512]{0:T(512)S(1)} %broadcast_multiply_fusion) | copy-start | bytes 6148
  46.7 29.6 %copy-start.58 = (f32[512]{0:T(512)}, f32[512]{0:T(512)S(1)}, u32[]{:S(2)}) copy-start(f32[512]{0:T(512)S(1)} %multiply_reduce_fusion.3) | copy-start | bytes 6148
  46.7 29.6 %copy-start.49 = (f32[512]{0:T(512)}, f32[512]{0:T(512)S(1)}, u32[]{:S(2)}) copy-start(f32[512]{0:T(512)S(1)} %fusion.53) | copy-start | bytes 6148
  89.5 207.6 %reduce-scatter.17.cloned.1.call-start = ((), (), s32[]{:S(2)}) async-start(), calls=%async_computation.10 | async-start | bytes 3244032
  89.7 6.5 %copy-start.34 = (f32[384]{0:T(512)S(1)}, f32[384]{0:T(512)}, u32[]{:S(2)}) copy-start(f32[384]{0:T(512)} %copy-done.33) | copy-start | bytes 4612
  89.7 6.5 %copy-start.40 = (f32[384]{0:T(512)S(1)}, f32[384]{0:T(512)}, u32[]{:S(2)}) copy-start(f32[384]{0:T(512)} %copy-done.39) | copy-start | bytes 4612
  89.7 6.5 %copy-start.42 = (f32[512]{0:T(512)S(1)}, f32[512]{0:T(512)}, u32[]{:S(2)}) copy-start(f32[512]{0:T(512)} %copy-done.41) | copy-start | bytes 6148
  89.7 6.5 %copy-start.50 = (f32[512]{0:T(512)S(1)}, f32[512]{0:T(512)}, u32[]{:S(2)}) copy-start(f32[512]{0:T(512)} %copy-done.49) | copy-start | bytes 6148
  99.3 4.8 copy-start.17
  99.3 4.8 copy-start.35
  99.3 4.8 copy-start.43
  99.3 4.8 copy-start.51
  99.4 4.8 copy-start.74
  105.9 2.0 copy-start.19
  105.9 297.1 %reduce-scatter.15.cloned.1.call-start = ((), (), s32[]{:S(2)}) async-start(), calls=%async_computation.9 | async-start | bytes 3244032
  108.3 3.7 copy-start.6
  108.3 3.7 copy-start.21
  111.9 5.4 copy-start.22
  111.9 5.4 slice-start
  112.0 5.4 slice-start.1
  122.4 6.4 %copy-start.24 = (bf16[6,64,512]{2,1,0:T(8,128)(2,1)}, bf16[6,64,512]{2,1,0:T(8,128)(2,1)S(1)}, u32[]{:S(2)}) copy-start(bf16[6,64,512]{2,1,0:T(8,128)(2,1)S(1)} %get-tuple-element.168) | copy-start | bytes 1179652
  122.5 7.1 %copy-start.28 = (bf16[6,64,512]{2,1,0:T(8,128)(2,1)S(1)}, bf16[6,64,512]{2,1,0:T(8,128)(2,1)}, u32[]{:S(2)}) copy-start(bf16[6,64,512]{2,1,0:T(8,128)(2,1)} %fusion.13) | copy-start | bytes 1179652
  122.5 7.1 %copy-start.31 = (f32[512]{0:T(512)S(1)}, f32[512]{0:T(512)}, u32[]{:S(2)}) copy-start(f32[512]{0:T(512)} %copy-done.30) | copy-start | bytes 6148
  122.5 7.1 %copy-start.37 = (f32[384]{0:T(512)S(1)}, f32[384]{0:T(512)}, u32[]{:S(2)}) copy-start(f32[384]{0:T(512)} %copy-done.36) | copy-start | bytes 4612
  122.5 7.1 %copy-start.47 = (f32[512]{0:T(512)S(1)}, f32[512]{0:T(512)}, u32[]{:S(2)}) copy-start(f32[512]{0:T(512)} %copy-done.46) | copy-start | bytes 6148
  122.5 7.1 %copy-start.64 = (f32[384]{0:T(512)S(1)}, f32[384]{0:T(512)}, u32[]{:S(2)}) copy-start(f32[384]{0:T(512)} %copy-done.63) | copy-start | bytes 4612
  122.5 386.3 %reduce-scatter.13.cloned.1.call-start = ((), (), s32[]{:S(2)}) async-start(), calls=%async_computation.8 | async-start | bytes 3244032
  137.9 55.0 %copy-start.71 = (f32[384]{0:T(512)S(1)}, f32[384]{0:T(512)}, u32[]{:S(2)}) copy-start(f32[384]{0:T(512)} %get-tuple-element.151) | copy-start | bytes 4612
  137.9 413.8 %all-gather.12.cloned.1.call-start = ((), (), s32[]{:S(2)}) async-start(), calls=%async_computation.7 | async-start | bytes 1671168 | tf_op jit(solution)/shard_map/all_gather | solution.py:166
  192.9 400.3 %all-gather.10.cloned.1.call-start = ((), (), s32[]{:S(2)}) async-start(), calls=%async_computation.6 | async-start | bytes 1671168 | tf_op jit(solution)/shard_map/all_gather | solution.py:165
  193.0 4.6 copy-start.15
  193.0 4.6 copy-start.25
  197.6 2.3 copy-start.32
  197.6 2.3 copy-start.38
  200.9 97.8 %copy-start.68 = (f32[384]{0:T(512)S(1)}, f32[384]{0:T(512)}, u32[]{:S(2)}) copy-start(f32[384]{0:T(512)} %get-tuple-element.136) | copy-start | bytes 4612
  200.9 97.8 %copy-start.73 = (f32[384]{0:T(512)S(1)}, f32[384]{0:T(512)}, u32[]{:S(2)}) copy-start(f32[384]{0:T(512)} %get-tuple-element.128) | copy-start | bytes 4612
  200.9 97.9 %copy-start.72 = (f32[384]{0:T(512)S(1)}, f32[384]{0:T(512)}, u32[]{:S(2)}) copy-start(f32[384]{0:T(512)} %get-tuple-element.132) | copy-start | bytes 4612
  200.9 97.9 %copy-start.69 = (f32[1536]{0:T(1024)S(1)}, f32[1536]{0:T(1024)}, u32[]{:S(2)}) copy-start(f32[1536]{0:T(1024)} %get-tuple-element.171) | copy-start | bytes 18436
  200.9 197.3 %copy-start.45 = (f32[2304]{0:T(1024)S(1)}, f32[2304]{0:T(1024)}, u32[]{:S(2)}) copy-start(f32[2304]{0:T(1024)} %param.29) | copy-start | bytes 27652
  200.9 197.3 %copy-start.61 = (f32[2304]{0:T(1024)S(1)}, f32[2304]{0:T(1024)}, u32[]{:S(2)}) copy-start(f32[2304]{0:T(1024)} %param.30) | copy-start | bytes 27652
  200.9 197.3 %copy-start.62 = (f32[2304]{0:T(1024)S(1)}, f32[2304]{0:T(1024)}, u32[]{:S(2)}) copy-start(f32[2304]{0:T(1024)} %param.31) | copy-start | bytes 27652
  398.8 135.5 %copy-start.7 = (f32[192,1536]{1,0:T(8,128)S(1)}, f32[192,1536]{1,0:T(8,128)}, u32[]{:S(2)}) copy-start(f32[192,1536]{1,0:T(8,128)} %param.23) | copy-start | bytes 3538948
  538.3 57.8 %copy-start.2 = (f32[192,3072]{1,0:T(8,128)S(1)}, f32[192,3072]{1,0:T(8,128)}, u32[]{:S(2)}) copy-start(f32[192,3072]{1,0:T(8,128)} %param.26) | copy-start | bytes 7077892
  (25 other events, 32.0 us)
Sparse Core Ops, SparseCore 0:
  10.1 25.4 all-gather.5
  37.8 36.0 all-gather.7
  89.6 101.6 reduce-scatter.18
  196.5 100.4 reduce-scatter.16
  302.3 100.6 reduce-scatter.14
  408.3 100.4 reduce-scatter.12
  511.6 40.0 all-gather.11
  554.6 38.5 all-gather.9
where the time goes:
time: 619 us; the launch traced here: 610 us
  waiting for transfers between devices  331 us (53%)
  blocking collectives  150 us (24%)
  local copies, waits for them, and re-layouts  48.3 us (8%)
  matrix products  42.7 us (7%)
  other arithmetic  21.3 us (3%)
  between operations  16.4 us (3%)
    unnamed x12, waiting for transfers between devices  233 us
    reshape x1, blocking collectives, body(): shard_vec = shard_vec.reshape(-1)  58.9 us
    unnamed x1, blocking collectives  40 us
    all_gather x1, waiting for transfers between devices, body(): lax.all_gather(flat_up, 'dp', axis=1, tiled=True)  39.6 us
    unnamed x185, local copies, waits for them, and re-layouts  31.5 us
    all_gather x1, waiting for transfers between devices, body(): lax.all_gather(w_mlp.astype(jnp.bfloat16), 'opt', axis=0, tiled=True)  27.2 us
    all_gather x1, blocking collectives, body(): lax.all_gather(flat_qkv, 'dp', axis=1, tiled=True)  24.2 us
    all_gather x1, blocking collectives, body(): lax.all_gather(flat_outw, 'dp', axis=1, tiled=True)  21.2 us
  transfers between devices with their start and end apart: 8, of which 8 were waited for; matrix products, arithmetic and copies ran while one was open for 13% of the time, Pallas kernels for 0%

commit v1 on v0

v1 whole, which is shorter than its diff:
```python
import functools
import math

import jax
import jax.numpy as jnp
from jax import lax
from jax.experimental import pallas as pl
from jax.experimental.pallas import tpu as pltpu
from jax.sharding import PartitionSpec as P

D = 384
HEADS = 6
HEAD_DIM = 64
FF = 1536
TOK = 512
QBLK = 256
STEP = 10
VEC_ROWS = 16

norm_eps = 1e-05
beta_one = 0.9
beta_two = 0.95
adam_eps = 1e-08
matrix_rate = 0.15
vector_rate = 0.6
matrix_decay = 0.1
neg_large = -1e30
gelu_c = math.sqrt(2.0 / math.pi)

f32 = jnp.float32
bf16 = jnp.bfloat16
VMEM_BYTES = 48 * 1024 * 1024

vmem = pl.BlockSpec(memory_space=pltpu.VMEM)
smem = pl.BlockSpec(memory_space=pltpu.SMEM)


def dot(left, right, dims):
    return lax.dot_general(left, right, ((dims[:1], dims[1:]), ((), ())), preferred_element_type=f32)


def mm(left, right):
    return dot(left, right, (1, 0))


def mm_nt(left, right):
    return dot(left, right, (1, 1))


def mm_tn(left, right):
    return dot(left, right, (0, 0))


def ln_parts(values):
    mean = jnp.mean(values, axis=-1, keepdims=True)
    centred = values - mean
    var = jnp.mean(centred * centred, axis=-1, keepdims=True)
    rstd = lax.rsqrt(var + norm_eps)
    return centred * rstd, rstd


def ln_back(grad, gain, normed, rstd):
    e = grad * gain
    mean_e = jnp.mean(e, axis=-1, keepdims=True)
    mean_en = jnp.mean(e * normed, axis=-1, keepdims=True)
    return (e - mean_e - normed * mean_en) * rstd


def call(kernel, outs, ins, args, scratch=(), flops=0, name=None):
    moved = sum(math.prod(a.shape) * a.dtype.itemsize for a in args)
    moved += sum(math.prod(o.shape) * o.dtype.itemsize for o in outs)
    return pl.pallas_call(
        kernel,
        out_shape=list(outs),
        in_specs=list(ins),
        out_specs=[vmem] * len(outs),
        scratch_shapes=list(scratch),
        compiler_params=pltpu.CompilerParams(vmem_limit_bytes=VMEM_BYTES),
        cost_estimate=pl.CostEstimate(flops=flops, bytes_accessed=moved, transcendentals=0),
        name=name,
    )(*args)


def shaped(shape, dtype):
    return jax.ShapeDtypeStruct(shape, dtype)


class Plan:
    def __init__(self, mesh):
        self.n_dp = mesh.shape["dp"]
        self.n_opt = mesh.shape["opt"]
        self.n_z = self.n_dp // 4
        self.own = D // self.n_opt
        self.chunk = self.own // self.n_z
        self.unit = math.gcd(self.chunk, 16)
        self.per = self.chunk // self.unit
        self.vec_units = VEC_ROWS // self.unit


def assemble(plan, idx_ref, own_ref, direct_refs, cross_refs, full_ref):
    core, op = idx_ref[0], idx_ref[3]
    width = full_ref.shape[3]
    full_ref[op, 0] = own_ref[:, :width].astype(bf16)
    full_ref[op, 1] = own_ref[:, width:].astype(bf16)
    for m in range(1, plan.n_opt):
        full_ref[op ^ m, core] = direct_refs[m - 1][: plan.own, :]
        full_ref[op ^ m, 1 - core] = cross_refs[m - 1][: plan.own, :]


def store_chunks(plan, ref, base_of, value, mats, mat, idx_ref):
    zi, op = idx_ref[2], idx_ref[3]
    for i in range(plan.n_opt * plan.n_z):
        rel = ((i // plan.n_z) ^ op) * plan.n_z + ((i % plan.n_z) ^ zi)
        for t in range(plan.per):
            row = i * plan.chunk + t * plan.unit
            at = base_of + (rel * mats + mat) * plan.per + t
            ref[at] = value[row : row + plan.unit].astype(ref.dtype)


def attn_forward(plan, *refs):
    n = plan.n_opt - 1
    idx_ref, tok_ref, segc_ref, segr_ref, vec_ref, own_ref = refs[:6]
    direct_refs, cross_refs = refs[6 : 6 + n], refs[6 + n : 6 + 2 * n]
    full_ref, qkv_ref, mixed_ref, lse_ref, resid_ref, bias_ref = refs[6 + 2 * n :]
    assemble(plan, idx_ref, own_ref, direct_refs, cross_refs, full_ref)
    hidden = tok_ref[...].astype(f32)
    normed, _ = ln_parts(hidden)
    first_in = (normed * vec_ref[0:1, :] + vec_ref[1:2, :]).astype(bf16)
    for number, row in ((0, 2), (1, None), (2, 3)):
        lane = (number % 2) * D
        weight = full_ref[:, number // 2, :, lane : lane + D].reshape(D, D)
        part = mm(first_in, weight)
        if row is not None:
            part = part + vec_ref[row : row + 1, :]
        qkv_ref[number] = part.astype(bf16).T
    fill_bias(segc_ref, segr_ref, bias_ref)

    def one_head(head, carry):
        rows = pl.ds(pl.multiple_of(head * HEAD_DIM, HEAD_DIM), HEAD_DIM)
        for blk in range(TOK // QBLK):
            cols = slice(blk * QBLK, (blk + 1) * QBLK)
            keys = (blk + 1) * QBLK
            query = qkv_ref[0, rows, cols] * bf16(HEAD_DIM**-0.5)
            scores = mm_tn(qkv_ref[1, rows, :keys], query) + bias_ref[:keys, cols]
            top = jnp.max(scores, axis=0, keepdims=True)
            e = jnp.exp(scores - top)
            total = jnp.sum(e, axis=0, keepdims=True)
            probs = (e * (1.0 / total)).astype(bf16)
            mixed_ref[rows, cols] = mm(qkv_ref[2, rows, :keys], probs).astype(bf16)
            lse_ref[pl.ds(head, 1), :, cols] = (top + jnp.log(total)).reshape(1, 1, QBLK)
        return carry

    lax.fori_loop(0, HEADS, one_head, 0, unroll=True)
    out_weight = full_ref[:, 1, :, D:].reshape(D, D)
    resid_ref[...] = hidden + (mm_tn(mixed_ref[...], out_weight) + vec_ref[4:5, :])


def fill_bias(segc_ref, segr_ref, bias_ref):
    key = lax.broadcasted_iota(jnp.int32, (TOK, TOK), 0)
    query = lax.broadcasted_iota(jnp.int32, (TOK, TOK), 1)
    seg_query = segr_ref[...]
    allowed = (segc_ref[...] == seg_query) & (key <= query) & ((seg_query >= 0) | (key == query))
    bias_ref[...] = jnp.where(allowed, 0.0, neg_large)


def mlp_step(plan, *refs):
    n = plan.n_opt - 1
    idx_ref, resid_ref, cot_ref, segc_ref, vec_ref, bup_ref, own_ref = refs[:7]
    direct_refs, cross_refs = refs[7 : 7 + n], refs[7 + n : 7 + 2 * n]
    (keep_ref, send_ref, act_ref, dres_ref, gvec_ref, gbup_ref, full_ref, out_acc, db_acc) = refs[7 + 2 * n :]
    assemble(plan, idx_ref, own_ref, direct_refs, cross_refs, full_ref)
    core, ybit = idx_ref[0], idx_ref[1]
    resid = resid_ref[...]
    normed, rstd = ln_parts(resid)
    second_in = (normed * vec_ref[5:6, :] + vec_ref[6:7, :]).astype(bf16)
    second_t = second_in.T
    dy = jnp.where(segc_ref[...] >= 0, cot_ref[...].astype(f32), 0.0)
    dy_low = dy.astype(bf16)
    dy_t = dy_low.T
    out_acc[...] = jnp.zeros_like(out_acc)
    db_acc[...] = jnp.zeros_like(db_acc)
    wide = FF // 2
    units = plan.n_opt * plan.n_z * 2 * plan.per

    def one_block(blk, carry):
        cols = pl.ds(pl.multiple_of(blk * wide, wide), wide)
        up = full_ref[:, 0, :, cols].reshape(D, wide)
        down = full_ref[:, 1, :, cols].reshape(D, wide)
        pre = mm(second_in, up) + bup_ref[blk]
        sq = pre * pre
        th = jnp.tanh(gelu_c * pre * (1.0 + 0.044715 * sq))
        half = 0.5 * (1.0 + th)
        act = (pre * half).astype(bf16)
        slope = half + (0.5 * gelu_c) * pre * (1.0 - th * th) * (1.0 + (3 * 0.044715) * sq)
        out_acc[...] += mm_nt(act, down)
        dpre = (mm(dy_low, down) * slope).astype(bf16)
        gbup_ref[blk] = jnp.sum(dpre.astype(f32), axis=0, keepdims=True)
        db_acc[...] += mm_nt(dpre, up)
        base = (blk ^ ybit) * units
        for mat, (left, right) in enumerate(((second_t, dpre), (dy_t, act))):
            grad = mm(left, right)
            first, last = grad[:, :D], grad[:, D:]
            store_chunks(plan, keep_ref, base, jnp.where(core == 0, first, last), 2, mat, idx_ref)
            store_chunks(plan, send_ref, base, jnp.where(core == 0, last, first), 2, mat, idx_ref)
        return carry

    lax.fori_loop(0, 2, one_block, 0, unroll=True)
    act_ref[...] = (resid + out_acc[...] + vec_ref[7:8, :]).astype(bf16)
    db = db_acc[...]
    dres_ref[...] = dy + ln_back(db, vec_ref[5:6, :], normed, rstd)
    gvec_ref[0:1, :] = jnp.sum(db * normed, axis=0, keepdims=True)
    gvec_ref[1:2, :] = jnp.sum(db, axis=0, keepdims=True)
    gvec_ref[2:3, :] = jnp.sum(dy, axis=0, keepdims=True)
    gvec_ref[3:8, :] = jnp.zeros((5, D), f32)


def back_heads(first, last, qkv_ref, bias_ref, lse_ref, dmix_ref, dqkv_ref, dkv_acc):
    scale = HEAD_DIM**-0.5
    for head in range(first, last):
        rows = slice(head * HEAD_DIM, (head + 1) * HEAD_DIM)
        out_rows = slice((head - first) * HEAD_DIM, (head - first + 1) * HEAD_DIM)
        for blk in range(TOK // QBLK):
            cols = slice(blk * QBLK, (blk + 1) * QBLK)
            keys = (blk + 1) * QBLK
            query = qkv_ref[0, rows, cols]
            key = qkv_ref[1, rows, :keys]
            value = qkv_ref[2, rows, :keys]
            dmix = dmix_ref[rows, cols]
            scores = mm_tn(key, query * bf16(scale)) + bias_ref[:keys, cols]
            probs = jnp.exp(scores - lse_ref[head][:, cols])
            dprobs = mm_tn(value, dmix)
            row_dot = jnp.sum(probs * dprobs, axis=0, keepdims=True)
            dscores = (probs * (dprobs - row_dot)).astype(bf16)
            dqkv_ref[0, out_rows, cols] = (mm(key, dscores) * scale).astype(bf16)
            dkey = mm_nt(query, dscores)
            dvalue = mm_nt(dmix, probs.astype(bf16))
            if blk == 0:
                dkv_acc[0, :, :QBLK] = dkey
                dkv_acc[1, :, :QBLK] = dvalue
            else:
                dkv_acc[0, :, :QBLK] += dkey[:, :QBLK]
                dkv_acc[1, :, :QBLK] += dvalue[:, :QBLK]
                dkv_acc[0, :, QBLK:] = dkey[:, QBLK:]
                dkv_acc[1, :, QBLK:] = dvalue[:, QBLK:]
        dqkv_ref[1, out_rows, :] = (dkv_acc[0] * scale).astype(bf16)
        dqkv_ref[2, out_rows, :] = dkv_acc[1].astype(bf16)


def attn_back_first(last, segc_ref, segr_ref, dres_ref, full_ref, mixed_ref, qkv_ref, lse_ref,
                    dmix_ref, gout_ref, gbo_ref, dqkv_ref, bias_ref, dkv_acc):
    dz = dres_ref[...].astype(bf16)
    gbo_ref[...] = jnp.broadcast_to(jnp.sum(dz.astype(f32), axis=0, keepdims=True), (8, D))
    out_weight = full_ref[:, 1, :, D:].reshape(D, D)
    dmix_ref[...] = mm_nt(out_weight, dz).astype(bf16)
    gout_ref[...] = mm(mixed_ref[...], dz)
    fill_bias(segc_ref, segr_ref, bias_ref)
    back_heads(0, last, qkv_ref, bias_ref, lse_ref, dmix_ref, dqkv_ref, dkv_acc)


def attn_back_next(first, last, segc_ref, segr_ref, dmix_ref, qkv_ref, lse_ref, dqkv_ref, bias_ref, dkv_acc):
    fill_bias(segc_ref, segr_ref, bias_ref)
    back_heads(first, last, qkv_ref, bias_ref, lse_ref, dmix_ref, dqkv_ref, dkv_acc)


def attn_back_last(plan, count, *refs):
    idx_ref, tok_ref, dres_ref, full_ref, vec_ref, gout_ref, gbo_ref, gvec_ref, gbup_ref = refs[:9]
    parts = refs[9 : 9 + count]
    keep_ref, send_ref, igrad_ref = refs[9 + count :]
    core, ybit = idx_ref[0], idx_ref[1]
    hidden = tok_ref[...].astype(f32)
    normed, rstd = ln_parts(hidden)
    first_in = (normed * vec_ref[0:1, :] + vec_ref[1:2, :]).astype(bf16)
    first_t = first_in.T
    dqkv = [jnp.concatenate([part[number] for part in parts], axis=0) for number in range(3)]
    grads = [mm_nt(first_t, dpart) for dpart in dqkv] + [gout_ref[...]]
    units = plan.n_opt * plan.n_z * plan.per
    for pair in range(2):
        base = (pair ^ ybit) * units
        first, last = grads[2 * pair], grads[2 * pair + 1]
        store_chunks(plan, keep_ref, base, jnp.where(core == 0, first, last), 1, 0, idx_ref)
        store_chunks(plan, send_ref, base, jnp.where(core == 0, last, first), 1, 0, idx_ref)
    da_t = jnp.zeros((D, TOK), f32)
    for number in range(3):
        lane = (number % 2) * D
        weight = full_ref[:, number // 2, :, lane : lane + D].reshape(D, D)
        da_t = da_t + mm(weight, dqkv[number])
    da = da_t.T
    igrad_ref[...] = dres_ref[...] + ln_back(da, vec_ref[0:1, :], normed, rstd)
    ones = jnp.ones((8, TOK), bf16)
    rows = [
        jnp.sum(da * normed, axis=0, keepdims=True),
        jnp.sum(da, axis=0, keepdims=True),
        mm_nt(ones, dqkv[0])[0:1, :],
        mm_nt(ones, dqkv[2])[0:1, :],
        gbo_ref[0:1, :],
        gvec_ref[0:3, :],
    ]
    for blk in range(2):
        rows += [gbup_ref[blk][:, :D], gbup_ref[blk][:, D:]]
    rows.append(jnp.zeros((VEC_ROWS - 12, D), f32))
    total = jnp.concatenate(rows, axis=0)
    for t in range(plan.vec_units):
        piece = total[t * plan.unit : (t + 1) * plan.unit]
        keep_ref[2 * units + t] = piece
        send_ref[2 * units + t] = piece.astype(bf16)


def add_pieces(count, size, tail, keep_dtype, *refs):
    keep_ref, others, outs = refs[0], refs[1 : -count], refs[-count:]
    for number in range(count):
        part = pl.ds(number * size, size)
        total = keep_ref[part].astype(f32)
        for other in others:
            total = total + other[part].astype(f32)
        outs[number][:size] = total.astype(outs[number].dtype)
    if tail:
        part = pl.ds(count * size, tail)
        total = keep_ref[part].astype(f32)
        for other in others:
            total = total + other[part].astype(f32)
        for number in range(count):
            outs[number][size:] = total.astype(outs[number].dtype)


def add_last(size, tail, keep_ref, *refs):
    others, outs = refs[: -(2 if tail else 1)], refs[-(2 if tail else 1) :]
    total = keep_ref[...]
    for other in others:
        total = total + other[...].astype(f32)
    outs[0][...] = total[:size].astype(bf16)
    if tail:
        outs[1][...] = total[size:]


def swap_core(n_dp, value):
    return lax.ppermute(value, "dp", [(i, i ^ 1) for i in range(n_dp)])


def reduce_scatter(plan, keep, send, mats, tail, tag):
    n_dp, n_opt, n_z = plan.n_dp, plan.n_opt, plan.n_z
    lead = plan.unit
    got = swap_core(n_dp, send)
    count = 2 * n_opt
    size = n_z * mats * plan.per
    outs = [shaped((size + tail, lead, D), f32 if k == 0 else bf16) for k in range(count)]
    parts = call(
        functools.partial(add_pieces, count, size, tail, f32), outs, [vmem] * 2, [keep, got], name="add_core_" + tag
    )
    got = []
    for number in range(1, count):
        mask_y, mask_o = number // n_opt, number % n_opt
        perm = [
            ((d * n_opt + o), ((d ^ (2 * mask_y)) * n_opt + (o ^ mask_o))) for d in range(n_dp) for o in range(n_opt)
        ]
        got.append(lax.ppermute(parts[number], ("dp", "opt"), perm))
    size = mats * plan.per
    outs = [shaped((size + tail, lead, D), f32 if k == 0 else bf16) for k in range(n_z)]
    parts = call(
        functools.partial(add_pieces, n_z, size, tail, f32),
        outs,
        [vmem] * count,
        [parts[0], *got],
        name="add_plane_" + tag,
    )
    got = [lax.ppermute(parts[m], "dp", [(i, i ^ (4 * m)) for i in range(n_dp)]) for m in range(1, n_z)]
    outs = [shaped((size, lead, D), bf16)]
    if tail:
        outs.append(shaped((tail, lead, D), f32))
    return call(
        functools.partial(add_last, size, tail), outs, [vmem] * n_z, [parts[0], *got], name="add_column_" + tag
    )


def gather(plan, shard):
    n_dp = plan.n_dp
    got = [lax.ppermute(shard, "dp", [(i, i ^ (4 * m)) for i in range(n_dp)]) for m in range(1, plan.n_z)]
    column = jnp.concatenate([shard, *got], axis=0)
    far = lax.ppermute(column, "dp", [(i, i ^ 2) for i in range(n_dp)])
    return column, swap_core(n_dp, column), far, swap_core(n_dp, far)


def adamw(weight, first, second, grad, rate, decay):
    first = beta_one * first + (1.0 - beta_one) * grad
    second = beta_two * second + (1.0 - beta_two) * grad * grad
    first_hat = first * (1.0 / (1.0 - beta_one**STEP))
    second_hat = second * (1.0 / (1.0 - beta_two**STEP))
    weight = weight - rate * (first_hat / (jnp.sqrt(second_hat) + adam_eps) + decay * weight)
    return weight, first, second


def adam_kernel(plan, mats, idx_ref, g0, g1, g2, g3, w_ref, m_ref, v_ref, nw_ref, nm_ref, nv_ref):
    mat = pl.program_id(0) // 4
    rel = (pl.program_id(0) % 4) ^ (idx_ref[0] + 2 * idx_ref[1])
    zi = idx_ref[2]
    for z in range(plan.n_z):
        for t in range(plan.per):
            at = ((z ^ zi) * mats + mat) * plan.per + t
            near = jnp.where(rel == 0, g0[at], g1[at])
            far = jnp.where(rel == 2, g2[at], g3[at])
            grad = jnp.where(rel < 2, near, far).astype(f32)
            rows = slice(z * plan.chunk + t * plan.unit, z * plan.chunk + (t + 1) * plan.unit)
            out = adamw(w_ref[rows], m_ref[rows], v_ref[rows], grad, matrix_rate, matrix_decay)
            nw_ref[rows], nm_ref[rows], nv_ref[rows] = out


def adam_matrix(plan, idx, grads, weight, first, second, mats):
    block = pl.BlockSpec((plan.own, D), lambda i: (0, i))
    whole = pl.BlockSpec(grads[0].shape, lambda i: (0, 0, 0))
    shape = shaped(weight.shape, f32)
    return pl.pallas_call(
        functools.partial(adam_kernel, plan, mats),
        grid=(4 * mats,),
        out_shape=[shape] * 3,
        in_specs=[smem] + [whole] * 4 + [block] * 3,
        out_specs=[block] * 3,
        compiler_params=pltpu.CompilerParams(vmem_limit_bytes=VMEM_BYTES),
        cost_estimate=pl.CostEstimate(
            flops=16 * weight.size, bytes_accessed=24 * weight.size, transcendentals=weight.size
        ),
        name="adam_" + str(mats),
    )(idx, *grads, weight, first, second)


def body(plan, tokens, segment, cotangent, w_attn, m_attn, v_attn, w_mlp, m_mlp, v_mlp, vectors, m_vec, v_vec):
    n_dp, n_opt = plan.n_dp, plan.n_opt
    dp, op = lax.axis_index("dp"), lax.axis_index("opt")
    core = dp & 1
    idx = jnp.stack([core, (dp >> 1) & 1, dp >> 2, op]).astype(jnp.int32)
    segc, segr = segment.reshape(TOK, 1), segment.reshape(1, TOK)

    def spread(send):
        direct = [
            lax.ppermute(send, "opt", [(o, o ^ m) for o in range(n_opt)]) for m in range(1, n_opt)
        ]
        return direct, [swap_core(n_dp, piece) for piece in direct]

    width = 2 * D
    length = vectors.shape[0]
    vec_rows = -(-length // width)
    vec_pad = jnp.pad(vectors.astype(bf16), (0, 16 * width - length)).reshape(16, width)
    attn_half = lax.dynamic_slice(w_attn, (0, core * width), (plan.own, width)).astype(bf16)
    attn_direct, attn_cross = spread(jnp.concatenate([attn_half, vec_pad], axis=0))
    mlp_half = lax.dynamic_slice(w_mlp, (0, core * FF), (plan.own, FF)).astype(bf16)
    mlp_direct, mlp_cross = spread(mlp_half)
    vec_parts = [vectors.astype(bf16)] + [
        piece[plan.own : plan.own + vec_rows].reshape(-1)[:length] for piece in attn_direct
    ]
    if n_opt == 2:
        low = jnp.where(op == 0, vec_parts[0], vec_parts[1])
        high = jnp.where(op == 0, vec_parts[1], vec_parts[0])
        vec = jnp.concatenate([low, high])
    else:
        vec = jnp.stack(vec_parts)[jnp.arange(n_opt) ^ op].reshape(-1)
    vec = vec.astype(f32)
    vec8 = vec[: 8 * D].reshape(8, D)
    bup = vec[8 * D :].reshape(2, 1, FF // 2)

    full, qkv, mixed, lse, resid = call(
        functools.partial(attn_forward, plan),
        [
            shaped((n_opt, 2, plan.own, width), bf16),
            shaped((3, D, TOK), bf16),
            shaped((D, TOK), bf16),
            shaped((HEADS, 1, TOK), f32),
            shaped((TOK, D), f32),
        ],
        [smem] + [vmem] * (5 + 2 * (n_opt - 1)),
        [idx, tokens, segc, segr, vec8, w_attn, *attn_direct, *attn_cross],
        [pltpu.VMEM((TOK, TOK), f32)],
        flops=2 * TOK * D * 4 * D + 8 * TOK * TOK * D,
        name="attn_forward",
    )
    units = 2 * n_opt * plan.n_z * plan.per
    mlp_keep, mlp_send, activations, dres, gvec, gbup = call(
        functools.partial(mlp_step, plan),
        [
            shaped((2 * units, plan.unit, D), f32),
            shaped((2 * units, plan.unit, D), bf16),
            shaped((TOK, D), bf16),
            shaped((TOK, D), f32),
            shaped((8, D), f32),
            shaped((2, 1, FF // 2), f32),
        ],
        [smem] + [vmem] * (6 + 2 * (n_opt - 1)),
        [idx, resid, cotangent, segc, vec8, bup, w_mlp, *mlp_direct, *mlp_cross],
        [
            pltpu.VMEM((n_opt, 2, plan.own, FF), bf16),
            pltpu.VMEM((TOK, D), f32),
            pltpu.VMEM((TOK, D), f32),
        ],
        flops=12 * TOK * D * FF,
        name="mlp_step",
    )
    (mlp_shard,) = reduce_scatter(plan, mlp_keep, mlp_send, 2, 0, "mlp")
    mlp_grads = gather(plan, mlp_shard)

    head_flops = 14 * TOK * TOK * HEAD_DIM
    head_scratch = [pltpu.VMEM((TOK, TOK), f32), pltpu.VMEM((2, HEAD_DIM, TOK), f32)]
    cuts = (0, 2, 4, 6)
    dmix, gout, gbo, part = call(
        functools.partial(attn_back_first, cuts[1]),
        [
            shaped((D, TOK), bf16),
            shaped((D, D), f32),
            shaped((8, D), f32),
            shaped((3, cuts[1] * HEAD_DIM, TOK), bf16),
        ],
        [vmem] * 7,
        [segc, segr, dres, full, mixed, qkv, lse],
        head_scratch,
        flops=4 * TOK * D * D + cuts[1] * head_flops,
        name="attn_back_first",
    )
    parts = [part]
    for first, last in zip(cuts[1:-1], cuts[2:]):
        (part,) = call(
            functools.partial(attn_back_next, first, last),
            [shaped((3, (last - first) * HEAD_DIM, TOK), bf16)],
            [vmem] * 5,
            [segc, segr, dmix, qkv, lse],
            head_scratch,
            flops=(last - first) * head_flops,
            name="attn_back_next",
        )
        parts.append(part)
    attn_keep, attn_send, input_grad = call(
        functools.partial(attn_back_last, plan, len(parts)),
        [
            shaped((units + plan.vec_units, plan.unit, D), f32),
            shaped((units + plan.vec_units, plan.unit, D), bf16),
            shaped((TOK, D), f32),
        ],
        [smem] + [vmem] * (8 + len(parts)),
        [idx, tokens, dres, full, vec8, gout, gbo, gvec, gbup, *parts],
        flops=12 * TOK * D * D,
        name="attn_back_last",
    )
    attn_shard, vec_grad = reduce_scatter(plan, attn_keep, attn_send, 1, plan.vec_units, "attn")
    attn_grads = gather(plan, attn_shard)
    new_mlp, first_mlp, second_mlp = adam_matrix(plan, idx, mlp_grads, w_mlp, m_mlp, v_mlp, 2)
    new_attn, first_attn, second_attn = adam_matrix(plan, idx, attn_grads, w_attn, m_attn, v_attn, 1)
    own_vec = lax.dynamic_slice(vec_grad.reshape(-1), (op * length,), (length,))
    new_vec, first_vec, second_vec = adamw(vectors, m_vec, v_vec, own_vec, vector_rate, 0.0)
    return (
        activations,
        input_grad,
        new_attn,
        first_attn,
        second_attn,
        new_mlp,
        first_mlp,
        second_mlp,
        new_vec,
        first_vec,
        second_vec,
    )


def solution(mesh):
    rows, both = P("opt", None), P(("dp", "opt"), None)
    in_specs = (both, P(("dp", "opt")), both) + (rows,) * 6 + (P("opt"),) * 3
    out_specs = (both, both) + (rows,) * 6 + (P("opt"),) * 3
    return jax.shard_map(
        functools.partial(body, Plan(mesh)), mesh=mesh, in_specs=in_specs, out_specs=out_specs, check_vma=False
    )
```

time: 619 us -> 142 us (0.23); the launches traced: 610 us -> 141 us
  waiting for transfers between devices: 331 us -> 49.3 us
  blocking collectives: 150 us -> 0 us
  matrix products: 42.7 us -> 0 us
  starting transfers between devices: 0.72 us -> 38.4 us
  Pallas kernels: 0 us -> 37.6 us
  local copies, waits for them, and re-layouts: 48.3 us -> 11.8 us
  other arithmetic: 21.3 us -> 3.05 us
  between operations: 16.4 us -> 0.94 us
    unnamed x12 -> x0, waiting for transfers between devices: 233 us -> none
    all_gather x4 -> x0, waiting for transfers between devices: 97.8 us -> none  [the longest x1 39.6 us: body(): lax.all_gather(flat_up, 'dp', axis=1, tiled=True)]
    reshape x1 -> x0, blocking collectives: 58.9 us -> none  [body(): shard_vec = shard_vec.reshape(-1)]
    all_gather x3 -> x0, blocking collectives: 50.9 us -> none  [the longest x1 24.2 us: body(): lax.all_gather(flat_qkv, 'dp', axis=1, tiled=True)]
    ppermute x0 -> x30, waiting for transfers between devices: none -> 49.3 us  [the longest x2 19 us: spread(): lax.ppermute(send, 'opt', [(o, o ^ m) for o in range(n_opt)])]
    dot_general x18 -> x0, matrix products: 42.7 us -> none  [the longest x4 8.6 us: contract_cols(): lax.dot_general(left_arr, right_arr, (((1,), (1,)), ((), ())), preferred_...]
    unnamed x1 -> x0, blocking collectives: 40 us -> none
    ppermute x0 -> x30, starting transfers between devices: none -> 38.4 us  [the longest x6 13.1 us: reduce_scatter(): lax.ppermute(parts[m], 'dp', [(i, i ^ 4 * m) for i in range(n_dp)])]
  transfers between devices with their start and end apart: 8 -> 30, of which waited for: 8 -> 12; matrix products, arithmetic and copies ran while one was open for 13% -> 5% of each run, Pallas kernels for 0% -> 15%
where the time goes in v1:
time: 142 us; the launch traced here: 141 us
  waiting for transfers between devices  49.3 us (35%)
  starting transfers between devices  38.4 us (27%)
  Pallas kernels  37.6 us (26%)
  local copies, waits for them, and re-layouts  11.8 us (8%)
  other arithmetic  3.05 us (2%)
    pallas_call x12, Pallas kernels, call(): pl.pallas_call(kernel, out_shape=list(outs), in_specs=list(ins), out_spec...  25.9 us
    ppermute x2, waiting for transfers between devices, spread(): lax.ppermute(send, 'opt', [(o, o ^ m) for o in range(n_opt)])  19 us
    ppermute x6, waiting for transfers between devices, reduce_scatter(): got.append(lax.ppermute(parts[number], ('dp', 'opt'), perm))  14.6 us
    ppermute x6, starting transfers between devices, reduce_scatter(): lax.ppermute(parts[m], 'dp', [(i, i ^ 4 * m) for i in range(n_dp)])  13.1 us
    pallas_call x2, Pallas kernels, adam_matrix(): pl.pallas_call(functools.partial(adam_kernel, plan, mats), grid=(4 * mats...  11.7 us
    ppermute x6, starting transfers between devices, reduce_scatter(): got.append(lax.ppermute(parts[number], ('dp', 'opt'), perm))  9.49 us
    ppermute x6, starting transfers between devices, gather(): lax.ppermute(shard, 'dp', [(i, i ^ 4 * m) for i in range(n_dp)])  9.08 us
    unnamed x33, local copies, waits for them, and re-layouts  8.12 us
  transfers between devices with their start and end apart: 30, of which 12 were waited for; matrix products, arithmetic and copies ran while one was open for 5% of the time, Pallas kernels for 15%

profile of v1, /device:TPU:0, one launch (start us, length us, event | category | flops | bytes accessed | tf_op | source)
XLA Modules:
  0.0 141.1 jit_solution(5097055432331849614)
XLA Ops:
  0.7 1.4 %dynamic-slice_convert_fusion = bf16[192,1536]{1,0:T(8,128)(2,1)S(1)} fusion(f32[192,3072]{1,0:T(8,128)} %w_ref.3, s32[]{:T(128)S(6)} %select_n.25), kind=kLoop, calls=%fused_computation | loop fusion | bytes 1179652 | tf_op jit(solution)/shard_map/convert_element_type | solution.py:443
  2.1 3.0 %collective-permute-start.2 = (bf16[192,1536]{1,0:T(8,128)(2,1)S(1)}, bf16[192,1536]{1,0:T(8,128)(2,1)S(1)}, u32[]{:S(2)}, u32[]{:S(2)}) collective-permute-start(bf16[192,1536]{1,0:T(8,128)(2,1)S(1)} %dynamic-slice_convert_fusion), channel_id=1, source_target_pairs={{0,1},{1,0},{2,3},{3,2},{4,5},{5,4},{6,7},{7,6},{8,9},{9,8},{10,11... | collective-permute-start | bytes 1769480 | tf_op jit(solution)/shard_map/ppermute | solution.py:433
  5.3 0.7 pad_maximum_fusion
  6.1 0.1 copy.23.refs_2_.refs_3_.segc_ref
  6.3 19.0 %collective-permute-done.refs_6_ = bf16[208,768]{1,0:T(8,128)(2,1)S(1)} collective-permute-done((bf16[208,768]{1,0:T(8,128)(2,1)}, bf16[208,768]{1,0:T(8,128)(2,1)S(1)}, u32[]{:S(2)}, u32[]{:S(2)}) %collective-permute-start) | collective-permute-done | bytes 319520 | tf_op jit(solution)/shard_map/ppermute | solution.py:433
  25.5 0.5 collective-permute-start.1
  26.1 1.9 %collective-permute-done.1.refs_7_ = bf16[208,768]{1,0:T(8,128)(2,1)} collective-permute-done((bf16[208,768]{1,0:T(8,128)(2,1)S(1)}, bf16[208,768]{1,0:T(8,128)(2,1)}, u32[]{:S(2)}, u32[]{:S(2)}) %collective-permute-start.1) | collective-permute-done | bytes 319520 | tf_op jit(solution)/shard_map/ppermute | solution.py:336
  28.0 5.9 %attn_forward.1 = (bf16[2,2,192,768]{3,2,1,0:T(8,128)(2,1)S(1)}, bf16[3,384,512]{2,1,0:T(8,128)(2,1)S(1)}, bf16[384,512]{1,0:T(8,128)(2,1)S(1)}, f32[6,1,512]{2,1,0:T(1,128)S(1)}, f32[512,384]{1,0:T(8,128)S(1)}) custom-call(s32[4]{0:T(128)S(1)} %pad_add_fusion.refs_0_.idx_ref, bf16[512,384]{1,0:T(8,128)(2,1)S(1)} %copy-done.6, ...), custom_call_target="tpu_custom_call" | custom-call | flops 1409286144 | bytes 5779472 | tf_op jit(solution)/shard_map/attn_forward/pallas_call | solution.py:72
  34.0 0.8 copy-done.11
  34.8 1.1 copy-done.10
  35.8 1.1 copy-done.12
  36.9 9.2 %mlp_step.1 = (f32[96,16,384]{2,1,0:T(8,128)}, bf16[96,16,384]{2,1,0:T(8,128)(2,1)S(1)}, bf16[512,384]{1,0:T(8,128)(2,1)}, f32[512,384]{1,0:T(8,128)S(1)}, f32[8...) custom-call(s32[4]{0:T(128)S(1)} %pad_add_fusion.refs_0_.idx_ref, f32[512,384]{1,0:T(8,128)S(1)} %get-tuple-element.53.refs_1_, ...), custom_call_target="tpu_custom_call" | custom-call | flops 3623878656 | bytes 9476112 | tf_op jit(solution)/shard_map/mlp_step/pallas_call | solution.py:72
  46.1 0.2 collective-permute-start.17
  46.2 2.6 %attn_back_first.1 = (bf16[384,512]{1,0:T(8,128)(2,1)S(1)}, f32[384,384]{1,0:T(8,128)S(1)}, f32[8,384]{1,0:T(8,128)S(1)}, bf16[3,128,512]{2,1,0:T(8,128)(2,1)S(1)}) custom-call(s32[512,1]{1,0:T(8,128)S(1)} %copy.23.refs_2_.refs_3_.segc_ref, s32[1,512]{1,0:T(1,128)S(1)} %bitcast.8, f32[512,384]{1,0:T(8,128)S(1)} %get-tuple-element.55.dres_ref.refs_2_, ...), custom_call_target="tpu_custom_call" | custom-call | flops 771751936 | bytes 4943872 | tf_op jit(solution)/shard_map/attn_back_first/pallas_call | solution.py:72
  48.9 2.0 %attn_back_next.2.refs_10_ = bf16[3,128,512]{2,1,0:T(8,128)(2,1)S(1)} custom-call(s32[512,1]{1,0:T(8,128)S(1)} %copy.23.refs_2_.refs_3_.segc_ref, s32[1,512]{1,0:T(1,128)S(1)} %bitcast.9, bf16[384,512]{1,0:T(8,128)(2,1)S(1)} %get-tuple-element.65.dmix_ref, bf16[3,384,512]{2,1,0:T(8,128)(2,1)S(1)} %get-tuple-element.58.qkv_ref, ...), custom_call_target="tpu_custom_call" | custom-call | flops 469762048 | bytes 1982464 | tf_op jit(solution)/shard_map/attn_back_next/pallas_call | solution.py:72
  50.9 2.0 %attn_back_next.3.refs_11_ = bf16[3,128,512]{2,1,0:T(8,128)(2,1)S(1)} custom-call(s32[512,1]{1,0:T(8,128)S(1)} %copy.23.refs_2_.refs_3_.segc_ref, s32[1,512]{1,0:T(1,128)S(1)} %bitcast.10, bf16[384,512]{1,0:T(8,128)(2,1)S(1)} %get-tuple-element.65.dmix_ref, bf16[3,384,512]{2,1,0:T(8,128)(2,1)S(1)} %get-tuple-element.58.qkv_ref, ...), custom_call_target="tpu_custom_call" | custom-call | flops 469762048 | bytes 1982464 | tf_op jit(solution)/shard_map/attn_back_next/pallas_call | solution.py:72
  52.9 3.6 %attn_back_last.1 = (f32[49,16,384]{2,1,0:T(8,128)S(1)}, bf16[49,16,384]{2,1,0:T(8,128)(2,1)S(1)}, f32[512,384]{1,0:T(8,128)}) custom-call(s32[4]{0:T(128)S(1)} %pad_add_fusion.refs_0_.idx_ref, bf16[512,384]{1,0:T(8,128)(2,1)S(1)} %copy-done.6, f32[512,384]{1,0:T(8,128)S(1)} %get-tuple-element.55.dres_ref.refs_2_, ...), custom_call_target="tpu_custom_call" | custom-call | flops 905969664 | bytes 6764560 | tf_op jit(solution)/shard_map/attn_back_last/pallas_call | solution.py:72
  56.5 0.4 collective-permute-start.4
  56.8 1.7 %collective-permute-done.4.refs_1_ = bf16[49,16,384]{2,1,0:T(8,128)(2,1)S(1)} collective-permute-done((bf16[49,16,384]{2,1,0:T(8,128)(2,1)S(1)}, bf16[49,16,384]{2,1,0:T(8,128)(2,1)S(1)}, u32[]{:S(2)}, u32[]{:S(2)}) %collective-permute-start.4) | collective-permute-done | bytes 602144 | tf_op jit(solution)/shard_map/ppermute | solution.py:336
  58.5 0.1 add_core_attn.1
  58.6 1.8 %collective-permute-start.5 = (bf16[13,16,384]{2,1,0:T(8,128)(2,1)S(1)}, bf16[13,16,384]{2,1,0:T(8,128)(2,1)S(1)}, u32[]{:S(2)}, u32[]{:S(2)}) collective-permute-start(bf16[13,16,384]{2,1,0:T(8,128)(2,1)S(1)} %get-tuple-element.70), channel_id=1, source_target_pairs={{0,1},{1,0},{2,3},{3,2},{4,5},{5,4},{6,7},{7,6},{8,9},{9,8},{10,11... | collective-permute-start | bytes 479240 | tf_op jit(solution)/shard_map/ppermute | solution.py:355
  60.5 0.2 add_core_mlp.1
  60.7 0.3 collective-permute-start.18
  61.0 1.8 %collective-permute-start.19 = (bf16[24,16,384]{2,1,0:T(8,128)(2,1)S(1)}, bf16[24,16,384]{2,1,0:T(8,128)(2,1)S(1)}, u32[]{:S(2)}, u32[]{:S(2)}) collective-permute-start(bf16[24,16,384]{2,1,0:T(8,128)(2,1)S(1)} %get-tuple-element.85), channel_id=1, source_target_pairs={{0,4},{1,5},{2,6},{3,7},{4,0},{5,1},{6,2},{7,3},{8,12},{9,13},{10,... | collective-permute-start | bytes 884744 | tf_op jit(solution)/shard_map/ppermute | solution.py:355
  62.8 1.4 %collective-permute-start.20 = (bf16[24,16,384]{2,1,0:T(8,128)(2,1)S(1)}, bf16[24,16,384]{2,1,0:T(8,128)(2,1)S(1)}, u32[]{:S(2)}, u32[]{:S(2)}) collective-permute-start(bf16[24,16,384]{2,1,0:T(8,128)(2,1)S(1)} %get-tuple-element.86), channel_id=1, source_target_pairs={{0,5},{1,4},{2,7},{3,6},{4,1},{5,0},{6,3},{7,2},{8,13},{9,12},{10,... | collective-permute-start | bytes 884744 | tf_op jit(solution)/shard_map/ppermute | solution.py:355
  64.2 1.5 %collective-permute-start.6 = (bf16[13,16,384]{2,1,0:T(8,128)(2,1)S(1)}, bf16[13,16,384]{2,1,0:T(8,128)(2,1)S(1)}, u32[]{:S(2)}, u32[]{:S(2)}) collective-permute-start(bf16[13,16,384]{2,1,0:T(8,128)(2,1)S(1)} %get-tuple-element.71), channel_id=1, source_target_pairs={{0,4},{1,5},{2,6},{3,7},{4,0},{5,1},{6,2},{7,3},{8,12},{9,13},{10,... | collective-permute-start | bytes 479240 | tf_op jit(solution)/shard_map/ppermute | solution.py:355
  65.8 2.6 %collective-permute-start.7 = (bf16[13,16,384]{2,1,0:T(8,128)(2,1)S(1)}, bf16[13,16,384]{2,1,0:T(8,128)(2,1)S(1)}, u32[]{:S(2)}, u32[]{:S(2)}) collective-permute-start(bf16[13,16,384]{2,1,0:T(8,128)(2,1)S(1)} %get-tuple-element.72), channel_id=1, source_target_pairs={{0,5},{1,4},{2,7},{3,6},{4,1},{5,0},{6,3},{7,2},{8,13},{9,12},{10,... | collective-permute-start | bytes 479240 | tf_op jit(solution)/shard_map/ppermute | solution.py:355
  68.3 14.6 %collective-permute-done.6.refs_2_ = bf16[13,16,384]{2,1,0:T(8,128)(2,1)S(1)} collective-permute-done((bf16[13,16,384]{2,1,0:T(8,128)(2,1)S(1)}, bf16[13,16,384]{2,1,0:T(8,128)(2,1)S(1)}, u32[]{:S(2)}, u32[]{:S(2)}) %collective-permute-start.6) | collective-permute-done | bytes 159776 | tf_op jit(solution)/shard_map/ppermute | solution.py:355
  83.0 0.1 add_plane_attn.1
  83.1 1.8 %collective-permute-start.8 = (bf16[4,16,384]{2,1,0:T(8,128)(2,1)S(1)}, bf16[4,16,384]{2,1,0:T(8,128)(2,1)S(1)}, u32[]{:S(2)}, u32[]{:S(2)}) collective-permute-start(bf16[4,16,384]{2,1,0:T(8,128)(2,1)S(1)} %get-tuple-element.74), channel_id=1, source_target_pairs={{0,8},{2,10},{4,12},{6,14},{8,0},{10,2},{12,4},{14,6},{16,24},{18,... | collective-permute-start | bytes 147464 | tf_op jit(solution)/shard_map/ppermute | solution.py:365
  84.9 2.6 %collective-permute-start.9 = (bf16[4,16,384]{2,1,0:T(8,128)(2,1)S(1)}, bf16[4,16,384]{2,1,0:T(8,128)(2,1)S(1)}, u32[]{:S(2)}, u32[]{:S(2)}) collective-permute-start(bf16[4,16,384]{2,1,0:T(8,128)(2,1)S(1)} %get-tuple-element.75), channel_id=1, source_target_pairs={{0,16},{2,18},{4,20},{6,22},{8,24},{10,26},{12,28},{14,30},{16,0},... | collective-permute-start | bytes 147464 | tf_op jit(solution)/shard_map/ppermute | solution.py:365
  87.5 0.2 collective-permute-done.8.refs_0_
  87.7 3.3 %collective-permute-start.10 = (bf16[4,16,384]{2,1,0:T(8,128)(2,1)S(1)}, bf16[4,16,384]{2,1,0:T(8,128)(2,1)S(1)}, u32[]{:S(2)}, u32[]{:S(2)}) collective-permute-start(bf16[4,16,384]{2,1,0:T(8,128)(2,1)S(1)} %get-tuple-element.76), channel_id=1, source_target_pairs={{0,24},{2,26},{4,28},{6,30},{8,16},{10,18},{12,20},{14,22},{16,8},... | collective-permute-start | bytes 147464 | tf_op jit(solution)/shard_map/ppermute | solution.py:365
  91.0 2.6 %collective-permute-done.10.refs_2_ = bf16[4,16,384]{2,1,0:T(8,128)(2,1)S(1)} collective-permute-done((bf16[4,16,384]{2,1,0:T(8,128)(2,1)S(1)}, bf16[4,16,384]{2,1,0:T(8,128)(2,1)S(1)}, u32[]{:S(2)}, u32[]{:S(2)}) %collective-permute-start.10) | collective-permute-done | bytes 49184 | tf_op jit(solution)/shard_map/ppermute | solution.py:365
  93.6 0.6 copy-done.8
  94.2 0.1 add_plane_mlp.1
  94.4 2.1 %collective-permute-start.21 = (bf16[6,16,384]{2,1,0:T(8,128)(2,1)S(1)}, bf16[6,16,384]{2,1,0:T(8,128)(2,1)S(1)}, u32[]{:S(2)}, u32[]{:S(2)}) collective-permute-start(bf16[6,16,384]{2,1,0:T(8,128)(2,1)S(1)} %get-tuple-element.88), channel_id=1, source_target_pairs={{0,8},{2,10},{4,12},{6,14},{8,0},{10,2},{12,4},{14,6},{16,24},{18,... | collective-permute-start | bytes 221192 | tf_op jit(solution)/shard_map/ppermute | solution.py:365
  96.4 1.9 %collective-permute-start.22 = (bf16[6,16,384]{2,1,0:T(8,128)(2,1)S(1)}, bf16[6,16,384]{2,1,0:T(8,128)(2,1)S(1)}, u32[]{:S(2)}, u32[]{:S(2)}) collective-permute-start(bf16[6,16,384]{2,1,0:T(8,128)(2,1)S(1)} %get-tuple-element.89), channel_id=1, source_target_pairs={{0,16},{2,18},{4,20},{6,22},{8,24},{10,26},{12,28},{14,30},{16,0},... | collective-permute-start | bytes 221192 | tf_op jit(solution)/shard_map/ppermute | solution.py:365
  98.4 1.4 collective-permute-start.23
  99.8 0.6 constant_dynamic-update-slice_fusion.3
  100.4 2.0 %collective-permute-start.12 = (bf16[3,16,384]{2,1,0:T(8,128)(2,1)S(1)}, bf16[3,16,384]{2,1,0:T(8,128)(2,1)S(1)}, u32[]{:S(2)}, u32[]{:S(2)}) collective-permute-start(bf16[3,16,384]{2,1,0:T(8,128)(2,1)S(1)} %get-tuple-element.77), channel_id=1, source_target_pairs={{0,16},{2,18},{4,20},{6,22},{8,24},{10,26},{12,28},{14,30},{16,0},... | collective-permute-start | bytes 110600 | tf_op jit(solution)/shard_map/ppermute | solution.py:376
  102.4 0.9 collective-permute-start.13
  103.3 1.3 collective-permute-done.23.refs_2_
  104.6 4.9 %collective-permute-start.26 = (bf16[6,16,384]{2,1,0:T(8,128)(2,1)S(1)}, bf16[6,16,384]{2,1,0:T(8,128)(2,1)S(1)}, u32[]{:S(2)}, u32[]{:S(2)}) collective-permute-start(bf16[6,16,384]{2,1,0:T(8,128)(2,1)S(1)} %add_column_mlp.1), channel_id=1, source_target_pairs={{0,24},{2,26},{4,28},{6,30},{8,16},{10,18},{12,20},{14,22},{16,8},... | collective-permute-start | bytes 221192 | tf_op jit(solution)/shard_map/ppermute | solution.py:376
  109.5 0.8 collective-permute-start.25
  110.3 0.5 collective-permute-start.24
  110.8 0.6 constant_dynamic-update-slice_fusion.2
  111.4 0.4 collective-permute-done.26
  111.8 3.0 %collective-permute-done.25 = bf16[6,16,384]{2,1,0:T(8,128)(2,1)S(1)} collective-permute-done((bf16[6,16,384]{2,1,0:T(8,128)(2,1)S(1)}, bf16[6,16,384]{2,1,0:T(8,128)(2,1)S(1)}, u32[]{:S(2)}, u32[]{:S(2)}) %collective-permute-start.25) | collective-permute-done | bytes 73760 | tf_op jit(solution)/shard_map/ppermute | solution.py:376
  114.8 0.6 collective-permute-done.24
  115.4 0.8 pad_maximum_fusion.1.g0
  116.2 1.5 %collective-permute-start.28 = (bf16[24,16,384]{2,1,0:T(8,128)(2,1)}, bf16[24,16,384]{2,1,0:T(8,128)(2,1)}, u32[]{:S(2)}, u32[]{:S(2)}) collective-permute-start(bf16[24,16,384]{2,1,0:T(8,128)(2,1)} %pad_maximum_fusion.1.g0), channel_id=1, source_target_pairs={{0,4},{2,6},{4,0},{6,2},{8,12},{10,14},{12,8},{14,10},{16,20},{18,... | collective-permute-start | bytes 884744 | tf_op jit(solution)/shard_map/ppermute | solution.py:378
  117.7 0.6 constant_dynamic-update-slice_fusion.1
  118.3 0.6 constant_dynamic-update-slice_fusion.g0
  119.0 0.5 collective-permute-start.15
  119.5 3.8 %collective-permute-done.28.g2 = bf16[24,16,384]{2,1,0:T(8,128)(2,1)} collective-permute-done((bf16[24,16,384]{2,1,0:T(8,128)(2,1)}, bf16[24,16,384]{2,1,0:T(8,128)(2,1)}, u32[]{:S(2)}, u32[]{:S(2)}) %collective-permute-start.28) | collective-permute-done | bytes 294944 | tf_op jit(solution)/shard_map/ppermute | solution.py:378
  123.2 1.3 reshape.77
  124.6 0.5 collective-permute-start.14
  125.1 1.4 %multiply_subtract_fusion = (f32[2304]{0:T(1024)}, f32[2304]{0:T(1024)}, f32[2304]{0:T(1024)}) fusion(f32[2304]{0:T(1024)S(1)} %copy-done.14, f32[6144]{0:T(1024)} %reshape.77, s32[]{:T(128)S(6)} %select_n.26, f32[2304]{0:T(1024)} %param.22, f32[2304]{0:T(1024)} %param.23), kind=kLoop, calls=%fused_computation.6 | loop fusion | flops 34560 | bytes 64516 | tf_op jit(solution)/shard_map/sub | solution.py:387
  126.5 0.1 collective-permute-done.16.g3
  126.7 1.4 copy-done.4
  128.1 1.3 copy-done.5
  129.4 3.8 %adam_1.1 = (f32[192,1536]{1,0:T(8,128)}, f32[192,1536]{1,0:T(8,128)}, f32[192,1536]{1,0:T(8,128)}) custom-call(s32[4]{0:T(128)S(1)} %pad_add_fusion.refs_0_.idx_ref, bf16[12,16,384]{2,1,0:T(8,128)(2,1)} %constant_dynamic-update-slice_fusion.g0, bf16[12,16,384]{2,1,0:T(8,128)(2,1)S(1)} %collective-permute-done.14.g1, ...), custom_call_target="tpu_custom_call" | custom-call | flops 4718592 | bytes 7077888 | tf_op jit(solution)/shard_map/adam_1/pallas_call | solution.py:410
  133.2 7.9 %adam_2.1 = (f32[192,3072]{1,0:T(8,128)}, f32[192,3072]{1,0:T(8,128)}, f32[192,3072]{1,0:T(8,128)}) custom-call(s32[4]{0:T(128)S(1)} %pad_add_fusion.refs_0_.idx_ref, bf16[24,16,384]{2,1,0:T(8,128)(2,1)} %pad_maximum_fusion.1.g0, bf16[24,16,384]{2,1,0:T(8,128)(2,1)} %collective-permute-done.27.g1, bf16[24,16,384]{2,1,0:T(8,128)(2,1)} %collective-permute-done.28.g2, ...), custom_call_target="tpu_custom_call" | custom-call | flops 9437184 | bytes 14155776 | tf_op jit(solution)/shard_map/adam_2/pallas_call | solution.py:410
  (63 shorter events, 0.6 us)
Async XLA Ops:
  0.6 4.5 %copy-start.14 = (f32[2304]{0:T(1024)S(1)}, f32[2304]{0:T(1024)}, u32[]{:S(2)}) copy-start(f32[2304]{0:T(1024)} %param.21) | copy-start | bytes 27652
  0.7 4.6 %copy-start.3 = (f32[192,1536]{1,0:T(8,128)S(1)}, f32[192,1536]{1,0:T(8,128)}, u32[]{:S(2)}) copy-start(f32[192,1536]{1,0:T(8,128)} %w_ref.2) | copy-start | bytes 3538948
  0.7 5.4 %copy-start.7 = (s32[512]{0:T(512)S(1)}, s32[512]{0:T(512)}, u32[]{:S(2)}) copy-start(s32[512]{0:T(512)} %param.13) | copy-start | bytes 6148
  0.7 27.3 %copy-start.6 = (bf16[512,384]{1,0:T(8,128)(2,1)S(1)}, bf16[512,384]{1,0:T(8,128)(2,1)}, u32[]{:S(2)}) copy-start(bf16[512,384]{1,0:T(8,128)(2,1)} %refs_1_.3) | copy-start | bytes 1179652
  2.1 23.2 %collective-permute-start.2 = (bf16[192,1536]{1,0:T(8,128)(2,1)S(1)}, bf16[192,1536]{1,0:T(8,128)(2,1)S(1)}, u32[]{:S(2)}, u32[]{:S(2)}) collective-permute-start(bf16[192,1536]{1,0:T(8,128)(2,1)S(1)} %dynamic-slice_convert_fusion), channel_id=1, source_target_pairs={{0,1},{1,0},{2,3},{3,2},{4,5},{5,4},{6,7},{7,6},{8,9},{9,8},{10,11... | collective-permute-start | bytes 1769480 | tf_op jit(solution)/shard_map/ppermute | solution.py:433
  6.0 19.3 %collective-permute-start = (bf16[208,768]{1,0:T(8,128)(2,1)}, bf16[208,768]{1,0:T(8,128)(2,1)S(1)}, u32[]{:S(2)}, u32[]{:S(2)}) collective-permute-start(bf16[208,768]{1,0:T(8,128)(2,1)} %pad_maximum_fusion), channel_id=1, source_target_pairs={{0,1},{1,0},{2,3},{3,2},{4,5},{5,4},{6,7},{7,6},{8,9},{9,8},{10,11... | collective-permute-start | bytes 958472 | tf_op jit(solution)/shard_map/ppermute | solution.py:433
  25.4 8.6 %copy-start.9 = (bf16[192,1536]{1,0:T(8,128)(2,1)}, bf16[192,1536]{1,0:T(8,128)(2,1)S(1)}, u32[]{:S(2)}) copy-start(bf16[192,1536]{1,0:T(8,128)(2,1)S(1)} %collective-permute-done.2.refs_7_) | copy-start | bytes 1769476
  25.4 8.6 %collective-permute-start.3 = (bf16[192,1536]{1,0:T(8,128)(2,1)S(1)}, bf16[192,1536]{1,0:T(8,128)(2,1)S(1)}, u32[]{:S(2)}, u32[]{:S(2)}) collective-permute-start(bf16[192,1536]{1,0:T(8,128)(2,1)S(1)} %collective-permute-done.2.refs_7_), channel_id=1, source_target_pairs={{0,2},{2,0},{4,6},{6,4},{8,10},{10,8},{12,14},{14,12},{16,18},{18,... | collective-permute-start | bytes 1769480 | tf_op jit(solution)/shard_map/ppermute | solution.py:336
  25.5 2.5 %collective-permute-start.1 = (bf16[208,768]{1,0:T(8,128)(2,1)S(1)}, bf16[208,768]{1,0:T(8,128)(2,1)}, u32[]{:S(2)}, u32[]{:S(2)}) collective-permute-start(bf16[208,768]{1,0:T(8,128)(2,1)S(1)} %collective-permute-done.refs_6_), channel_id=1, source_target_pairs={{0,2},{2,0},{4,6},{6,4},{8,10},{10,8},{12,14},{14,12},{16,18},{18,... | collective-permute-start | bytes 958472 | tf_op jit(solution)/shard_map/ppermute | solution.py:336
  28.0 6.8 %copy-start.13 = (bf16[512,384]{1,0:T(8,128)(2,1)S(1)}, bf16[512,384]{1,0:T(8,128)(2,1)}, u32[]{:S(2)}) copy-start(bf16[512,384]{1,0:T(8,128)(2,1)} %refs_2_.1) | copy-start | bytes 1179652
  34.0 0.8 copy-start.11
  34.8 1.1 copy-start.10
  35.8 1.1 copy-start.12
  46.1 14.4 %collective-permute-start.17 = (bf16[96,16,384]{2,1,0:T(8,128)(2,1)S(1)}, bf16[96,16,384]{2,1,0:T(8,128)(2,1)S(1)}, u32[]{:S(2)}, u32[]{:S(2)}) collective-permute-start(bf16[96,16,384]{2,1,0:T(8,128)(2,1)S(1)} %get-tuple-element.82), channel_id=1, source_target_pairs={{0,2},{2,0},{4,6},{6,4},{8,10},{10,8},{12,14},{14,12},{16,18},{18,... | collective-permute-start | bytes 3538952 | tf_op jit(solution)/shard_map/ppermute | solution.py:336
  52.9 7.6 %copy-start.1 = (f32[96,16,384]{2,1,0:T(8,128)S(1)}, f32[96,16,384]{2,1,0:T(8,128)}, u32[]{:S(2)}) copy-start(f32[96,16,384]{2,1,0:T(8,128)} %get-tuple-element.81.refs_0_) | copy-start | bytes 7077892
  56.5 2.0 %collective-permute-start.4 = (bf16[49,16,384]{2,1,0:T(8,128)(2,1)S(1)}, bf16[49,16,384]{2,1,0:T(8,128)(2,1)S(1)}, u32[]{:S(2)}, u32[]{:S(2)}) collective-permute-start(bf16[49,16,384]{2,1,0:T(8,128)(2,1)S(1)} %get-tuple-element.68), channel_id=1, source_target_pairs={{0,2},{2,0},{4,6},{6,4},{8,10},{10,8},{12,14},{14,12},{16,18},{18,... | collective-permute-start | bytes 1806344 | tf_op jit(solution)/shard_map/ppermute | solution.py:336
  58.6 7.1 %collective-permute-start.5 = (bf16[13,16,384]{2,1,0:T(8,128)(2,1)S(1)}, bf16[13,16,384]{2,1,0:T(8,128)(2,1)S(1)}, u32[]{:S(2)}, u32[]{:S(2)}) collective-permute-start(bf16[13,16,384]{2,1,0:T(8,128)(2,1)S(1)} %get-tuple-element.70), channel_id=1, source_target_pairs={{0,1},{1,0},{2,3},{3,2},{4,5},{5,4},{6,7},{7,6},{8,9},{9,8},{10,11... | collective-permute-start | bytes 479240 | tf_op jit(solution)/shard_map/ppermute | solution.py:355
  60.7 33.5 %collective-permute-start.18 = (bf16[24,16,384]{2,1,0:T(8,128)(2,1)S(1)}, bf16[24,16,384]{2,1,0:T(8,128)(2,1)S(1)}, u32[]{:S(2)}, u32[]{:S(2)}) collective-permute-start(bf16[24,16,384]{2,1,0:T(8,128)(2,1)S(1)} %get-tuple-element.84), channel_id=1, source_target_pairs={{0,1},{1,0},{2,3},{3,2},{4,5},{5,4},{6,7},{7,6},{8,9},{9,8},{10,11... | collective-permute-start | bytes 884744 | tf_op jit(solution)/shard_map/ppermute | solution.py:355
  61.0 33.2 %collective-permute-start.19 = (bf16[24,16,384]{2,1,0:T(8,128)(2,1)S(1)}, bf16[24,16,384]{2,1,0:T(8,128)(2,1)S(1)}, u32[]{:S(2)}, u32[]{:S(2)}) collective-permute-start(bf16[24,16,384]{2,1,0:T(8,128)(2,1)S(1)} %get-tuple-element.85), channel_id=1, source_target_pairs={{0,4},{1,5},{2,6},{3,7},{4,0},{5,1},{6,2},{7,3},{8,12},{9,13},{10,... | collective-permute-start | bytes 884744 | tf_op jit(solution)/shard_map/ppermute | solution.py:355
  62.8 31.4 %collective-permute-start.20 = (bf16[24,16,384]{2,1,0:T(8,128)(2,1)S(1)}, bf16[24,16,384]{2,1,0:T(8,128)(2,1)S(1)}, u32[]{:S(2)}, u32[]{:S(2)}) collective-permute-start(bf16[24,16,384]{2,1,0:T(8,128)(2,1)S(1)} %get-tuple-element.86), channel_id=1, source_target_pairs={{0,5},{1,4},{2,7},{3,6},{4,1},{5,0},{6,3},{7,2},{8,13},{9,12},{10,... | collective-permute-start | bytes 884744 | tf_op jit(solution)/shard_map/ppermute | solution.py:355
  64.2 18.7 %collective-permute-start.6 = (bf16[13,16,384]{2,1,0:T(8,128)(2,1)S(1)}, bf16[13,16,384]{2,1,0:T(8,128)(2,1)S(1)}, u32[]{:S(2)}, u32[]{:S(2)}) collective-permute-start(bf16[13,16,384]{2,1,0:T(8,128)(2,1)S(1)} %get-tuple-element.71), channel_id=1, source_target_pairs={{0,4},{1,5},{2,6},{3,7},{4,0},{5,1},{6,2},{7,3},{8,12},{9,13},{10,... | collective-permute-start | bytes 479240 | tf_op jit(solution)/shard_map/ppermute | solution.py:355
  65.8 17.2 %collective-permute-start.7 = (bf16[13,16,384]{2,1,0:T(8,128)(2,1)S(1)}, bf16[13,16,384]{2,1,0:T(8,128)(2,1)S(1)}, u32[]{:S(2)}, u32[]{:S(2)}) collective-permute-start(bf16[13,16,384]{2,1,0:T(8,128)(2,1)S(1)} %get-tuple-element.72), channel_id=1, source_target_pairs={{0,5},{1,4},{2,7},{3,6},{4,1},{5,0},{6,3},{7,2},{8,13},{9,12},{10,... | collective-permute-start | bytes 479240 | tf_op jit(solution)/shard_map/ppermute | solution.py:355
  83.1 4.6 %collective-permute-start.8 = (bf16[4,16,384]{2,1,0:T(8,128)(2,1)S(1)}, bf16[4,16,384]{2,1,0:T(8,128)(2,1)S(1)}, u32[]{:S(2)}, u32[]{:S(2)}) collective-permute-start(bf16[4,16,384]{2,1,0:T(8,128)(2,1)S(1)} %get-tuple-element.74), channel_id=1, source_target_pairs={{0,8},{2,10},{4,12},{6,14},{8,0},{10,2},{12,4},{14,6},{16,24},{18,... | collective-permute-start | bytes 147464 | tf_op jit(solution)/shard_map/ppermute | solution.py:365
  84.9 6.1 %collective-permute-start.9 = (bf16[4,16,384]{2,1,0:T(8,128)(2,1)S(1)}, bf16[4,16,384]{2,1,0:T(8,128)(2,1)S(1)}, u32[]{:S(2)}, u32[]{:S(2)}) collective-permute-start(bf16[4,16,384]{2,1,0:T(8,128)(2,1)S(1)} %get-tuple-element.75), channel_id=1, source_target_pairs={{0,16},{2,18},{4,20},{6,22},{8,24},{10,26},{12,28},{14,30},{16,0},... | collective-permute-start | bytes 147464 | tf_op jit(solution)/shard_map/ppermute | solution.py:365
  87.7 5.9 %collective-permute-start.10 = (bf16[4,16,384]{2,1,0:T(8,128)(2,1)S(1)}, bf16[4,16,384]{2,1,0:T(8,128)(2,1)S(1)}, u32[]{:S(2)}, u32[]{:S(2)}) collective-permute-start(bf16[4,16,384]{2,1,0:T(8,128)(2,1)S(1)} %get-tuple-element.76), channel_id=1, source_target_pairs={{0,24},{2,26},{4,28},{6,30},{8,16},{10,18},{12,20},{14,22},{16,8},... | collective-permute-start | bytes 147464 | tf_op jit(solution)/shard_map/ppermute | solution.py:365
  93.6 0.6 copy-start.8
  94.2 16.1 %collective-permute-start.11 = (bf16[3,16,384]{2,1,0:T(8,128)(2,1)S(1)}, bf16[3,16,384]{2,1,0:T(8,128)(2,1)S(1)}, u32[]{:S(2)}, u32[]{:S(2)}) collective-permute-start(bf16[3,16,384]{2,1,0:T(8,128)(2,1)S(1)} %get-tuple-element.77), channel_id=1, source_target_pairs={{0,8},{2,10},{4,12},{6,14},{8,0},{10,2},{12,4},{14,6},{16,24},{18,... | collective-permute-start | bytes 110600 | tf_op jit(solution)/shard_map/ppermute | solution.py:376
  94.4 8.1 %collective-permute-start.21 = (bf16[6,16,384]{2,1,0:T(8,128)(2,1)S(1)}, bf16[6,16,384]{2,1,0:T(8,128)(2,1)S(1)}, u32[]{:S(2)}, u32[]{:S(2)}) collective-permute-start(bf16[6,16,384]{2,1,0:T(8,128)(2,1)S(1)} %get-tuple-element.88), channel_id=1, source_target_pairs={{0,8},{2,10},{4,12},{6,14},{8,0},{10,2},{12,4},{14,6},{16,24},{18,... | collective-permute-start | bytes 221192 | tf_op jit(solution)/shard_map/ppermute | solution.py:365
  96.4 6.9 %collective-permute-start.22 = (bf16[6,16,384]{2,1,0:T(8,128)(2,1)S(1)}, bf16[6,16,384]{2,1,0:T(8,128)(2,1)S(1)}, u32[]{:S(2)}, u32[]{:S(2)}) collective-permute-start(bf16[6,16,384]{2,1,0:T(8,128)(2,1)S(1)} %get-tuple-element.89), channel_id=1, source_target_pairs={{0,16},{2,18},{4,20},{6,22},{8,24},{10,26},{12,28},{14,30},{16,0},... | collective-permute-start | bytes 221192 | tf_op jit(solution)/shard_map/ppermute | solution.py:365
  98.4 6.2 %collective-permute-start.23 = (bf16[6,16,384]{2,1,0:T(8,128)(2,1)S(1)}, bf16[6,16,384]{2,1,0:T(8,128)(2,1)S(1)}, u32[]{:S(2)}, u32[]{:S(2)}) collective-permute-start(bf16[6,16,384]{2,1,0:T(8,128)(2,1)S(1)} %get-tuple-element.90), channel_id=1, source_target_pairs={{0,24},{2,26},{4,28},{6,30},{8,16},{10,18},{12,20},{14,22},{16,8},... | collective-permute-start | bytes 221192 | tf_op jit(solution)/shard_map/ppermute | solution.py:365
  100.4 17.3 %collective-permute-start.12 = (bf16[3,16,384]{2,1,0:T(8,128)(2,1)S(1)}, bf16[3,16,384]{2,1,0:T(8,128)(2,1)S(1)}, u32[]{:S(2)}, u32[]{:S(2)}) collective-permute-start(bf16[3,16,384]{2,1,0:T(8,128)(2,1)S(1)} %get-tuple-element.77), channel_id=1, source_target_pairs={{0,16},{2,18},{4,20},{6,22},{8,24},{10,26},{12,28},{14,30},{16,0},... | collective-permute-start | bytes 110600 | tf_op jit(solution)/shard_map/ppermute | solution.py:376
  102.4 15.9 %collective-permute-start.13 = (bf16[3,16,384]{2,1,0:T(8,128)(2,1)S(1)}, bf16[3,16,384]{2,1,0:T(8,128)(2,1)S(1)}, u32[]{:S(2)}, u32[]{:S(2)}) collective-permute-start(bf16[3,16,384]{2,1,0:T(8,128)(2,1)S(1)} %get-tuple-element.77), channel_id=1, source_target_pairs={{0,24},{2,26},{4,28},{6,30},{8,16},{10,18},{12,20},{14,22},{16,8},... | collective-permute-start | bytes 110600 | tf_op jit(solution)/shard_map/ppermute | solution.py:376
  104.6 7.2 %collective-permute-start.26 = (bf16[6,16,384]{2,1,0:T(8,128)(2,1)S(1)}, bf16[6,16,384]{2,1,0:T(8,128)(2,1)S(1)}, u32[]{:S(2)}, u32[]{:S(2)}) collective-permute-start(bf16[6,16,384]{2,1,0:T(8,128)(2,1)S(1)} %add_column_mlp.1), channel_id=1, source_target_pairs={{0,24},{2,26},{4,28},{6,30},{8,16},{10,18},{12,20},{14,22},{16,8},... | collective-permute-start | bytes 221192 | tf_op jit(solution)/shard_map/ppermute | solution.py:376
  109.5 5.4 %collective-permute-start.25 = (bf16[6,16,384]{2,1,0:T(8,128)(2,1)S(1)}, bf16[6,16,384]{2,1,0:T(8,128)(2,1)S(1)}, u32[]{:S(2)}, u32[]{:S(2)}) collective-permute-start(bf16[6,16,384]{2,1,0:T(8,128)(2,1)S(1)} %add_column_mlp.1), channel_id=1, source_target_pairs={{0,16},{2,18},{4,20},{6,22},{8,24},{10,26},{12,28},{14,30},{16,0},... | collective-permute-start | bytes 221192 | tf_op jit(solution)/shard_map/ppermute | solution.py:376
  110.3 5.1 %collective-permute-start.24 = (bf16[6,16,384]{2,1,0:T(8,128)(2,1)S(1)}, bf16[6,16,384]{2,1,0:T(8,128)(2,1)S(1)}, u32[]{:S(2)}, u32[]{:S(2)}) collective-permute-start(bf16[6,16,384]{2,1,0:T(8,128)(2,1)S(1)} %add_column_mlp.1), channel_id=1, source_target_pairs={{0,8},{2,10},{4,12},{6,14},{8,0},{10,2},{12,4},{14,6},{16,24},{18,... | collective-permute-start | bytes 221192 | tf_op jit(solution)/shard_map/ppermute | solution.py:376
  115.4 17.7 %copy-start.2 = (f32[192,3072]{1,0:T(8,128)S(1)}, f32[192,3072]{1,0:T(8,128)}, u32[]{:S(2)}) copy-start(f32[192,3072]{1,0:T(8,128)} %m_ref.3) | copy-start | bytes 7077892
  116.2 7.0 %collective-permute-start.28 = (bf16[24,16,384]{2,1,0:T(8,128)(2,1)}, bf16[24,16,384]{2,1,0:T(8,128)(2,1)}, u32[]{:S(2)}, u32[]{:S(2)}) collective-permute-start(bf16[24,16,384]{2,1,0:T(8,128)(2,1)} %pad_maximum_fusion.1.g0), channel_id=1, source_target_pairs={{0,4},{2,6},{4,0},{6,2},{8,12},{10,14},{12,8},{14,10},{16,20},{18,... | collective-permute-start | bytes 884744 | tf_op jit(solution)/shard_map/ppermute | solution.py:378
  119.0 6.1 %collective-permute-start.15 = (bf16[12,16,384]{2,1,0:T(8,128)(2,1)}, bf16[12,16,384]{2,1,0:T(8,128)(2,1)}, u32[]{:S(2)}, u32[]{:S(2)}) collective-permute-start(bf16[12,16,384]{2,1,0:T(8,128)(2,1)} %constant_dynamic-update-slice_fusion.g0), channel_id=1, source_target_pairs={{0,4},{2,6},{4,0},{6,2},{8,12},{10,14},{12,8},{14,10},{16,20},{18,... | collective-permute-start | bytes 442376 | tf_op jit(solution)/shard_map/ppermute | solution.py:378
  119.5 13.7 %collective-permute-start.27 = (bf16[24,16,384]{2,1,0:T(8,128)(2,1)}, bf16[24,16,384]{2,1,0:T(8,128)(2,1)}, u32[]{:S(2)}, u32[]{:S(2)}) collective-permute-start(bf16[24,16,384]{2,1,0:T(8,128)(2,1)} %pad_maximum_fusion.1.g0), channel_id=1, source_target_pairs={{0,2},{2,0},{4,6},{6,4},{8,10},{10,8},{12,14},{14,12},{16,18},{18,... | collective-permute-start | bytes 884744 | tf_op jit(solution)/shard_map/ppermute | solution.py:336
  123.2 9.9 %collective-permute-start.29 = (bf16[24,16,384]{2,1,0:T(8,128)(2,1)}, bf16[24,16,384]{2,1,0:T(8,128)(2,1)}, u32[]{:S(2)}, u32[]{:S(2)}) collective-permute-start(bf16[24,16,384]{2,1,0:T(8,128)(2,1)} %collective-permute-done.28.g2), channel_id=1, source_target_pairs={{0,2},{2,0},{4,6},{6,4},{8,10},{10,8},{12,14},{14,12},{16,18},{18,... | collective-permute-start | bytes 884744 | tf_op jit(solution)/shard_map/ppermute | solution.py:336
  124.6 2.0 %collective-permute-start.14 = (bf16[12,16,384]{2,1,0:T(8,128)(2,1)}, bf16[12,16,384]{2,1,0:T(8,128)(2,1)S(1)}, u32[]{:S(2)}, u32[]{:S(2)}) collective-permute-start(bf16[12,16,384]{2,1,0:T(8,128)(2,1)} %constant_dynamic-update-slice_fusion.g0), channel_id=1, source_target_pairs={{0,2},{2,0},{4,6},{6,4},{8,10},{10,8},{12,14},{14,12},{16,18},{18,... | collective-permute-start | bytes 442376 | tf_op jit(solution)/shard_map/ppermute | solution.py:336
  125.1 1.6 %collective-permute-start.16 = (bf16[12,16,384]{2,1,0:T(8,128)(2,1)}, bf16[12,16,384]{2,1,0:T(8,128)(2,1)S(1)}, u32[]{:S(2)}, u32[]{:S(2)}) collective-permute-start(bf16[12,16,384]{2,1,0:T(8,128)(2,1)} %collective-permute-done.15.g2), channel_id=1, source_target_pairs={{0,2},{2,0},{4,6},{6,4},{8,10},{10,8},{12,14},{14,12},{16,18},{18,... | collective-permute-start | bytes 442376 | tf_op jit(solution)/shard_map/ppermute | solution.py:336
  126.5 6.7 %copy-start = (f32[192,3072]{1,0:T(8,128)S(1)}, f32[192,3072]{1,0:T(8,128)}, u32[]{:S(2)}) copy-start(f32[192,3072]{1,0:T(8,128)} %w_ref.3) | copy-start | bytes 7077892
  126.7 1.4 copy-start.4
  128.1 1.3 copy-start.5

commit v2 on v1

v2 whole, which is shorter than its diff:
```python
import functools
import math

import jax
import jax.numpy as jnp
from jax import lax
from jax.experimental import pallas as pl
from jax.experimental.pallas import tpu as pltpu
from jax.sharding import PartitionSpec as P

D = 384
HEADS = 6
HEAD_DIM = 64
FF = 1536
TOK = 512
QBLK = 256
STEP = 10
VEC_ROWS = 16

norm_eps = 1e-05
beta_one = 0.9
beta_two = 0.95
adam_eps = 1e-08
matrix_rate = 0.15
vector_rate = 0.6
matrix_decay = 0.1
neg_large = -1e30
gelu_c = math.sqrt(2.0 / math.pi)

f32 = jnp.float32
bf16 = jnp.bfloat16
MIB = 1024 * 1024
HOLD = False
ROWS = 96
MLP_CUT = (1536,)

vmem = pl.BlockSpec(memory_space=pltpu.VMEM)


def dot(left, right, dims):
    return lax.dot_general(left, right, ((dims[:1], dims[1:]), ((), ())), preferred_element_type=f32)


def mm(left, right):
    return dot(left, right, (1, 0))


def mm_nt(left, right):
    return dot(left, right, (1, 1))


def mm_tn(left, right):
    return dot(left, right, (0, 0))


def ln_parts(values):
    mean = jnp.mean(values, axis=-1, keepdims=True)
    centred = values - mean
    var = jnp.mean(centred * centred, axis=-1, keepdims=True)
    rstd = lax.rsqrt(var + norm_eps)
    return centred * rstd, rstd


def ln_back(grad, gain, normed, rstd):
    e = grad * gain
    mean_e = jnp.mean(e, axis=-1, keepdims=True)
    mean_en = jnp.mean(e * normed, axis=-1, keepdims=True)
    return (e - mean_e - normed * mean_en) * rstd


def after(value, *others):
    return lax.optimization_barrier((value, *others))[0]


def call(kernel, outs, ins, args, scratch=(), flops=0, name=None, room=12, light=False):
    moved = sum(math.prod(a.shape) * a.dtype.itemsize for a in args)
    moved += sum(math.prod(o.shape) * o.dtype.itemsize for o in outs)
    return pl.pallas_call(
        kernel,
        out_shape=list(outs),
        in_specs=list(ins),
        out_specs=[vmem] * len(outs),
        scratch_shapes=list(scratch),
        compiler_params=pltpu.CompilerParams(vmem_limit_bytes=room * MIB),
        cost_estimate=pl.CostEstimate(
            flops=0 if light else flops, bytes_accessed=0 if light else moved, transcendentals=0
        ),
        name=name,
    )(*args)


def shaped(shape, dtype):
    return jax.ShapeDtypeStruct(shape, dtype)


class Plan:
    def __init__(self, mesh):
        self.n_dp = mesh.shape["dp"]
        self.n_opt = mesh.shape["opt"]
        self.n_z = self.n_dp // 4
        self.own = D // self.n_opt
        self.attn = Stream(self, "attn", 1, 1, VEC_ROWS)
        self.mlp = Stream(self, "mlp", 2, 2, 0)


class Stream:
    def __init__(self, plan, name, mats, split, tail):
        self.name, self.mats, self.split = name, mats, split
        self.chunk = plan.own // split
        self.unit = math.gcd(self.chunk, 16)
        self.per = self.chunk // self.unit
        self.tail = tail // self.unit
        self.shard = mats * self.per
        self.places = 2 * plan.n_opt
        self.piece = split * self.shard
        self.total = self.places * self.piece


def position():
    dp, op = lax.axis_index("dp"), lax.axis_index("opt")
    return dp & 1, (dp >> 1) & 1, dp >> 2, op


def assemble(plan, own_ref, direct, cross, full_ref):
    core, _, _, op = position()
    width = full_ref.shape[3]
    full_ref[op, 0] = own_ref[:, :width]
    full_ref[op, 1] = own_ref[:, width:]
    for half, messages in ((core, direct), (1 - core, cross)):
        lane = 0
        for pieces in messages:
            cols = slice(lane, lane + pieces[0].shape[1])
            lane += pieces[0].shape[1]
            for m in range(1, plan.n_opt):
                full_ref[op ^ m, half, :, cols] = pieces[m - 1][: plan.own, :]


def store_chunks(plan, stream, ref, base, value, mat):
    _, _, zi, op = position()
    for i in range(plan.n_opt * stream.split):
        rel = ((i // stream.split) ^ op) * stream.split + ((i % stream.split) ^ (zi & (stream.split - 1)))
        for t in range(stream.per):
            row = i * stream.chunk + t * stream.unit
            at = base + (rel * stream.mats + mat) * stream.per + t
            ref[at] = value[row : row + stream.unit].astype(ref.dtype)


def split_sends(stream, whole_ref, refs):
    for number, ref in enumerate(refs):
        ref[...] = whole_ref[number * stream.piece : (number + 1) * stream.piece]


def column_of(row):
    return jnp.broadcast_to(row.astype(f32), (8, TOK)).T[:, :1]


def fill_bias(seg_ref, bias_ref):
    key = lax.broadcasted_iota(jnp.int32, (TOK, TOK), 0)
    query = lax.broadcasted_iota(jnp.int32, (TOK, TOK), 1)
    seg_query = seg_ref[...].astype(f32)
    allowed = (column_of(seg_ref[...]) == seg_query) & (key <= query) & ((seg_query >= 0) | (key == query))
    bias_ref[...] = jnp.where(allowed, 0.0, neg_large)


def spread_vec(plan, length, own_ref, direct, piece_ref, vec_ref, bup_ref):
    _, _, _, op = position()
    size = piece_ref.shape[2]
    count, width = length // size, own_ref.shape[1]
    for m in range(plan.n_opt):
        ref = own_ref if m == 0 else direct[m - 1]
        rows = ref[plan.own : plan.own + 16, :].astype(f32)
        for k in range(count):
            row, lane = (k * size) // width, (k * size) % width
            piece_ref[(op ^ m) * count + k] = rows[row : row + 1, lane : lane + size]
    per = D // size

    def row_of(number):
        return jnp.concatenate([piece_ref[number * per + k] for k in range(per)], axis=1)

    for number in range(8):
        vec_ref[number : number + 1, :] = row_of(number)
    for blk in range(2):
        bup_ref[blk] = jnp.concatenate([row_of(8 + 2 * blk), row_of(9 + 2 * blk)], axis=1)


def cast_weights(plan, attn_ref, mlp_ref, attn_low, mlp_low, *halves):
    core = position()[0]
    attn_low[...] = attn_ref[...].astype(bf16)
    mlp_low[...] = mlp_ref[...].astype(bf16)
    lane = 0
    for ref in halves:
        start = pl.multiple_of(core * FF + lane, 128)
        ref[...] = mlp_low[:, pl.ds(start, ref.shape[1])]
        lane += ref.shape[1]


def attn_forward(plan, length, *refs):
    n = plan.n_opt - 1
    tok_ref, seg_ref, own_ref, sent_ref = refs[:4]
    direct, cross = refs[4 : 4 + n], refs[4 + n : 4 + 2 * n]
    full_ref, qkv_ref, mixed_ref, lse_ref, resid_ref, vec_ref, bup_ref, bias_ref, piece_ref = refs[4 + 2 * n :]
    assemble(plan, own_ref, [direct], [cross], full_ref)
    spread_vec(plan, length, sent_ref, direct, piece_ref, vec_ref, bup_ref)
    hidden = tok_ref[...].astype(f32)
    normed, _ = ln_parts(hidden)
    first_in = (normed * vec_ref[0:1, :] + vec_ref[1:2, :]).astype(bf16)
    for number, row in ((0, 2), (1, None), (2, 3)):
        lane = (number % 2) * D
        weight = full_ref[:, number // 2, :, lane : lane + D].reshape(D, D)
        part = mm(first_in, weight)
        if row is not None:
            part = part + vec_ref[row : row + 1, :]
        qkv_ref[number] = part.astype(bf16).T
    fill_bias(seg_ref, bias_ref)

    def one_head(head, carry):
        rows = pl.ds(pl.multiple_of(head * HEAD_DIM, HEAD_DIM), HEAD_DIM)
        for blk in range(TOK // QBLK):
            cols = slice(blk * QBLK, (blk + 1) * QBLK)
            keys = (blk + 1) * QBLK
            query = qkv_ref[0, rows, cols] * bf16(HEAD_DIM**-0.5)
            scores = mm_tn(qkv_ref[1, rows, :keys], query) + bias_ref[:keys, cols]
            top = jnp.max(scores, axis=0, keepdims=True)
            e = jnp.exp(scores - top)
            total = jnp.sum(e, axis=0, keepdims=True)
            probs = (e * (1.0 / total)).astype(bf16)
            mixed_ref[rows, cols] = mm(qkv_ref[2, rows, :keys], probs).astype(bf16)
            lse_ref[pl.ds(head, 1), :, cols] = (top + jnp.log(total)).reshape(1, 1, QBLK)
        return carry

    lax.fori_loop(0, HEADS, one_head, 0, unroll=True)
    out_weight = full_ref[:, 1, :, D:].reshape(D, D)
    resid_ref[...] = hidden + (mm_tn(mixed_ref[...], out_weight) + vec_ref[4:5, :])


def mlp_step(plan, cuts, *refs):
    n = plan.n_opt - 1
    stream = plan.mlp
    resid_ref, cot_ref, seg_ref, vec_ref, bup_ref, own_ref = refs[:6]
    pieces = [refs[6 + n * k : 6 + n * (k + 1)] for k in range(2 * cuts)]
    outs, send_ref = refs[6 + 2 * cuts * n : -1], refs[-1]
    keep_ref, sends = outs[0], outs[1 : 1 + stream.places]
    act_ref, dres_ref, gvec_ref, gbup_ref, full_ref, out_acc, db_acc = outs[1 + stream.places :]
    assemble(plan, own_ref, pieces[:cuts], pieces[cuts:], full_ref)
    core, ybit = position()[:2]
    resid = resid_ref[...]
    normed, rstd = ln_parts(resid)
    second_in = (normed * vec_ref[5:6, :] + vec_ref[6:7, :]).astype(bf16)
    second_t = second_in.T
    dy = jnp.where(column_of(seg_ref[...]) >= 0, cot_ref[...].astype(f32), 0.0)
    dy_low = dy.astype(bf16)
    dy_t = dy_low.T
    out_acc[...] = jnp.zeros_like(out_acc)
    db_acc[...] = jnp.zeros_like(db_acc)
    wide = FF // 2

    def one_block(blk, carry):
        cols = pl.ds(pl.multiple_of(blk * wide, wide), wide)
        up = full_ref[:, 0, :, cols].reshape(D, wide)
        down = full_ref[:, 1, :, cols].reshape(D, wide)
        pre = mm(second_in, up) + bup_ref[blk]
        sq = pre * pre
        th = jnp.tanh(gelu_c * pre * (1.0 + 0.044715 * sq))
        half = 0.5 * (1.0 + th)
        act = (pre * half).astype(bf16)
        slope = half + (0.5 * gelu_c) * pre * (1.0 - th * th) * (1.0 + (3 * 0.044715) * sq)
        out_acc[...] += mm_nt(act, down)
        dpre = (mm(dy_low, down) * slope).astype(bf16)
        gbup_ref[blk] = jnp.sum(dpre.astype(f32), axis=0, keepdims=True)
        db_acc[...] += mm_nt(dpre, up)
        base = (blk ^ ybit) * (stream.total // 2)
        for mat, (left, right) in enumerate(((second_t, dpre), (dy_t, act))):
            grad = mm(left, right)
            first, last = grad[:, :D], grad[:, D:]
            store_chunks(plan, stream, keep_ref, base, jnp.where(core == 0, first, last), mat)
            store_chunks(plan, stream, send_ref, base, jnp.where(core == 0, last, first), mat)
        return carry

    lax.fori_loop(0, 2, one_block, 0, unroll=True)
    split_sends(stream, send_ref, sends)
    act_ref[...] = (resid + out_acc[...] + vec_ref[7:8, :]).astype(bf16)
    db = db_acc[...]
    dres_ref[...] = dy + ln_back(db, vec_ref[5:6, :], normed, rstd)
    gvec_ref[0:1, :] = jnp.sum(db * normed, axis=0, keepdims=True)
    gvec_ref[1:2, :] = jnp.sum(db, axis=0, keepdims=True)
    gvec_ref[2:3, :] = jnp.sum(dy, axis=0, keepdims=True)
    gvec_ref[3:8, :] = jnp.zeros((5, D), f32)


def back_heads(first, last, qkv_ref, bias_ref, lse_ref, dmix_ref, dqkv_ref, dkv_acc):
    scale = HEAD_DIM**-0.5
    for head in range(first, last):
        rows = slice(head * HEAD_DIM, (head + 1) * HEAD_DIM)
        out_rows = slice((head - first) * HEAD_DIM, (head - first + 1) * HEAD_DIM)
        for blk in range(TOK // QBLK):
            cols = slice(blk * QBLK, (blk + 1) * QBLK)
            keys = (blk + 1) * QBLK
            query = qkv_ref[0, rows, cols]
            key = qkv_ref[1, rows, :keys]
            value = qkv_ref[2, rows, :keys]
            dmix = dmix_ref[rows, cols]
            scores = mm_tn(key, query * bf16(scale)) + bias_ref[:keys, cols]
            probs = jnp.exp(scores - lse_ref[head][:, cols])
            dprobs = mm_tn(value, dmix)
            row_dot = jnp.sum(probs * dprobs, axis=0, keepdims=True)
            dscores = (probs * (dprobs - row_dot)).astype(bf16)
            dqkv_ref[0, out_rows, cols] = (mm(key, dscores) * scale).astype(bf16)
            dkey = mm_nt(query, dscores)
            dvalue = mm_nt(dmix, probs.astype(bf16))
            if blk == 0:
                dkv_acc[0, :, :QBLK] = dkey
                dkv_acc[1, :, :QBLK] = dvalue
            else:
                dkv_acc[0, :, :QBLK] += dkey[:, :QBLK]
                dkv_acc[1, :, :QBLK] += dvalue[:, :QBLK]
                dkv_acc[0, :, QBLK:] = dkey[:, QBLK:]
                dkv_acc[1, :, QBLK:] = dvalue[:, QBLK:]
        dqkv_ref[1, out_rows, :] = (dkv_acc[0] * scale).astype(bf16)
        dqkv_ref[2, out_rows, :] = dkv_acc[1].astype(bf16)


def attn_back_first(last, seg_ref, dres_ref, full_ref, mixed_ref, qkv_ref, lse_ref,
                    dmix_ref, gout_ref, gbo_ref, dqkv_ref, bias_ref, dkv_acc):
    dz = dres_ref[...].astype(bf16)
    gbo_ref[...] = jnp.broadcast_to(jnp.sum(dz.astype(f32), axis=0, keepdims=True), (8, D))
    out_weight = full_ref[:, 1, :, D:].reshape(D, D)
    dmix_ref[...] = mm_nt(out_weight, dz).astype(bf16)
    gout_ref[...] = mm(mixed_ref[...], dz)
    fill_bias(seg_ref, bias_ref)
    back_heads(0, last, qkv_ref, bias_ref, lse_ref, dmix_ref, dqkv_ref, dkv_acc)


def attn_back_next(first, last, seg_ref, dmix_ref, qkv_ref, lse_ref, *refs):
    sources, dqkv_ref, states, (bias_ref, dkv_acc, sems) = refs[:6], refs[6], refs[7:13], refs[13:]
    copies = [pltpu.make_async_copy(src, dst, sems.at[k]) for k, (src, dst) in enumerate(zip(sources, states))]
    for copy in copies:
        copy.start()
    fill_bias(seg_ref, bias_ref)
    back_heads(first, last, qkv_ref, bias_ref, lse_ref, dmix_ref, dqkv_ref, dkv_acc)
    for copy in copies:
        copy.wait()


def attn_back_last(plan, count, *refs):
    stream = plan.attn
    tok_ref, dres_ref, full_ref, vec_ref, gout_ref, gbo_ref, gvec_ref, gbup_ref = refs[:8]
    parts = refs[8 : 8 + count]
    keep_ref, sends = refs[8 + count], refs[9 + count : 9 + count + stream.places]
    tail_ref, igrad_ref, send_ref = refs[9 + count + stream.places :]
    core, ybit = position()[:2]
    hidden = tok_ref[...].astype(f32)
    normed, rstd = ln_parts(hidden)
    first_in = (normed * vec_ref[0:1, :] + vec_ref[1:2, :]).astype(bf16)
    first_t = first_in.T
    dqkv = [jnp.concatenate([part[number] for part in parts], axis=0) for number in range(3)]
    grads = [mm_nt(first_t, dpart) for dpart in dqkv] + [gout_ref[...]]
    for pair in range(2):
        base = (pair ^ ybit) * (stream.total // 2)
        first, last = grads[2 * pair], grads[2 * pair + 1]
        store_chunks(plan, stream, keep_ref, base, jnp.where(core == 0, first, last), 0)
        store_chunks(plan, stream, send_ref, base, jnp.where(core == 0, last, first), 0)
    split_sends(stream, send_ref, sends)
    da_t = jnp.zeros((D, TOK), f32)
    for number in range(3):
        lane = (number % 2) * D
        weight = full_ref[:, number // 2, :, lane : lane + D].reshape(D, D)
        da_t = da_t + mm(weight, dqkv[number])
    da = da_t.T
    igrad_ref[...] = dres_ref[...] + ln_back(da, vec_ref[0:1, :], normed, rstd)
    ones = jnp.ones((8, TOK), bf16)
    rows = [
        jnp.sum(da * normed, axis=0, keepdims=True),
        jnp.sum(da, axis=0, keepdims=True),
        mm_nt(ones, dqkv[0])[0:1, :],
        mm_nt(ones, dqkv[2])[0:1, :],
        gbo_ref[0:1, :],
        gvec_ref[0:3, :],
    ]
    for blk in range(2):
        rows += [gbup_ref[blk][:, :D], gbup_ref[blk][:, D:]]
    rows.append(jnp.zeros((VEC_ROWS - 12, D), f32))
    total = jnp.concatenate(rows, axis=0)
    for t in range(stream.tail):
        piece = total[t * stream.unit : (t + 1) * stream.unit]
        keep_ref[stream.total + t] = piece
        tail_ref[t] = piece.astype(bf16)


def add_core(stream, keep_ref, *refs):
    others, outs = refs[: -stream.places], refs[-stream.places :]
    size = stream.piece
    for number in range(stream.places):
        total = keep_ref[number * size : (number + 1) * size] + others[number][...].astype(f32)
        outs[number][:size] = total.astype(outs[number].dtype)
    if stream.tail:
        total = keep_ref[stream.total :] + others[stream.places][...].astype(f32)
        for number in range(stream.places):
            outs[number][size:] = total.astype(outs[number].dtype)


def add_plane(stream, keep_ref, *refs):
    others, outs = refs[: -stream.split], refs[-stream.split :]
    size = outs[0].shape[0]
    for number, out in enumerate(outs):
        part = slice(number * size, (number + 1) * size)
        total = keep_ref[part]
        for other in others:
            total = total + other[part].astype(f32)
        out[...] = total.astype(out.dtype)


def add_two(left_ref, right_ref, *outs):
    total = left_ref[...].astype(f32) + right_ref[...].astype(f32)
    size = outs[0].shape[0]
    outs[0][...] = total[:size].astype(outs[0].dtype)
    if len(outs) > 1:
        outs[1][...] = total[size:]


def add_last(plan, stream, left_ref, right_ref, w_ref, m_ref, v_ref, out_ref, nw_ref, nm_ref, nv_ref, sum_ref):
    out_ref[...] = (left_ref[: stream.shard].astype(f32) + right_ref[: stream.shard].astype(f32)).astype(bf16)
    total = left_ref[stream.shard :].astype(f32) + right_ref[stream.shard :].astype(f32)
    sum_ref[...] = total.reshape(VEC_ROWS, D)
    op = position()[3]
    count = w_ref.shape[0] // D
    for k in range(count):
        grad = sum_ref[pl.ds(op * count + k, 1), :].reshape(D)
        here = slice(k * D, (k + 1) * D)
        out = adamw(w_ref[here], m_ref[here], v_ref[here], grad, vector_rate, 0.0)
        nw_ref[here], nm_ref[here], nv_ref[here] = out


def swap_core(n_dp, value):
    return lax.ppermute(value, "dp", [(i, i ^ 1) for i in range(n_dp)])


def swap_dp(plan, value, mask):
    return lax.ppermute(value, "dp", [(i, i ^ mask) for i in range(plan.n_dp)])


def reduce_core(plan, stream, keep, sends):
    got = [swap_core(plan.n_dp, send) for send in sends]
    shape = (stream.piece + stream.tail, stream.unit, D)
    outs = [shaped(shape, f32 if k == 0 else bf16) for k in range(stream.places)]

    def finish(got):
        return call(
            functools.partial(add_core, stream),
            outs,
            [vmem] * (1 + len(got)),
            [keep, *got],
            name="add_core_" + stream.name,
        )

    return got, finish


def send_plane(plan, parts):
    n_dp, n_opt = plan.n_dp, plan.n_opt
    got = []
    for number in range(1, 2 * n_opt):
        mask_y, mask_o = number // n_opt, number % n_opt
        perm = [
            ((d * n_opt + o), ((d ^ (2 * mask_y)) * n_opt + (o ^ mask_o))) for d in range(n_dp) for o in range(n_opt)
        ]
        got.append(lax.ppermute(parts[number], ("dp", "opt"), perm))
    return got


def reduce_plane(stream, keep, got):
    size = (stream.piece + stream.tail) // stream.split
    first = f32 if stream.split > 1 else bf16
    outs = [shaped((size, stream.unit, D), first if k == 0 else bf16) for k in range(stream.split)]
    return call(
        functools.partial(add_plane, stream),
        outs,
        [vmem] * (1 + len(got)),
        [keep, *got],
        name="add_plane_" + stream.name,
    )


def reduce_pair(stream, left, right, last=False):
    shapes = [shaped(left.shape, bf16)]
    if last and stream.tail:
        shapes = [shaped((stream.shard, stream.unit, D), bf16), shaped((stream.tail, stream.unit, D), f32)]
    return call(add_two, shapes, [vmem] * 2, [left, right], name="add_two_" + stream.name)


def adamw(weight, first, second, grad, rate, decay):
    first = beta_one * first + (1.0 - beta_one) * grad
    second = beta_two * second + (1.0 - beta_two) * grad * grad
    first_hat = first * (1.0 / (1.0 - beta_one**STEP))
    second_hat = second * (1.0 / (1.0 - beta_two**STEP))
    root = second_hat * lax.rsqrt(second_hat)
    weight = weight - rate * (first_hat / (root + adam_eps) + decay * weight)
    return weight, first, second


def adam_kernel(stream, rows, *refs):
    count = 4 * stream.split
    grads = refs[:count]
    w_ref, m_ref, v_ref, nw_ref, nm_ref, nv_ref = refs[count:]
    mat, part = pl.program_id(0), pl.program_id(1)
    core, ybit, zi, _ = position()
    place = core + 2 * ybit
    cuts = stream.chunk // rows
    zrel = (part // cuts) ^ (zi & (stream.split - 1))
    for z in range(stream.split):

        @pl.when(zrel == z)
        def _(z=z):
            for number in range(4):
                ref = grads[z * 4 + number]
                cols = pl.ds(pl.multiple_of((number ^ place) * D, D), D)
                for step in range(rows // stream.unit):
                    at = mat * stream.per + (part % cuts) * (rows // stream.unit) + step
                    here = (slice(step * stream.unit, (step + 1) * stream.unit), cols)
                    grad = ref[at].astype(f32)
                    out = adamw(w_ref[here], m_ref[here], v_ref[here], grad, matrix_rate, matrix_decay)
                    nw_ref[here], nm_ref[here], nv_ref[here] = out


def adam_matrix(plan, stream, grads, weight, first, second):
    rows = min(stream.chunk, ROWS)
    block = pl.BlockSpec((rows, 4 * D), lambda i, k: (k, i))
    shape = shaped(weight.shape, f32)
    states = [weight, first, second]
    if HOLD:
        states = [pltpu.with_memory_space_constraint(x, pltpu.HBM) for x in states]
    return pl.pallas_call(
        functools.partial(adam_kernel, stream, rows),
        grid=(stream.mats, plan.own // rows),
        out_shape=[shape] * 3,
        in_specs=[vmem] * len(grads) + [block] * 3,
        out_specs=[block] * 3,
        compiler_params=pltpu.CompilerParams(vmem_limit_bytes=16 * MIB),
        cost_estimate=pl.CostEstimate(
            flops=16 * weight.size, bytes_accessed=24 * weight.size, transcendentals=weight.size
        ),
        name="adam_" + stream.name,
    )(*grads, *states)


def body(plan, tokens, segment, cotangent, w_attn, m_attn, v_attn, w_mlp, m_mlp, v_mlp, vectors, m_vec, v_vec):
    n_dp, n_opt, own = plan.n_dp, plan.n_opt, plan.own
    core = lax.axis_index("dp") & 1
    seg = segment.reshape(1, TOK)

    def spread(send):
        return [lax.ppermute(send, "opt", [(o, o ^ m) for o in range(n_opt)]) for m in range(1, n_opt)]

    width = 2 * D
    length = vectors.shape[0]
    vec_pad = jnp.pad(vectors.astype(bf16), (0, 16 * width - length)).reshape(16, width)
    attn_half = lax.dynamic_slice(w_attn, (0, core * width), (own, width)).astype(bf16)
    attn_send = jnp.concatenate([attn_half, vec_pad], axis=0)
    attn_direct = spread(attn_send)
    attn_cross = [swap_core(n_dp, piece) for piece in attn_direct]
    widths = MLP_CUT
    attn_low, mlp_low, *mlp_halves = call(
        functools.partial(cast_weights, plan),
        [shaped((own, 4 * D), bf16), shaped((own, 2 * FF), bf16)] + [shaped((own, w), bf16) for w in widths],
        [vmem] * 2,
        [w_attn, after(w_mlp, attn_send)],
        name="cast_weights",
        room=20,
    )
    mlp_direct = [spread(half) for k, half in enumerate(mlp_halves)]
    size = math.gcd(length, D)
    full, qkv, mixed, lse, resid, vec8, bup = call(
        functools.partial(attn_forward, plan, length),
        [
            shaped((n_opt, 2, own, width), bf16),
            shaped((3, D, TOK), bf16),
            shaped((D, TOK), bf16),
            shaped((HEADS, 1, TOK), f32),
            shaped((TOK, D), f32),
            shaped((8, D), f32),
            shaped((2, 1, FF // 2), f32),
        ],
        [vmem] * (4 + 2 * (n_opt - 1)),
        [tokens, seg, attn_low, attn_send, *attn_direct, *attn_cross],
        [pltpu.VMEM((TOK, TOK), f32), pltpu.VMEM((n_opt * length // size, 1, size), f32)],
        flops=2 * TOK * D * 4 * D + 8 * TOK * TOK * D,
        name="attn_forward",
    )
    mlp_cross = [[swap_core(n_dp, after(piece, resid)) for piece in pieces] for pieces in mlp_direct]
    stream = plan.mlp
    mlp_keep, *rest = call(
        functools.partial(mlp_step, plan, len(widths)),
        [
            shaped((stream.total, stream.unit, D), f32),
            *[shaped((stream.piece, stream.unit, D), bf16)] * stream.places,
            shaped((TOK, D), bf16),
            shaped((TOK, D), f32),
            shaped((8, D), f32),
            shaped((2, 1, FF // 2), f32),
        ],
        [vmem] * (6 + 2 * len(widths) * (n_opt - 1)),
        [resid, cotangent, seg, vec8, bup, mlp_low, *sum(mlp_direct, []), *sum(mlp_cross, [])],
        [
            pltpu.VMEM((n_opt, 2, own, FF), bf16),
            pltpu.VMEM((TOK, D), f32),
            pltpu.VMEM((TOK, D), f32),
            pltpu.VMEM((stream.total, stream.unit, D), bf16),
        ],
        flops=12 * TOK * D * FF,
        room=20,
        name="mlp_step",
    )
    mlp_sends, (activations, dres, gvec, gbup) = rest[: stream.places], rest[stream.places :]
    mlp_got, finish = reduce_core(plan, stream, mlp_keep, mlp_sends)

    head_flops = 14 * TOK * TOK * HEAD_DIM
    head_scratch = [pltpu.VMEM((TOK, TOK), f32), pltpu.VMEM((2, HEAD_DIM, TOK), f32)]
    cuts = (0, 2, 6)
    dmix, gout, gbo, part = call(
        functools.partial(attn_back_first, cuts[1]),
        [
            shaped((D, TOK), bf16),
            shaped((D, D), f32),
            shaped((8, D), f32),
            shaped((3, cuts[1] * HEAD_DIM, TOK), bf16),
        ],
        [vmem] * 6,
        [seg, dres, full, mixed, qkv, lse],
        head_scratch,
        flops=4 * TOK * D * D + cuts[1] * head_flops,
        name="attn_back_first",
    )
    mlp_got[0] = after(mlp_got[0], dmix)
    mlp_parts = finish(mlp_got)
    dmix = after(dmix, *mlp_parts)
    states = [w_mlp, m_mlp, v_mlp, w_attn, m_attn, v_attn]
    next_part, *states = call(
        functools.partial(attn_back_next, cuts[1], cuts[2]),
        [shaped((3, (cuts[2] - cuts[1]) * HEAD_DIM, TOK), bf16)] + [shaped(x.shape, f32) for x in states],
        [vmem] * 4 + [pl.BlockSpec(memory_space=pl.ANY)] * 6,
        [seg, dmix, qkv, lse] + [pltpu.with_memory_space_constraint(x, pltpu.HBM) for x in states],
        head_scratch + [pltpu.SemaphoreType.DMA((6,))],
        light=True,
        room=24,
        name="attn_back_next",
    )
    parts = [part, next_part]
    stream = plan.attn
    attn_keep, *attn_sends, input_grad = call(
        functools.partial(attn_back_last, plan, len(parts)),
        [
            shaped((stream.total + stream.tail, stream.unit, D), f32),
            *[shaped((stream.piece, stream.unit, D), bf16)] * stream.places,
            shaped((stream.tail, stream.unit, D), bf16),
            shaped((TOK, D), f32),
        ],
        [vmem] * (8 + len(parts)),
        [tokens, dres, full, vec8, gout, gbo, gvec, gbup, *parts],
        [pltpu.VMEM((stream.total, stream.unit, D), bf16)],
        light=True,
        flops=12 * TOK * D * D,
        name="attn_back_last",
    )
    mlp, attn = plan.mlp, plan.attn
    zbits = [4 << k for k in range(plan.n_z.bit_length() - 1)]
    attn_got, finish = reduce_core(plan, attn, attn_keep, attn_sends)
    mlp_got = send_plane(plan, mlp_parts)
    mlp_keep, mlp_send = reduce_plane(mlp, mlp_parts[0], mlp_got)
    attn_got[0] = after(attn_got[0], mlp_send)
    attn_parts = finish(attn_got)
    mlp_got = swap_dp(plan, mlp_send, zbits[0])
    attn_got = send_plane(plan, attn_parts)
    mlp_got = after(mlp_got, attn_parts[1])
    (mlp_own,) = reduce_pair(mlp, mlp_keep, mlp_got)
    mlp_got = swap_dp(plan, mlp_own, zbits[1])
    attn_got[0] = after(attn_got[0], mlp_own)
    (attn_own,) = reduce_plane(attn, attn_parts[0], attn_got)
    attn_got = swap_dp(plan, attn_own, zbits[0])
    mlp_got = after(mlp_got, attn_own)
    (mlp_own,) = reduce_pair(mlp, mlp_own, mlp_got)
    for mask in zbits[2:]:
        (mlp_own,) = reduce_pair(mlp, mlp_own, swap_dp(plan, mlp_own, mask))
    mlp_z = swap_dp(plan, mlp_own, zbits[0])
    mlp_y = swap_dp(plan, mlp_own, 2)
    attn_got = after(attn_got, mlp_own)
    (attn_own,) = reduce_pair(attn, attn_own, attn_got)
    for mask in zbits[2:]:
        (attn_own,) = reduce_pair(attn, attn_own, swap_dp(plan, attn_own, mask))
    attn_got = swap_dp(plan, attn_own, zbits[1])
    mlp_z = after(mlp_z, attn_own)
    mlp_yz = swap_dp(plan, mlp_z, 2)
    near = [mlp_own, mlp_y, mlp_z, mlp_yz]
    cross = [swap_core(n_dp, x) for x in near]
    mlp_grads = [near[0], cross[0], near[1], cross[1], near[2], cross[2], near[3], cross[3]]
    if length % D == 0:
        vec = shaped((length,), f32)
        attn_own, new_vec, first_vec, second_vec = call(
            functools.partial(add_last, plan, attn),
            [shaped((attn.shard, attn.unit, D), bf16), vec, vec, vec],
            [vmem] * 5,
            [attn_own, attn_got, vectors, m_vec, v_vec],
            [pltpu.VMEM((VEC_ROWS, D), f32)],
            name="add_last",
        )
    else:
        attn_own, vec_grad = reduce_pair(attn, attn_own, attn_got, last=True)
        own_vec = lax.dynamic_slice(vec_grad.reshape(-1), (lax.axis_index("opt") * length,), (length,))
        new_vec, first_vec, second_vec = adamw(vectors, m_vec, v_vec, own_vec, vector_rate, 0.0)
    attn_y = swap_dp(plan, attn_own, 2)
    mlp_grads[0] = after(mlp_grads[0], attn_own)
    new_mlp, first_mlp, second_mlp = adam_matrix(plan, mlp, mlp_grads, *states[:3])
    attn_y = after(attn_y, new_mlp)
    attn_grads = [attn_own, swap_core(n_dp, attn_own), attn_y, swap_core(n_dp, attn_y)]
    new_attn, first_attn, second_attn = adam_matrix(plan, attn, attn_grads, *states[3:])
    return (
        activations,
        input_grad,
        new_attn,
        first_attn,
        second_attn,
        new_mlp,
        first_mlp,
        second_mlp,
        new_vec,
        first_vec,
        second_vec,
    )


def solution(mesh):
    rows, both = P("opt", None), P(("dp", "opt"), None)
    in_specs = (both, P(("dp", "opt")), both) + (rows,) * 6 + (P("opt"),) * 3
    out_specs = (both, both) + (rows,) * 6 + (P("opt"),) * 3
    return jax.shard_map(
        functools.partial(body, Plan(mesh)), mesh=mesh, in_specs=in_specs, out_specs=out_specs, check_vma=False
    )
```

time: 142 us -> 96.2 us (0.68)
  starting transfers between devices: 38.4 us -> 23.5 us
  waiting for transfers between devices: 49.3 us -> 36.9 us
  local copies, waits for them, and re-layouts: 11.8 us -> 2.85 us
  Pallas kernels: 37.6 us -> 31 us
  other arithmetic: 3.05 us -> 0.83 us
    ppermute x20 -> x14, starting transfers between devices: 33.7 us -> 17.6 us  [the longest x8 10.5 us: swap_dp(): return lax.ppermute(value, 'dp', [(i, i ^ mask) for i in range(plan.n_dp)])]
    ppermute x2, waiting for transfers between devices: 19 us -> 11.7 us  [spread(): lax.ppermute(send, 'opt', [(o, o ^ m) for o in range(n_opt)])]
    ppermute x20 -> x14, waiting for transfers between devices: 26.5 us -> 19.6 us  [the longest x8 10.7 us: swap_dp(): return lax.ppermute(value, 'dp', [(i, i ^ mask) for i in range(plan.n_dp)])]
    unnamed x33 -> x16, local copies, waits for them, and re-layouts: 8.12 us -> 1.69 us
    pallas_call x2, Pallas kernels: 11.7 us -> 6.65 us  [adam_matrix(): pl.pallas_call(functools.partial(adam_kernel, stream, rows), grid=(stream...]
    ppermute x8 -> x17, waiting for transfers between devices: 3.76 us -> 5.68 us  [swap_core(): return lax.ppermute(value, 'dp', [(i, i ^ 1) for i in range(n_dp)])]
    pallas_call x12 -> x14, Pallas kernels: 25.9 us -> 24.3 us  [call(): pl.pallas_call(kernel, out_shape=list(outs), in_specs=list(ins), out_spec...]
    reshape x3 -> x0, local copies, waits for them, and re-layouts: 1.51 us -> none  [the longest x1 1.35 us: body(): own_vec = lax.dynamic_slice(vec_grad.reshape(-1), (op * length,), (length,))]
  transfers between devices with their start and end apart: 30 -> 33, of which waited for: 12 -> 15; matrix products, arithmetic and copies ran while one was open for 5% -> 0% of each run, Pallas kernels for 15% -> 23%
where the time goes in v2:
time: 96.2 us; the launch traced here: 95.9 us
  waiting for transfers between devices  36.9 us (38%)
  Pallas kernels  31 us (32%)
  starting transfers between devices  23.5 us (24%)
  local copies, waits for them, and re-layouts  2.85 us (3%)
    pallas_call x14, Pallas kernels, call(): pl.pallas_call(kernel, out_shape=list(outs), in_specs=list(ins), out_spec...  24.3 us
    ppermute x2, waiting for transfers between devices, spread(): lax.ppermute(send, 'opt', [(o, o ^ m) for o in range(n_opt)])  11.7 us
    ppermute x8, waiting for transfers between devices, swap_dp(): return lax.ppermute(value, 'dp', [(i, i ^ mask) for i in range(plan.n_dp)])  10.7 us
    ppermute x8, starting transfers between devices, swap_dp(): return lax.ppermute(value, 'dp', [(i, i ^ mask) for i in range(plan.n_dp)])  10.5 us
    ppermute x6, waiting for transfers between devices, send_plane(): got.append(lax.ppermute(parts[number], ('dp', 'opt'), perm))  8.88 us
    ppermute x6, starting transfers between devices, send_plane(): got.append(lax.ppermute(parts[number], ('dp', 'opt'), perm))  7.11 us
    pallas_call x2, Pallas kernels, adam_matrix(): pl.pallas_call(functools.partial(adam_kernel, stream, rows), grid=(stream...  6.65 us
    ppermute x17, waiting for transfers between devices, swap_core(): return lax.ppermute(value, 'dp', [(i, i ^ 1) for i in range(n_dp)])  5.68 us
  transfers between devices with their start and end apart: 33, of which 15 were waited for; matrix products, arithmetic and copies ran while one was open for 0% of the time, Pallas kernels for 23%

profile of v2, /device:TPU:0, one launch (start us, length us, event | category | flops | bytes accessed | tf_op | source)
XLA Modules:
  0.0 95.9 jit_solution(8819186418790783296)
XLA Ops:
  0.6 0.0 copy-start.1
  0.7 0.8 convert_element_type.9
  1.5 1.1 %dynamic-slice_convert_fusion = bf16[192,768]{1,0:T(8,128)(2,1)S(1)} fusion(f32[192,1536]{1,0:T(8,128)} %refs_3_.1, s32[]{:T(128)S(6)} %select_n.3), kind=kLoop, calls=%fused_computation | loop fusion | bytes 589828 | tf_op jit(solution)/shard_map/convert_element_type | solution.py:556
  2.7 3.0 %collective-permute-start = (bf16[208,768]{1,0:T(8,128)(2,1)S(1)}, bf16[208,768]{1,0:T(8,128)(2,1)S(1)}, u32[]{:S(2)}, u32[]{:S(2)}) collective-permute-start(bf16[208,768]{1,0:T(8,128)(2,1)S(1)} %pad_maximum_fusion.refs_3_), channel_id=1, source_target_pairs={{0,1},{1,0},{2,3},{3,2},{4,5},{5,4},{6,7},{7,6},{8,9},{9,8},{10,11... | collective-permute-start | bytes 958472 | tf_op jit(solution)/shard_map/ppermute | solution.py:551
  5.7 1.7 %copy-done = f32[192,3072]{1,0:T(8,128)S(1)} copy-done((f32[192,3072]{1,0:T(8,128)S(1)}, f32[192,3072]{1,0:T(8,128)}, u32[]{:S(2)}) %copy-start) | copy-done | bytes 2359320
  7.3 0.2 cast_weights.1
  7.6 0.1 collective-permute-start.2
  7.6 6.4 %collective-permute-done.refs_4_ = bf16[208,768]{1,0:T(8,128)(2,1)S(1)} collective-permute-done((bf16[208,768]{1,0:T(8,128)(2,1)S(1)}, bf16[208,768]{1,0:T(8,128)(2,1)S(1)}, u32[]{:S(2)}, u32[]{:S(2)}) %collective-permute-start) | collective-permute-done | bytes 319520 | tf_op jit(solution)/shard_map/ppermute | solution.py:551
  14.0 0.0 collective-permute-start.1
  14.0 1.6 %collective-permute-done.1.refs_5_ = bf16[208,768]{1,0:T(8,128)(2,1)S(1)} collective-permute-done((bf16[208,768]{1,0:T(8,128)(2,1)S(1)}, bf16[208,768]{1,0:T(8,128)(2,1)S(1)}, u32[]{:S(2)}, u32[]{:S(2)}) %collective-permute-start.1) | collective-permute-done | bytes 319520 | tf_op jit(solution)/shard_map/ppermute | solution.py:434
  15.7 4.9 %attn_forward.1 = (bf16[2,2,192,768]{3,2,1,0:T(8,128)(2,1)S(1)}, bf16[3,384,512]{2,1,0:T(8,128)(2,1)S(1)}, bf16[384,512]{1,0:T(8,128)(2,1)S(1)}, f32[6,1,512]{2,...) custom-call(bf16[512,384]{1,0:T(8,128)(2,1)S(1)} %copy-done.2, ...), custom_call_target="tpu_custom_call" | custom-call | flops 1409286144 | bytes 5513216 | tf_op jit(solution)/shard_map/attn_forward/pallas_call | solution.py:78
  20.6 5.3 %collective-permute-done.2.refs_6_ = bf16[192,1536]{1,0:T(8,128)(2,1)S(1)} collective-permute-done((bf16[192,1536]{1,0:T(8,128)(2,1)S(1)}, bf16[192,1536]{1,0:T(8,128)(2,1)S(1)}, u32[]{:S(2)}, u32[]{:S(2)}) %collective-permute-start.2) | collective-permute-done | bytes 589856 | tf_op jit(solution)/shard_map/ppermute | solution.py:551
  25.8 0.0 collective-permute-start.3
  25.8 2.0 %collective-permute-done.3.refs_7_ = bf16[192,1536]{1,0:T(8,128)(2,1)S(1)} collective-permute-done((bf16[192,1536]{1,0:T(8,128)(2,1)S(1)}, bf16[192,1536]{1,0:T(8,128)(2,1)S(1)}, u32[]{:S(2)}, u32[]{:S(2)}) %collective-permute-start.3) | collective-permute-done | bytes 589856 | tf_op jit(solution)/shard_map/ppermute | solution.py:434
  27.8 6.8 %mlp_step.1 = (f32[96,16,384]{2,1,0:T(8,128)S(1)}, bf16[24,16,384]{2,1,0:T(8,128)(2,1)S(1)}, bf16[24,16,384]{2,1,0:T(8,128)(2,1)S(1)}, bf16[24,16,384]{2,1,0:T(8...) custom-call(f32[512,384]{1,0:T(8,128)S(1)} %get-tuple-element.82.ref, ...), custom_call_target="tpu_custom_call" | custom-call | flops 3623878656 | bytes 8296448 | tf_op jit(solution)/shard_map/mlp_step/pallas_call | solution.py:78
  34.6 0.1 collective-permute-start.4
  34.8 0.4 collective-permute-start.5
  35.2 0.1 collective-permute-start.6
  35.3 0.4 collective-permute-start.7
  35.7 2.6 %attn_back_first.1 = (bf16[384,512]{1,0:T(8,128)(2,1)S(1)}, f32[384,384]{1,0:T(8,128)S(1)}, f32[8,384]{1,0:T(8,128)S(1)}, bf16[3,128,512]{2,1,0:T(8,128)(2,1)S(1)}) custom-call(s32[1,512]{1,0:T(1,128)S(1)} %bitcast.3, f32[512,384]{1,0:T(8,128)S(1)} %get-tuple-element.89.dres_ref.refs_1_, bf16[2,2,192,768]{3,2,1,0:T(8,128)(2,1)S(1)} %get-tuple-element.90.full_ref.refs_2_, ...), custom_call_target="tpu_custom_call" | custom-call | flops 771751936 | bytes 4941824 | tf_op jit(solution)/shard_map/attn_back_first/pallas_call | solution.py:78
  38.3 0.0 collective-permute-done.4.refs_0_
  38.3 0.0 collective-permute-done.6.refs_2_
  38.3 0.0 collective-permute-done.7.refs_3_
  38.3 0.3 add_core_mlp.1
  38.6 1.8 %collective-permute-start.9 = (bf16[24,16,384]{2,1,0:T(8,128)(2,1)S(1)}, bf16[24,16,384]{2,1,0:T(8,128)(2,1)S(1)}, u32[]{:S(2)}, u32[]{:S(2)}) collective-permute-start(bf16[24,16,384]{2,1,0:T(8,128)(2,1)S(1)} %get-tuple-element.107), channel_id=1, source_target_pairs={{0,1},{1,0},{2,3},{3,2},{4,5},{5,4},{6,7},{7,6},{8,9},{9,8},{10,11... | collective-permute-start | bytes 884744 | tf_op jit(solution)/shard_map/ppermute | solution.py:466
  40.4 1.5 %collective-permute-start.10 = (bf16[24,16,384]{2,1,0:T(8,128)(2,1)S(1)}, bf16[24,16,384]{2,1,0:T(8,128)(2,1)S(1)}, u32[]{:S(2)}, u32[]{:S(2)}) collective-permute-start(bf16[24,16,384]{2,1,0:T(8,128)(2,1)S(1)} %get-tuple-element.108), channel_id=1, source_target_pairs={{0,4},{1,5},{2,6},{3,7},{4,0},{5,1},{6,2},{7,3},{8,12},{9,13},{10,... | collective-permute-start | bytes 884744 | tf_op jit(solution)/shard_map/ppermute | solution.py:466
  42.0 0.2 collective-permute-start.11
  42.2 5.4 %attn_back_next.1 = (bf16[3,256,512]{2,1,0:T(8,128)(2,1)S(1)}, f32[192,3072]{1,0:T(8,128)S(1)}, f32[192,3072]{1,0:T(8,128)S(1)}, f32[192,3072]{1,0:T(8,128)S(1)}...) custom-call(s32[1,512]{1,0:T(1,128)S(1)} %bitcast.4, ...), custom_call_target="tpu_custom_call" | custom-call | tf_op jit(solution)/shard_map/attn_back_next/pallas_call | solution.py:78
  47.6 3.0 %attn_back_last.1 = (f32[49,16,384]{2,1,0:T(8,128)S(1)}, bf16[12,16,384]{2,1,0:T(8,128)(2,1)S(1)}, bf16[12,16,384]{2,1,0:T(8,128)(2,1)S(1)}, bf16[12,16,384]{2,1...) custom-call(bf16[512,384]{1,0:T(8,128)(2,1)S(1)} %copy-done.2, ...), custom_call_target="tpu_custom_call" | custom-call | tf_op jit(solution)/shard_map/attn_back_last/pallas_call | solution.py:78
  50.6 0.0 collective-permute-start.8
  50.6 0.5 collective-permute-start.12
  51.1 0.0 collective-permute-start.13
  51.1 4.5 %collective-permute-done.10.refs_1_ = bf16[24,16,384]{2,1,0:T(8,128)(2,1)S(1)} collective-permute-done((bf16[24,16,384]{2,1,0:T(8,128)(2,1)S(1)}, bf16[24,16,384]{2,1,0:T(8,128)(2,1)S(1)}, u32[]{:S(2)}, u32[]{:S(2)}) %collective-permute-start.10) | collective-permute-done | bytes 294944 | tf_op jit(solution)/shard_map/ppermute | solution.py:466
  55.5 0.1 add_plane_mlp.1
  55.7 1.7 %collective-permute-start.17 = (bf16[12,16,384]{2,1,0:T(8,128)(2,1)S(1)}, bf16[12,16,384]{2,1,0:T(8,128)(2,1)S(1)}, u32[]{:S(2)}, u32[]{:S(2)}) collective-permute-start(bf16[12,16,384]{2,1,0:T(8,128)(2,1)S(1)} %get-tuple-element.115), channel_id=1, source_target_pairs={{0,8},{2,10},{4,12},{6,14},{8,0},{10,2},{12,4},{14,6},{16,24},{18,... | collective-permute-start | bytes 442376 | tf_op jit(solution)/shard_map/ppermute | solution.py:438
  57.3 0.2 collective-permute-start.15
  57.6 1.0 collective-permute-done.15.refs_4_
  58.5 0.1 add_core_attn.1
  58.7 1.3 %collective-permute-start.16 = (bf16[13,16,384]{2,1,0:T(8,128)(2,1)S(1)}, bf16[13,16,384]{2,1,0:T(8,128)(2,1)S(1)}, u32[]{:S(2)}, u32[]{:S(2)}) collective-permute-start(bf16[13,16,384]{2,1,0:T(8,128)(2,1)S(1)} %get-tuple-element.122), channel_id=1, source_target_pairs={{0,1},{1,0},{2,3},{3,2},{4,5},{5,4},{6,7},{7,6},{8,9},{9,8},{10,11... | collective-permute-start | bytes 479240 | tf_op jit(solution)/shard_map/ppermute | solution.py:466
  59.9 0.8 collective-permute-start.18
  60.8 1.4 %collective-permute-start.19 = (bf16[13,16,384]{2,1,0:T(8,128)(2,1)S(1)}, bf16[13,16,384]{2,1,0:T(8,128)(2,1)S(1)}, u32[]{:S(2)}, u32[]{:S(2)}) collective-permute-start(bf16[13,16,384]{2,1,0:T(8,128)(2,1)S(1)} %get-tuple-element.127), channel_id=1, source_target_pairs={{0,5},{1,4},{2,7},{3,6},{4,1},{5,0},{6,3},{7,2},{8,13},{9,12},{10,... | collective-permute-start | bytes 479240 | tf_op jit(solution)/shard_map/ppermute | solution.py:466
  62.3 2.6 %collective-permute-start.21 = (bf16[12,16,384]{2,1,0:T(8,128)(2,1)S(1)}, bf16[12,16,384]{2,1,0:T(8,128)(2,1)S(1)}, u32[]{:S(2)}, u32[]{:S(2)}) collective-permute-start(bf16[12,16,384]{2,1,0:T(8,128)(2,1)S(1)} %add_two_mlp.2.left_ref), channel_id=1, source_target_pairs={{0,16},{2,18},{4,20},{6,22},{8,24},{10,26},{12,28},{14,30},{16,0},... | collective-permute-start | bytes 442376 | tf_op jit(solution)/shard_map/ppermute | solution.py:438
  64.9 0.8 collective-permute-done.16.refs_0_
  65.7 2.0 %collective-permute-done.18.refs_1_ = bf16[13,16,384]{2,1,0:T(8,128)(2,1)S(1)} collective-permute-done((bf16[13,16,384]{2,1,0:T(8,128)(2,1)S(1)}, bf16[13,16,384]{2,1,0:T(8,128)(2,1)S(1)}, u32[]{:S(2)}, u32[]{:S(2)}) %collective-permute-start.18) | collective-permute-done | bytes 159776 | tf_op jit(solution)/shard_map/ppermute | solution.py:466
  67.7 1.6 %collective-permute-done.19.refs_2_ = bf16[13,16,384]{2,1,0:T(8,128)(2,1)S(1)} collective-permute-done((bf16[13,16,384]{2,1,0:T(8,128)(2,1)S(1)}, bf16[13,16,384]{2,1,0:T(8,128)(2,1)S(1)}, u32[]{:S(2)}, u32[]{:S(2)}) %collective-permute-start.19) | collective-permute-done | bytes 159776 | tf_op jit(solution)/shard_map/ppermute | solution.py:466
  69.3 0.1 add_plane_attn.1.left_ref
  69.4 0.5 collective-permute-start.20
  69.9 1.7 %collective-permute-done.21.right_ref = bf16[12,16,384]{2,1,0:T(8,128)(2,1)S(1)} collective-permute-done((bf16[12,16,384]{2,1,0:T(8,128)(2,1)S(1)}, bf16[12,16,384]{2,1,0:T(8,128)(2,1)S(1)}, u32[]{:S(2)}, u32[]{:S(2)}) %collective-permute-start.21) | collective-permute-done | bytes 147488 | tf_op jit(solution)/shard_map/ppermute | solution.py:438
  71.7 0.7 collective-permute-start.28
  72.4 4.1 %collective-permute-done.20.right_ref = bf16[13,16,384]{2,1,0:T(8,128)(2,1)S(1)} collective-permute-done((bf16[13,16,384]{2,1,0:T(8,128)(2,1)S(1)}, bf16[13,16,384]{2,1,0:T(8,128)(2,1)S(1)}, u32[]{:S(2)}, u32[]{:S(2)}) %collective-permute-start.20) | collective-permute-done | bytes 159776 | tf_op jit(solution)/shard_map/ppermute | solution.py:438
  76.6 1.9 %collective-permute-start.22 = (bf16[13,16,384]{2,1,0:T(8,128)(2,1)S(1)}, bf16[13,16,384]{2,1,0:T(8,128)(2,1)S(1)}, u32[]{:S(2)}, u32[]{:S(2)}) collective-permute-start(bf16[13,16,384]{2,1,0:T(8,128)(2,1)S(1)} %add_two_attn.1.left_ref), channel_id=1, source_target_pairs={{0,16},{2,18},{4,20},{6,22},{8,24},{10,26},{12,28},{14,30},{16,0},... | collective-permute-start | bytes 479240 | tf_op jit(solution)/shard_map/ppermute | solution.py:438
  78.5 1.5 %collective-permute-done.28.refs_4_ = bf16[12,16,384]{2,1,0:T(8,128)(2,1)S(1)} collective-permute-done((bf16[12,16,384]{2,1,0:T(8,128)(2,1)S(1)}, bf16[12,16,384]{2,1,0:T(8,128)(2,1)S(1)}, u32[]{:S(2)}, u32[]{:S(2)}) %collective-permute-start.28) | collective-permute-done | bytes 147488 | tf_op jit(solution)/shard_map/ppermute | solution.py:438
  79.9 1.4 %collective-permute-start.30 = (bf16[12,16,384]{2,1,0:T(8,128)(2,1)S(1)}, bf16[12,16,384]{2,1,0:T(8,128)(2,1)S(1)}, u32[]{:S(2)}, u32[]{:S(2)}) collective-permute-start(bf16[12,16,384]{2,1,0:T(8,128)(2,1)S(1)} %collective-permute-done.28.refs_4_), channel_id=1, source_target_pairs={{0,4},{2,6},{4,0},{6,2},{8,12},{10,14},{12,8},{14,10},{16,20},{18,... | collective-permute-start | bytes 442376 | tf_op jit(solution)/shard_map/ppermute | solution.py:438
  81.4 0.5 collective-permute-start.29
  81.9 1.7 %collective-permute-done.26.refs_2_ = bf16[12,16,384]{2,1,0:T(8,128)(2,1)S(1)} collective-permute-done((bf16[12,16,384]{2,1,0:T(8,128)(2,1)S(1)}, bf16[12,16,384]{2,1,0:T(8,128)(2,1)S(1)}, u32[]{:S(2)}, u32[]{:S(2)}) %collective-permute-start.26) | collective-permute-done | bytes 147488 | tf_op jit(solution)/shard_map/ppermute | solution.py:438
  83.6 1.6 %collective-permute-done.30.refs_6_ = bf16[12,16,384]{2,1,0:T(8,128)(2,1)S(1)} collective-permute-done((bf16[12,16,384]{2,1,0:T(8,128)(2,1)S(1)}, bf16[12,16,384]{2,1,0:T(8,128)(2,1)S(1)}, u32[]{:S(2)}, u32[]{:S(2)}) %collective-permute-start.30) | collective-permute-done | bytes 147488 | tf_op jit(solution)/shard_map/ppermute | solution.py:438
  85.2 0.1 collective-permute-done.22.right_ref
  85.2 0.7 add_last.1
  85.9 1.7 %collective-permute-start.24 = (bf16[12,16,384]{2,1,0:T(8,128)(2,1)S(1)}, bf16[12,16,384]{2,1,0:T(8,128)(2,1)S(1)}, u32[]{:S(2)}, u32[]{:S(2)}) collective-permute-start(bf16[12,16,384]{2,1,0:T(8,128)(2,1)S(1)} %get-tuple-element.130.refs_0_), channel_id=1, source_target_pairs={{0,4},{2,6},{4,0},{6,2},{8,12},{10,14},{12,8},{14,10},{16,20},{18,... | collective-permute-start | bytes 442376 | tf_op jit(solution)/shard_map/ppermute | solution.py:438
  87.7 0.2 collective-permute-start.23
  87.9 4.4 %adam_mlp.1 = (f32[192,3072]{1,0:T(8,128)}, f32[192,3072]{1,0:T(8,128)}, f32[192,3072]{1,0:T(8,128)}) custom-call(bf16[12,16,384]{2,1,0:T(8,128)(2,1)S(1)} %add_two_mlp.3.refs_0_, bf16[12,16,384]{2,1,0:T(8,128)(2,1)S(1)} %collective-permute-done.25.refs_1_, bf16[12,16,384]{2,1,0:T(8,128)(2,1)S(1)} %collective-permute-done.26.refs_2_, ...), custom_call_target="tpu_custom_call" | custom-call | flops 9437184 | bytes 14155776 | tf_op jit(solution)/shard_map/adam_mlp/pallas_call | solution.py:531
  92.3 0.3 collective-permute-start.32
  92.6 1.1 %collective-permute-done.32.refs_3_ = bf16[12,16,384]{2,1,0:T(8,128)(2,1)S(1)} collective-permute-done((bf16[12,16,384]{2,1,0:T(8,128)(2,1)S(1)}, bf16[12,16,384]{2,1,0:T(8,128)(2,1)S(1)}, u32[]{:S(2)}, u32[]{:S(2)}) %collective-permute-start.32) | collective-permute-done | bytes 147488 | tf_op jit(solution)/shard_map/ppermute | solution.py:434
  93.6 2.3 %adam_attn.1 = (f32[192,1536]{1,0:T(8,128)}, f32[192,1536]{1,0:T(8,128)}, f32[192,1536]{1,0:T(8,128)}) custom-call(bf16[12,16,384]{2,1,0:T(8,128)(2,1)S(1)} %get-tuple-element.130.refs_0_, bf16[12,16,384]{2,1,0:T(8,128)(2,1)S(1)} %collective-permute-done.23.refs_1_, bf16[12,16,384]{2,1,0:T(8,128)(2,1)S(1)} %collective-permute-done.24.refs_2_, ...), custom_call_target="tpu_custom_call" | custom-call | flops 4718592 | bytes 7077888 | tf_op jit(solution)/shard_map/adam_attn/pallas_call | solution.py:531
  (39 shorter events, 0.3 us)
Async XLA Ops:
  0.6 5.0 %copy-start.1 = (f32[192,1536]{1,0:T(8,128)S(1)}, f32[192,1536]{1,0:T(8,128)}, u32[]{:S(2)}) copy-start(f32[192,1536]{1,0:T(8,128)} %refs_3_.1) | copy-start | bytes 3538948
  2.7 11.4 %collective-permute-start = (bf16[208,768]{1,0:T(8,128)(2,1)S(1)}, bf16[208,768]{1,0:T(8,128)(2,1)S(1)}, u32[]{:S(2)}, u32[]{:S(2)}) collective-permute-start(bf16[208,768]{1,0:T(8,128)(2,1)S(1)} %pad_maximum_fusion.refs_3_), channel_id=1, source_target_pairs={{0,1},{1,0},{2,3},{3,2},{4,5},{5,4},{6,7},{7,6},{8,9},{9,8},{10,11... | collective-permute-start | bytes 958472 | tf_op jit(solution)/shard_map/ppermute | solution.py:551
  5.7 1.7 %copy-start = (f32[192,3072]{1,0:T(8,128)S(1)}, f32[192,3072]{1,0:T(8,128)}, u32[]{:S(2)}) copy-start(f32[192,3072]{1,0:T(8,128)} %refs_0_.4) | copy-start | bytes 7077892
  7.3 8.3 %copy-start.2 = (bf16[512,384]{1,0:T(8,128)(2,1)S(1)}, bf16[512,384]{1,0:T(8,128)(2,1)}, u32[]{:S(2)}) copy-start(bf16[512,384]{1,0:T(8,128)(2,1)} %refs_0_.5) | copy-start | bytes 1179652
  7.3 8.3 %copy-start.6 = (s32[512]{0:T(512)S(1)}, s32[512]{0:T(512)}, u32[]{:S(2)}) copy-start(s32[512]{0:T(512)} %param.13) | copy-start | bytes 6148
  7.6 18.3 %collective-permute-start.2 = (bf16[192,1536]{1,0:T(8,128)(2,1)S(1)}, bf16[192,1536]{1,0:T(8,128)(2,1)S(1)}, u32[]{:S(2)}, u32[]{:S(2)}) collective-permute-start(bf16[192,1536]{1,0:T(8,128)(2,1)S(1)} %get-tuple-element.86), channel_id=1, source_target_pairs={{0,1},{1,0},{2,3},{3,2},{4,5},{5,4},{6,7},{7,6},{8,9},{9,8},{10,11... | collective-permute-start | bytes 1769480 | tf_op jit(solution)/shard_map/ppermute | solution.py:551
  14.0 1.6 %collective-permute-start.1 = (bf16[208,768]{1,0:T(8,128)(2,1)S(1)}, bf16[208,768]{1,0:T(8,128)(2,1)S(1)}, u32[]{:S(2)}, u32[]{:S(2)}) collective-permute-start(bf16[208,768]{1,0:T(8,128)(2,1)S(1)} %collective-permute-done.refs_4_), channel_id=1, source_target_pairs={{0,2},{2,0},{4,6},{6,4},{8,10},{10,8},{12,14},{14,12},{16,18},{18,... | collective-permute-start | bytes 958472 | tf_op jit(solution)/shard_map/ppermute | solution.py:434
  15.7 12.2 %copy-start.7 = (bf16[512,384]{1,0:T(8,128)(2,1)S(1)}, bf16[512,384]{1,0:T(8,128)(2,1)}, u32[]{:S(2)}) copy-start(bf16[512,384]{1,0:T(8,128)(2,1)} %refs_1_.2) | copy-start | bytes 1179652
  25.8 2.0 %collective-permute-start.3 = (bf16[192,1536]{1,0:T(8,128)(2,1)S(1)}, bf16[192,1536]{1,0:T(8,128)(2,1)S(1)}, u32[]{:S(2)}, u32[]{:S(2)}) collective-permute-start(bf16[192,1536]{1,0:T(8,128)(2,1)S(1)} %collective-permute-done.2.refs_6_), channel_id=1, source_target_pairs={{0,2},{2,0},{4,6},{6,4},{8,10},{10,8},{12,14},{14,12},{16,18},{18,... | collective-permute-start | bytes 1769480 | tf_op jit(solution)/shard_map/ppermute | solution.py:434
  34.6 3.7 %collective-permute-start.4 = (bf16[24,16,384]{2,1,0:T(8,128)(2,1)S(1)}, bf16[24,16,384]{2,1,0:T(8,128)(2,1)S(1)}, u32[]{:S(2)}, u32[]{:S(2)}) collective-permute-start(bf16[24,16,384]{2,1,0:T(8,128)(2,1)S(1)} %get-tuple-element.101), channel_id=1, source_target_pairs={{0,2},{2,0},{4,6},{6,4},{8,10},{10,8},{12,14},{14,12},{16,18},{18,... | collective-permute-start | bytes 884744 | tf_op jit(solution)/shard_map/ppermute | solution.py:434
  34.8 3.5 %collective-permute-start.5 = (bf16[24,16,384]{2,1,0:T(8,128)(2,1)S(1)}, bf16[24,16,384]{2,1,0:T(8,128)(2,1)S(1)}, u32[]{:S(2)}, u32[]{:S(2)}) collective-permute-start(bf16[24,16,384]{2,1,0:T(8,128)(2,1)S(1)} %get-tuple-element.103), channel_id=1, source_target_pairs={{0,2},{2,0},{4,6},{6,4},{8,10},{10,8},{12,14},{14,12},{16,18},{18,... | collective-permute-start | bytes 884744 | tf_op jit(solution)/shard_map/ppermute | solution.py:434
  35.2 3.2 %collective-permute-start.6 = (bf16[24,16,384]{2,1,0:T(8,128)(2,1)S(1)}, bf16[24,16,384]{2,1,0:T(8,128)(2,1)S(1)}, u32[]{:S(2)}, u32[]{:S(2)}) collective-permute-start(bf16[24,16,384]{2,1,0:T(8,128)(2,1)S(1)} %get-tuple-element.104), channel_id=1, source_target_pairs={{0,2},{2,0},{4,6},{6,4},{8,10},{10,8},{12,14},{14,12},{16,18},{18,... | collective-permute-start | bytes 884744 | tf_op jit(solution)/shard_map/ppermute | solution.py:434
  35.3 3.1 %collective-permute-start.7 = (bf16[24,16,384]{2,1,0:T(8,128)(2,1)S(1)}, bf16[24,16,384]{2,1,0:T(8,128)(2,1)S(1)}, u32[]{:S(2)}, u32[]{:S(2)}) collective-permute-start(bf16[24,16,384]{2,1,0:T(8,128)(2,1)S(1)} %get-tuple-element.105), channel_id=1, source_target_pairs={{0,2},{2,0},{4,6},{6,4},{8,10},{10,8},{12,14},{14,12},{16,18},{18,... | collective-permute-start | bytes 884744 | tf_op jit(solution)/shard_map/ppermute | solution.py:434
  38.6 12.4 %collective-permute-start.9 = (bf16[24,16,384]{2,1,0:T(8,128)(2,1)S(1)}, bf16[24,16,384]{2,1,0:T(8,128)(2,1)S(1)}, u32[]{:S(2)}, u32[]{:S(2)}) collective-permute-start(bf16[24,16,384]{2,1,0:T(8,128)(2,1)S(1)} %get-tuple-element.107), channel_id=1, source_target_pairs={{0,1},{1,0},{2,3},{3,2},{4,5},{5,4},{6,7},{7,6},{8,9},{9,8},{10,11... | collective-permute-start | bytes 884744 | tf_op jit(solution)/shard_map/ppermute | solution.py:466
  40.4 15.1 %collective-permute-start.10 = (bf16[24,16,384]{2,1,0:T(8,128)(2,1)S(1)}, bf16[24,16,384]{2,1,0:T(8,128)(2,1)S(1)}, u32[]{:S(2)}, u32[]{:S(2)}) collective-permute-start(bf16[24,16,384]{2,1,0:T(8,128)(2,1)S(1)} %get-tuple-element.108), channel_id=1, source_target_pairs={{0,4},{1,5},{2,6},{3,7},{4,0},{5,1},{6,2},{7,3},{8,12},{9,13},{10,... | collective-permute-start | bytes 884744 | tf_op jit(solution)/shard_map/ppermute | solution.py:466
  42.0 13.6 %collective-permute-start.11 = (bf16[24,16,384]{2,1,0:T(8,128)(2,1)S(1)}, bf16[24,16,384]{2,1,0:T(8,128)(2,1)S(1)}, u32[]{:S(2)}, u32[]{:S(2)}) collective-permute-start(bf16[24,16,384]{2,1,0:T(8,128)(2,1)S(1)} %get-tuple-element.109), channel_id=1, source_target_pairs={{0,5},{1,4},{2,7},{3,6},{4,1},{5,0},{6,3},{7,2},{8,13},{9,12},{10,... | collective-permute-start | bytes 884744 | tf_op jit(solution)/shard_map/ppermute | solution.py:466
  50.6 6.8 %collective-permute-start.8 = (bf16[12,16,384]{2,1,0:T(8,128)(2,1)S(1)}, bf16[12,16,384]{2,1,0:T(8,128)(2,1)S(1)}, u32[]{:S(2)}, u32[]{:S(2)}) collective-permute-start(bf16[12,16,384]{2,1,0:T(8,128)(2,1)S(1)} %get-tuple-element.114), channel_id=1, source_target_pairs={{0,2},{2,0},{4,6},{6,4},{8,10},{10,8},{12,14},{14,12},{16,18},{18,... | collective-permute-start | bytes 442376 | tf_op jit(solution)/shard_map/ppermute | solution.py:434
  50.6 7.9 %collective-permute-start.12 = (bf16[12,16,384]{2,1,0:T(8,128)(2,1)S(1)}, bf16[12,16,384]{2,1,0:T(8,128)(2,1)S(1)}, u32[]{:S(2)}, u32[]{:S(2)}) collective-permute-start(bf16[12,16,384]{2,1,0:T(8,128)(2,1)S(1)} %get-tuple-element.117), channel_id=1, source_target_pairs={{0,2},{2,0},{4,6},{6,4},{8,10},{10,8},{12,14},{14,12},{16,18},{18,... | collective-permute-start | bytes 442376 | tf_op jit(solution)/shard_map/ppermute | solution.py:434
  51.1 7.4 %collective-permute-start.13 = (bf16[12,16,384]{2,1,0:T(8,128)(2,1)S(1)}, bf16[12,16,384]{2,1,0:T(8,128)(2,1)S(1)}, u32[]{:S(2)}, u32[]{:S(2)}) collective-permute-start(bf16[12,16,384]{2,1,0:T(8,128)(2,1)S(1)} %get-tuple-element.118), channel_id=1, source_target_pairs={{0,2},{2,0},{4,6},{6,4},{8,10},{10,8},{12,14},{14,12},{16,18},{18,... | collective-permute-start | bytes 442376 | tf_op jit(solution)/shard_map/ppermute | solution.py:434
  55.5 3.0 %collective-permute-start.14 = (bf16[12,16,384]{2,1,0:T(8,128)(2,1)S(1)}, bf16[12,16,384]{2,1,0:T(8,128)(2,1)S(1)}, u32[]{:S(2)}, u32[]{:S(2)}) collective-permute-start(bf16[12,16,384]{2,1,0:T(8,128)(2,1)S(1)} %get-tuple-element.119), channel_id=1, source_target_pairs={{0,2},{2,0},{4,6},{6,4},{8,10},{10,8},{12,14},{14,12},{16,18},{18,... | collective-permute-start | bytes 442376 | tf_op jit(solution)/shard_map/ppermute | solution.py:434
  55.7 6.6 %collective-permute-start.17 = (bf16[12,16,384]{2,1,0:T(8,128)(2,1)S(1)}, bf16[12,16,384]{2,1,0:T(8,128)(2,1)S(1)}, u32[]{:S(2)}, u32[]{:S(2)}) collective-permute-start(bf16[12,16,384]{2,1,0:T(8,128)(2,1)S(1)} %get-tuple-element.115), channel_id=1, source_target_pairs={{0,8},{2,10},{4,12},{6,14},{8,0},{10,2},{12,4},{14,6},{16,24},{18,... | collective-permute-start | bytes 442376 | tf_op jit(solution)/shard_map/ppermute | solution.py:438
  57.3 1.2 %collective-permute-start.15 = (bf16[1,16,384]{2,1,0:T(8,128)(2,1)S(1)}, bf16[1,16,384]{2,1,0:T(8,128)(2,1)S(1)}, u32[]{:S(2)}, u32[]{:S(2)}) collective-permute-start(bf16[1,16,384]{2,1,0:T(8,128)(2,1)S(1)} %get-tuple-element.120), channel_id=1, source_target_pairs={{0,2},{2,0},{4,6},{6,4},{8,10},{10,8},{12,14},{14,12},{16,18},{18,... | collective-permute-start | bytes 36872 | tf_op jit(solution)/shard_map/ppermute | solution.py:434
  58.7 7.0 %collective-permute-start.16 = (bf16[13,16,384]{2,1,0:T(8,128)(2,1)S(1)}, bf16[13,16,384]{2,1,0:T(8,128)(2,1)S(1)}, u32[]{:S(2)}, u32[]{:S(2)}) collective-permute-start(bf16[13,16,384]{2,1,0:T(8,128)(2,1)S(1)} %get-tuple-element.122), channel_id=1, source_target_pairs={{0,1},{1,0},{2,3},{3,2},{4,5},{5,4},{6,7},{7,6},{8,9},{9,8},{10,11... | collective-permute-start | bytes 479240 | tf_op jit(solution)/shard_map/ppermute | solution.py:466
  59.9 7.8 %collective-permute-start.18 = (bf16[13,16,384]{2,1,0:T(8,128)(2,1)S(1)}, bf16[13,16,384]{2,1,0:T(8,128)(2,1)S(1)}, u32[]{:S(2)}, u32[]{:S(2)}) collective-permute-start(bf16[13,16,384]{2,1,0:T(8,128)(2,1)S(1)} %get-tuple-element.126), channel_id=1, source_target_pairs={{0,4},{1,5},{2,6},{3,7},{4,0},{5,1},{6,2},{7,3},{8,12},{9,13},{10,... | collective-permute-start | bytes 479240 | tf_op jit(solution)/shard_map/ppermute | solution.py:466
  60.8 8.6 %collective-permute-start.19 = (bf16[13,16,384]{2,1,0:T(8,128)(2,1)S(1)}, bf16[13,16,384]{2,1,0:T(8,128)(2,1)S(1)}, u32[]{:S(2)}, u32[]{:S(2)}) collective-permute-start(bf16[13,16,384]{2,1,0:T(8,128)(2,1)S(1)} %get-tuple-element.127), channel_id=1, source_target_pairs={{0,5},{1,4},{2,7},{3,6},{4,1},{5,0},{6,3},{7,2},{8,13},{9,12},{10,... | collective-permute-start | bytes 479240 | tf_op jit(solution)/shard_map/ppermute | solution.py:466
  62.2 23.0 %copy-start.3 = (f32[2304]{0:T(1024)S(1)}, f32[2304]{0:T(1024)}, u32[]{:S(2)}) copy-start(f32[2304]{0:T(1024)} %w_ref.1) | copy-start | bytes 27652
  62.2 23.0 %copy-start.4 = (f32[2304]{0:T(1024)S(1)}, f32[2304]{0:T(1024)}, u32[]{:S(2)}) copy-start(f32[2304]{0:T(1024)} %m_ref.1) | copy-start | bytes 27652
  62.2 23.0 %copy-start.5 = (f32[2304]{0:T(1024)S(1)}, f32[2304]{0:T(1024)}, u32[]{:S(2)}) copy-start(f32[2304]{0:T(1024)} %v_ref.1) | copy-start | bytes 27652
  62.3 9.4 %collective-permute-start.21 = (bf16[12,16,384]{2,1,0:T(8,128)(2,1)S(1)}, bf16[12,16,384]{2,1,0:T(8,128)(2,1)S(1)}, u32[]{:S(2)}, u32[]{:S(2)}) collective-permute-start(bf16[12,16,384]{2,1,0:T(8,128)(2,1)S(1)} %add_two_mlp.2.left_ref), channel_id=1, source_target_pairs={{0,16},{2,18},{4,20},{6,22},{8,24},{10,26},{12,28},{14,30},{16,0},... | collective-permute-start | bytes 442376 | tf_op jit(solution)/shard_map/ppermute | solution.py:438
  69.4 7.1 %collective-permute-start.20 = (bf16[13,16,384]{2,1,0:T(8,128)(2,1)S(1)}, bf16[13,16,384]{2,1,0:T(8,128)(2,1)S(1)}, u32[]{:S(2)}, u32[]{:S(2)}) collective-permute-start(bf16[13,16,384]{2,1,0:T(8,128)(2,1)S(1)} %add_plane_attn.1.left_ref), channel_id=1, source_target_pairs={{0,8},{2,10},{4,12},{6,14},{8,0},{10,2},{12,4},{14,6},{16,24},{18,... | collective-permute-start | bytes 479240 | tf_op jit(solution)/shard_map/ppermute | solution.py:438
  71.7 8.2 %collective-permute-start.28 = (bf16[12,16,384]{2,1,0:T(8,128)(2,1)S(1)}, bf16[12,16,384]{2,1,0:T(8,128)(2,1)S(1)}, u32[]{:S(2)}, u32[]{:S(2)}) collective-permute-start(bf16[12,16,384]{2,1,0:T(8,128)(2,1)S(1)} %add_two_mlp.3.refs_0_), channel_id=1, source_target_pairs={{0,8},{2,10},{4,12},{6,14},{8,0},{10,2},{12,4},{14,6},{16,24},{18,... | collective-permute-start | bytes 442376 | tf_op jit(solution)/shard_map/ppermute | solution.py:438
  76.6 8.7 %collective-permute-start.22 = (bf16[13,16,384]{2,1,0:T(8,128)(2,1)S(1)}, bf16[13,16,384]{2,1,0:T(8,128)(2,1)S(1)}, u32[]{:S(2)}, u32[]{:S(2)}) collective-permute-start(bf16[13,16,384]{2,1,0:T(8,128)(2,1)S(1)} %add_two_attn.1.left_ref), channel_id=1, source_target_pairs={{0,16},{2,18},{4,20},{6,22},{8,24},{10,26},{12,28},{14,30},{16,0},... | collective-permute-start | bytes 479240 | tf_op jit(solution)/shard_map/ppermute | solution.py:438
  78.5 5.2 %collective-permute-start.26 = (bf16[12,16,384]{2,1,0:T(8,128)(2,1)S(1)}, bf16[12,16,384]{2,1,0:T(8,128)(2,1)S(1)}, u32[]{:S(2)}, u32[]{:S(2)}) collective-permute-start(bf16[12,16,384]{2,1,0:T(8,128)(2,1)S(1)} %add_two_mlp.3.refs_0_), channel_id=1, source_target_pairs={{0,4},{2,6},{4,0},{6,2},{8,12},{10,14},{12,8},{14,10},{16,20},{18,... | collective-permute-start | bytes 442376 | tf_op jit(solution)/shard_map/ppermute | solution.py:438
  79.9 5.3 %collective-permute-start.30 = (bf16[12,16,384]{2,1,0:T(8,128)(2,1)S(1)}, bf16[12,16,384]{2,1,0:T(8,128)(2,1)S(1)}, u32[]{:S(2)}, u32[]{:S(2)}) collective-permute-start(bf16[12,16,384]{2,1,0:T(8,128)(2,1)S(1)} %collective-permute-done.28.refs_4_), channel_id=1, source_target_pairs={{0,4},{2,6},{4,0},{6,2},{8,12},{10,14},{12,8},{14,10},{16,20},{18,... | collective-permute-start | bytes 442376 | tf_op jit(solution)/shard_map/ppermute | solution.py:438
  81.4 6.3 %collective-permute-start.25 = (bf16[12,16,384]{2,1,0:T(8,128)(2,1)S(1)}, bf16[12,16,384]{2,1,0:T(8,128)(2,1)S(1)}, u32[]{:S(2)}, u32[]{:S(2)}) collective-permute-start(bf16[12,16,384]{2,1,0:T(8,128)(2,1)S(1)} %add_two_mlp.3.refs_0_), channel_id=1, source_target_pairs={{0,2},{2,0},{4,6},{6,4},{8,10},{10,8},{12,14},{14,12},{16,18},{18,... | collective-permute-start | bytes 442376 | tf_op jit(solution)/shard_map/ppermute | solution.py:434
  81.4 6.5 %collective-permute-start.29 = (bf16[12,16,384]{2,1,0:T(8,128)(2,1)S(1)}, bf16[12,16,384]{2,1,0:T(8,128)(2,1)S(1)}, u32[]{:S(2)}, u32[]{:S(2)}) collective-permute-start(bf16[12,16,384]{2,1,0:T(8,128)(2,1)S(1)} %collective-permute-done.28.refs_4_), channel_id=1, source_target_pairs={{0,2},{2,0},{4,6},{6,4},{8,10},{10,8},{12,14},{14,12},{16,18},{18,... | collective-permute-start | bytes 442376 | tf_op jit(solution)/shard_map/ppermute | solution.py:434
  83.6 4.3 %collective-permute-start.27 = (bf16[12,16,384]{2,1,0:T(8,128)(2,1)S(1)}, bf16[12,16,384]{2,1,0:T(8,128)(2,1)S(1)}, u32[]{:S(2)}, u32[]{:S(2)}) collective-permute-start(bf16[12,16,384]{2,1,0:T(8,128)(2,1)S(1)} %collective-permute-done.26.refs_2_), channel_id=1, source_target_pairs={{0,2},{2,0},{4,6},{6,4},{8,10},{10,8},{12,14},{14,12},{16,18},{18,... | collective-permute-start | bytes 442376 | tf_op jit(solution)/shard_map/ppermute | solution.py:434
  85.2 2.7 %collective-permute-start.31 = (bf16[12,16,384]{2,1,0:T(8,128)(2,1)S(1)}, bf16[12,16,384]{2,1,0:T(8,128)(2,1)S(1)}, u32[]{:S(2)}, u32[]{:S(2)}) collective-permute-start(bf16[12,16,384]{2,1,0:T(8,128)(2,1)S(1)} %collective-permute-done.30.refs_6_), channel_id=1, source_target_pairs={{0,2},{2,0},{4,6},{6,4},{8,10},{10,8},{12,14},{14,12},{16,18},{18,... | collective-permute-start | bytes 442376 | tf_op jit(solution)/shard_map/ppermute | solution.py:434
  85.9 6.3 %collective-permute-start.24 = (bf16[12,16,384]{2,1,0:T(8,128)(2,1)S(1)}, bf16[12,16,384]{2,1,0:T(8,128)(2,1)S(1)}, u32[]{:S(2)}, u32[]{:S(2)}) collective-permute-start(bf16[12,16,384]{2,1,0:T(8,128)(2,1)S(1)} %get-tuple-element.130.refs_0_), channel_id=1, source_target_pairs={{0,4},{2,6},{4,0},{6,2},{8,12},{10,14},{12,8},{14,10},{16,20},{18,... | collective-permute-start | bytes 442376 | tf_op jit(solution)/shard_map/ppermute | solution.py:438
  87.7 4.9 %collective-permute-start.23 = (bf16[12,16,384]{2,1,0:T(8,128)(2,1)S(1)}, bf16[12,16,384]{2,1,0:T(8,128)(2,1)S(1)}, u32[]{:S(2)}, u32[]{:S(2)}) collective-permute-start(bf16[12,16,384]{2,1,0:T(8,128)(2,1)S(1)} %get-tuple-element.130.refs_0_), channel_id=1, source_target_pairs={{0,2},{2,0},{4,6},{6,4},{8,10},{10,8},{12,14},{14,12},{16,18},{18,... | collective-permute-start | bytes 442376 | tf_op jit(solution)/shard_map/ppermute | solution.py:434
  92.3 1.4 %collective-permute-start.32 = (bf16[12,16,384]{2,1,0:T(8,128)(2,1)S(1)}, bf16[12,16,384]{2,1,0:T(8,128)(2,1)S(1)}, u32[]{:S(2)}, u32[]{:S(2)}) collective-permute-start(bf16[12,16,384]{2,1,0:T(8,128)(2,1)S(1)} %collective-permute-done.24.refs_2_), channel_id=1, source_target_pairs={{0,2},{2,0},{4,6},{6,4},{8,10},{10,8},{12,14},{14,12},{16,18},{18,... | collective-permute-start | bytes 442376 | tf_op jit(solution)/shard_map/ppermute | solution.py:434

commit v3 on v2

--- a/solution.py
+++ b/solution.py
@@ -32,7 +32,8 @@
 MIB = 1024 * 1024
 HOLD = False
 ROWS = 96
-MLP_CUT = (1536,)
+WIDE = FF // 2
+EARLY = 384
 
 vmem = pl.BlockSpec(memory_space=pltpu.VMEM)
 
@@ -121,18 +122,24 @@
     return dp & 1, (dp >> 1) & 1, dp >> 2, op
 
 
-def assemble(plan, own_ref, direct, cross, full_ref):
+def assemble(plan, own_halves, messages, full_ref):
     core, _, _, op = position()
-    width = full_ref.shape[3]
-    full_ref[op, 0] = own_ref[:, :width]
-    full_ref[op, 1] = own_ref[:, width:]
-    for half, messages in ((core, direct), (1 - core, cross)):
-        lane = 0
-        for pieces in messages:
-            cols = slice(lane, lane + pieces[0].shape[1])
-            lane += pieces[0].shape[1]
+    for half, value in enumerate(own_halves):
+        full_ref[op, half] = value
+    for cols, direct, cross in messages:
+        for half, pieces in ((core, direct), (1 - core, cross)):
             for m in range(1, plan.n_opt):
-                full_ref[op ^ m, half, :, cols] = pieces[m - 1][: plan.own, :]
+                full_ref[op ^ m, half, :, cols] = pieces[m - 1][...]
+
+
+def assemble_quarters(plan, own_ref, pieces, full_ref):
+    core, ybit, _, op = position()
+    for half in range(2):
+        full_ref[op, half] = own_ref[:, half * 2 * D : (half + 1) * 2 * D]
+    for rel, messages in pieces.items():
+        cols = pl.ds(pl.multiple_of((ybit ^ (rel // 2)) * D, D), D)
+        for m in range(1, plan.n_opt):
+            full_ref[op ^ m, core ^ (rel % 2), :, cols] = messages[m - 1][: plan.own, :]
 
 
 def store_chunks(plan, stream, ref, base, value, mat):
@@ -147,7 +154,7 @@
 
 def split_sends(stream, whole_ref, refs):
     for number, ref in enumerate(refs):
-        ref[...] = whole_ref[number * stream.piece : (number + 1) * stream.piece]
+        ref[: stream.piece] = whole_ref[number * stream.piece : (number + 1) * stream.piece]
 
 
 def column_of(row):
@@ -183,38 +190,41 @@
         bup_ref[blk] = jnp.concatenate([row_of(8 + 2 * blk), row_of(9 + 2 * blk)], axis=1)
 
 
-def cast_weights(plan, attn_ref, mlp_ref, attn_low, mlp_low, *halves):
-    core = position()[0]
+def cast_weights(plan, attn_ref, mlp_ref, attn_low, mlp_low, early_ref, late_ref):
+    core, ybit = position()[:2]
     attn_low[...] = attn_ref[...].astype(bf16)
     mlp_low[...] = mlp_ref[...].astype(bf16)
-    lane = 0
-    for ref in halves:
-        start = pl.multiple_of(core * FF + lane, 128)
-        ref[...] = mlp_low[:, pl.ds(start, ref.shape[1])]
-        lane += ref.shape[1]
-
-
-def attn_forward(plan, length, *refs):
-    n = plan.n_opt - 1
-    tok_ref, seg_ref, own_ref, sent_ref = refs[:4]
-    direct, cross = refs[4 : 4 + n], refs[4 + n : 4 + 2 * n]
-    full_ref, qkv_ref, mixed_ref, lse_ref, resid_ref, vec_ref, bup_ref, bias_ref, piece_ref = refs[4 + 2 * n :]
-    assemble(plan, own_ref, [direct], [cross], full_ref)
-    spread_vec(plan, length, sent_ref, direct, piece_ref, vec_ref, bup_ref)
-    hidden = tok_ref[...].astype(f32)
-    normed, _ = ln_parts(hidden)
-    first_in = (normed * vec_ref[0:1, :] + vec_ref[1:2, :]).astype(bf16)
-    for number, row in ((0, 2), (1, None), (2, 3)):
-        lane = (number % 2) * D
-        weight = full_ref[:, number // 2, :, lane : lane + D].reshape(D, D)
-        part = mm(first_in, weight)
-        if row is not None:
-            part = part + vec_ref[row : row + 1, :]
-        qkv_ref[number] = part.astype(bf16).T
-    fill_bias(seg_ref, bias_ref)
-
-    def one_head(head, carry):
-        rows = pl.ds(pl.multiple_of(head * HEAD_DIM, HEAD_DIM), HEAD_DIM)
+    far = pl.multiple_of(core * FF + (ybit ^ 1) * WIDE, 128)
+    near = pl.multiple_of(core * FF + ybit * WIDE, 128)
+    early_ref[:, :WIDE] = mlp_low[:, pl.ds(far, WIDE)]
+    early_ref[:, WIDE:] = mlp_low[:, pl.ds(near, EARLY)]
+    late_ref[...] = mlp_low[:, pl.ds(near + EARLY, WIDE - EARLY)]
+
+
+def first_message(plan, w_ref, vec_ref, send_ref, part_ref, low_ref, sems):
+    core, ybit = position()[:2]
+    start = pl.multiple_of((2 * core + ybit) * D, D)
+    copies = [
+        pltpu.make_async_copy(w_ref.at[:, pl.ds(start, D)], part_ref, sems.at[0]),
+        pltpu.make_async_copy(vec_ref, low_ref, sems.at[1]),
+    ]
+    for copy in copies:
+        copy.start()
+    copies[1].wait()
+    if len(low_ref.shape) == 1:
+        rows = low_ref.shape[0] // D
+        pieces = [low_ref[k * D : (k + 1) * D].reshape(1, D) for k in range(rows)]
+        pieces.append(jnp.zeros((16 - rows, D), f32))
+        send_ref[plan.own :, :] = jnp.concatenate(pieces, axis=0).astype(bf16)
+    else:
+        send_ref[plan.own :, :] = low_ref[...].astype(bf16)
+    copies[0].wait()
+    send_ref[: plan.own, :] = part_ref[...].astype(bf16)
+
+
+def forward_heads(first, last, qkv_ref, bias_ref, mixed_ref, lse_ref):
+    for head in range(first, last):
+        rows = slice(head * HEAD_DIM, (head + 1) * HEAD_DIM)
         for blk in range(TOK // QBLK):
             cols = slice(blk * QBLK, (blk + 1) * QBLK)
             keys = (blk + 1) * QBLK
@@ -225,61 +235,84 @@
             total = jnp.sum(e, axis=0, keepdims=True)
             probs = (e * (1.0 / total)).astype(bf16)
             mixed_ref[rows, cols] = mm(qkv_ref[2, rows, :keys], probs).astype(bf16)
-            lse_ref[pl.ds(head, 1), :, cols] = (top + jnp.log(total)).reshape(1, 1, QBLK)
-        return carry
-
-    lax.fori_loop(0, HEADS, one_head, 0, unroll=True)
+            lse_ref[head, :, cols] = top + jnp.log(total)
+
+
+def attn_enter(plan, length, heads, *refs):
+    n = plan.n_opt - 1
+    tok_ref, seg_ref, own_ref, sent_ref = refs[:4]
+    pieces = {rel: refs[4 + n * rel : 4 + n * (rel + 1)] for rel in range(4)}
+    full_ref, qkv_ref, mixed_ref, lse_ref, bias_ref, vec_ref, bup_ref, piece_ref = refs[4 + 4 * n :]
+    assemble_quarters(plan, own_ref, pieces, full_ref)
+    spread_vec(plan, length, sent_ref, pieces[0], piece_ref, vec_ref, bup_ref)
+    normed, _ = ln_parts(tok_ref[...].astype(f32))
+    first_in = (normed * vec_ref[0:1, :] + vec_ref[1:2, :]).astype(bf16)
+    for number, row in ((0, 2), (1, None), (2, 3)):
+        lane = (number % 2) * D
+        weight = full_ref[:, number // 2, :, lane : lane + D].reshape(D, D)
+        part = mm(first_in, weight)
+        if row is not None:
+            part = part + vec_ref[row : row + 1, :]
+        qkv_ref[number] = part.astype(bf16).T
+    fill_bias(seg_ref, bias_ref)
+    forward_heads(0, heads, qkv_ref, bias_ref, mixed_ref, lse_ref)
+
+
+def attn_leave(heads, tok_ref, full_ref, qkv_ref, mixed_in, lse_in, bias_ref, vec_ref, mixed_ref, lse_ref, resid_ref):
+    mixed_ref[: heads * HEAD_DIM] = mixed_in[...]
+    lse_ref[:heads] = lse_in[...]
+    forward_heads(heads, HEADS, qkv_ref, bias_ref, mixed_ref, lse_ref)
     out_weight = full_ref[:, 1, :, D:].reshape(D, D)
-    resid_ref[...] = hidden + (mm_tn(mixed_ref[...], out_weight) + vec_ref[4:5, :])
-
-
-def mlp_step(plan, cuts, *refs):
+    resid_ref[...] = tok_ref[...].astype(f32) + (mm_tn(mixed_ref[...], out_weight) + vec_ref[4:5, :])
+
+
+def mlp_block(plan, rel, *refs):
     n = plan.n_opt - 1
     stream = plan.mlp
     resid_ref, cot_ref, seg_ref, vec_ref, bup_ref, own_ref = refs[:6]
-    pieces = [refs[6 + n * k : 6 + n * (k + 1)] for k in range(2 * cuts)]
-    outs, send_ref = refs[6 + 2 * cuts * n : -1], refs[-1]
-    keep_ref, sends = outs[0], outs[1 : 1 + stream.places]
-    act_ref, dres_ref, gvec_ref, gbup_ref, full_ref, out_acc, db_acc = outs[1 + stream.places :]
-    assemble(plan, own_ref, pieces[:cuts], pieces[cuts:], full_ref)
+    direct, cross, refs = refs[6 : 6 + n], refs[6 + n : 6 + 2 * n], refs[6 + 2 * n :]
+    messages = [(slice(0, WIDE), [r.at[:, :WIDE] for r in direct], [r.at[:, :WIDE] for r in cross])]
+    out_part, db_part = None, None
+    if rel == 0:
+        messages = [
+            (slice(0, EARLY), [r.at[:, WIDE:] for r in direct], [r.at[:, WIDE:] for r in cross]),
+            (slice(EARLY, WIDE), refs[:n], refs[n : 2 * n]),
+        ]
+        out_part, db_part, refs = refs[2 * n], refs[2 * n + 1], refs[2 * n + 2 :]
+    keep_ref, sends = refs[0], refs[1 : 1 + plan.n_opt]
+    gbup_ref, refs = refs[1 + plan.n_opt], refs[2 + plan.n_opt :]
     core, ybit = position()[:2]
+    blk = ybit ^ rel
+    full_ref, send_ref = refs[-2:]
+    halves = [own_ref[:, pl.ds(pl.multiple_of(mat * FF + blk * WIDE, 128), WIDE)] for mat in range(2)]
+    assemble(plan, halves, messages, full_ref)
+    up, down = full_ref[:, 0].reshape(D, WIDE), full_ref[:, 1].reshape(D, WIDE)
     resid = resid_ref[...]
     normed, rstd = ln_parts(resid)
     second_in = (normed * vec_ref[5:6, :] + vec_ref[6:7, :]).astype(bf16)
-    second_t = second_in.T
     dy = jnp.where(column_of(seg_ref[...]) >= 0, cot_ref[...].astype(f32), 0.0)
     dy_low = dy.astype(bf16)
-    dy_t = dy_low.T
-    out_acc[...] = jnp.zeros_like(out_acc)
-    db_acc[...] = jnp.zeros_like(db_acc)
-    wide = FF // 2
-
-    def one_block(blk, carry):
-        cols = pl.ds(pl.multiple_of(blk * wide, wide), wide)
-        up = full_ref[:, 0, :, cols].reshape(D, wide)
-        down = full_ref[:, 1, :, cols].reshape(D, wide)
-        pre = mm(second_in, up) + bup_ref[blk]
-        sq = pre * pre
-        th = jnp.tanh(gelu_c * pre * (1.0 + 0.044715 * sq))
-        half = 0.5 * (1.0 + th)
-        act = (pre * half).astype(bf16)
-        slope = half + (0.5 * gelu_c) * pre * (1.0 - th * th) * (1.0 + (3 * 0.044715) * sq)
-        out_acc[...] += mm_nt(act, down)
-        dpre = (mm(dy_low, down) * slope).astype(bf16)
-        gbup_ref[blk] = jnp.sum(dpre.astype(f32), axis=0, keepdims=True)
-        db_acc[...] += mm_nt(dpre, up)
-        base = (blk ^ ybit) * (stream.total // 2)
-        for mat, (left, right) in enumerate(((second_t, dpre), (dy_t, act))):
-            grad = mm(left, right)
-            first, last = grad[:, :D], grad[:, D:]
-            store_chunks(plan, stream, keep_ref, base, jnp.where(core == 0, first, last), mat)
-            store_chunks(plan, stream, send_ref, base, jnp.where(core == 0, last, first), mat)
-        return carry
-
-    lax.fori_loop(0, 2, one_block, 0, unroll=True)
+    pre = mm(second_in, up) + bup_ref[blk]
+    sq = pre * pre
+    th = jnp.tanh(gelu_c * pre * (1.0 + 0.044715 * sq))
+    half = 0.5 * (1.0 + th)
+    act = (pre * half).astype(bf16)
+    slope = half + (0.5 * gelu_c) * pre * (1.0 - th * th) * (1.0 + (3 * 0.044715) * sq)
+    dpre = (mm(dy_low, down) * slope).astype(bf16)
+    gbup_ref[...] = jnp.sum(dpre.astype(f32), axis=0, keepdims=True)
+    for mat, (left, right) in enumerate(((second_in.T, dpre), (dy_low.T, act))):
+        grad = mm(left, right)
+        first, last = grad[:, :D], grad[:, D:]
+        store_chunks(plan, stream, keep_ref, 0, jnp.where(core == 0, first, last), mat)
+        store_chunks(plan, stream, send_ref, 0, jnp.where(core == 0, last, first), mat)
     split_sends(stream, send_ref, sends)
-    act_ref[...] = (resid + out_acc[...] + vec_ref[7:8, :]).astype(bf16)
-    db = db_acc[...]
+    out, db = mm_nt(act, down), mm_nt(dpre, up)
+    if rel == 1:
+        refs[0][...], refs[1][...] = out, db
+        return
+    act_ref, dres_ref, gvec_ref = refs[:3]
+    act_ref[...] = (resid + (out_part[...] + out) + vec_ref[7:8, :]).astype(bf16)
+    db = db_part[...] + db
     dres_ref[...] = dy + ln_back(db, vec_ref[5:6, :], normed, rstd)
     gvec_ref[0:1, :] = jnp.sum(db * normed, axis=0, keepdims=True)
     gvec_ref[1:2, :] = jnp.sum(db, axis=0, keepdims=True)
@@ -319,23 +352,30 @@
         dqkv_ref[2, out_rows, :] = dkv_acc[1].astype(bf16)
 
 
-def attn_back_first(last, seg_ref, dres_ref, full_ref, mixed_ref, qkv_ref, lse_ref,
-                    dmix_ref, gout_ref, gbo_ref, dqkv_ref, bias_ref, dkv_acc):
+def start_loads(sources, targets, sems):
+    copies = [pltpu.make_async_copy(src, dst, sems.at[k]) for k, (src, dst) in enumerate(zip(sources, targets))]
+    for copy in copies:
+        copy.start()
+    return copies
+
+
+def attn_back_first(last, bias_ref, dres_ref, full_ref, mixed_ref, qkv_ref, lse_ref, *refs):
+    sources, (dmix_ref, gout_ref, gbo_ref, dqkv_ref), states = refs[:3], refs[3:7], refs[7:10]
+    dkv_acc, sems = refs[10:]
+    copies = start_loads(sources, states, sems)
     dz = dres_ref[...].astype(bf16)
     gbo_ref[...] = jnp.broadcast_to(jnp.sum(dz.astype(f32), axis=0, keepdims=True), (8, D))
     out_weight = full_ref[:, 1, :, D:].reshape(D, D)
     dmix_ref[...] = mm_nt(out_weight, dz).astype(bf16)
     gout_ref[...] = mm(mixed_ref[...], dz)
-    fill_bias(seg_ref, bias_ref)
     back_heads(0, last, qkv_ref, bias_ref, lse_ref, dmix_ref, dqkv_ref, dkv_acc)
-
-
-def attn_back_next(first, last, seg_ref, dmix_ref, qkv_ref, lse_ref, *refs):
-    sources, dqkv_ref, states, (bias_ref, dkv_acc, sems) = refs[:6], refs[6], refs[7:13], refs[13:]
-    copies = [pltpu.make_async_copy(src, dst, sems.at[k]) for k, (src, dst) in enumerate(zip(sources, states))]
     for copy in copies:
-        copy.start()
-    fill_bias(seg_ref, bias_ref)
+        copy.wait()
+
+
+def attn_back_next(first, last, bias_ref, dmix_ref, qkv_ref, lse_ref, *refs):
+    sources, dqkv_ref, states, (dkv_acc, sems) = refs[:3], refs[3], refs[4:7], refs[7:]
+    copies = start_loads(sources, states, sems)
     back_heads(first, last, qkv_ref, bias_ref, lse_ref, dmix_ref, dqkv_ref, dkv_acc)
     for copy in copies:
         copy.wait()
@@ -343,10 +383,10 @@
 
 def attn_back_last(plan, count, *refs):
     stream = plan.attn
-    tok_ref, dres_ref, full_ref, vec_ref, gout_ref, gbo_ref, gvec_ref, gbup_ref = refs[:8]
-    parts = refs[8 : 8 + count]
-    keep_ref, sends = refs[8 + count], refs[9 + count : 9 + count + stream.places]
-    tail_ref, igrad_ref, send_ref = refs[9 + count + stream.places :]
+    tok_ref, dres_ref, full_ref, vec_ref, gout_ref, gbo_ref, gvec_ref, gbup0, gbup1 = refs[:9]
+    parts = refs[9 : 9 + count]
+    keep_ref, sends = refs[9 + count], refs[10 + count : 10 + count + stream.places]
+    igrad_ref, send_ref = refs[10 + count + stream.places :]
     core, ybit = position()[:2]
     hidden = tok_ref[...].astype(f32)
     normed, rstd = ln_parts(hidden)
@@ -377,24 +417,26 @@
         gvec_ref[0:3, :],
     ]
     for blk in range(2):
-        rows += [gbup_ref[blk][:, :D], gbup_ref[blk][:, D:]]
+        near, far = (gbup0, gbup1) if blk == 0 else (gbup1, gbup0)
+        gbup = jnp.where(ybit == 0, near[...], far[...])
+        rows += [gbup[:, :D], gbup[:, D:]]
     rows.append(jnp.zeros((VEC_ROWS - 12, D), f32))
     total = jnp.concatenate(rows, axis=0)
     for t in range(stream.tail):
         piece = total[t * stream.unit : (t + 1) * stream.unit]
         keep_ref[stream.total + t] = piece
-        tail_ref[t] = piece.astype(bf16)
-
-
-def add_core(stream, keep_ref, *refs):
-    others, outs = refs[: -stream.places], refs[-stream.places :]
+        sends[-1][stream.piece + t] = piece.astype(bf16)
+
+
+def add_core(stream, count, keep_ref, *refs):
+    others, outs = refs[:-count], refs[-count:]
     size = stream.piece
-    for number in range(stream.places):
-        total = keep_ref[number * size : (number + 1) * size] + others[number][...].astype(f32)
+    for number in range(count):
+        total = keep_ref[number * size : (number + 1) * size] + others[number][:size].astype(f32)
         outs[number][:size] = total.astype(outs[number].dtype)
     if stream.tail:
-        total = keep_ref[stream.total :] + others[stream.places][...].astype(f32)
-        for number in range(stream.places):
+        total = keep_ref[count * size :] + others[-1][size:].astype(f32)
+        for number in range(count):
             outs[number][size:] = total.astype(outs[number].dtype)
 
 
@@ -438,21 +480,16 @@
     return lax.ppermute(value, "dp", [(i, i ^ mask) for i in range(plan.n_dp)])
 
 
-def reduce_core(plan, stream, keep, sends):
-    got = [swap_core(plan.n_dp, send) for send in sends]
+def reduce_core(stream, keep, got, keeps_first, count):
     shape = (stream.piece + stream.tail, stream.unit, D)
-    outs = [shaped(shape, f32 if k == 0 else bf16) for k in range(stream.places)]
-
-    def finish(got):
-        return call(
-            functools.partial(add_core, stream),
-            outs,
-            [vmem] * (1 + len(got)),
-            [keep, *got],
-            name="add_core_" + stream.name,
-        )
-
-    return got, finish
+    outs = [shaped(shape, f32 if k == 0 and keeps_first else bf16) for k in range(count)]
+    return call(
+        functools.partial(add_core, stream, count),
+        outs,
+        [vmem] * (1 + len(got)),
+        [keep, *got],
+        name="add_core_" + stream.name,
+    )
 
 
 def send_plane(plan, parts):
@@ -544,103 +581,143 @@
 
 def body(plan, tokens, segment, cotangent, w_attn, m_attn, v_attn, w_mlp, m_mlp, v_mlp, vectors, m_vec, v_vec):
     n_dp, n_opt, own = plan.n_dp, plan.n_opt, plan.own
-    core = lax.axis_index("dp") & 1
     seg = segment.reshape(1, TOK)
 
     def spread(send):
         return [lax.ppermute(send, "opt", [(o, o ^ m) for o in range(n_opt)]) for m in range(1, n_opt)]
 
-    width = 2 * D
+    any_spec = pl.BlockSpec(memory_space=pl.ANY)
     length = vectors.shape[0]
-    vec_pad = jnp.pad(vectors.astype(bf16), (0, 16 * width - length)).reshape(16, width)
-    attn_half = lax.dynamic_slice(w_attn, (0, core * width), (own, width)).astype(bf16)
-    attn_send = jnp.concatenate([attn_half, vec_pad], axis=0)
+    vec_in = vectors if length % D == 0 else jnp.pad(vectors, (0, 16 * D - length)).reshape(16, D)
+    (attn_send,) = call(
+        functools.partial(first_message, plan),
+        [shaped((own + 16, D), bf16)],
+        [any_spec] * 2,
+        [pltpu.with_memory_space_constraint(x, pltpu.HBM) for x in (w_attn, vec_in)],
+        [pltpu.VMEM((own, D), f32), pltpu.VMEM(vec_in.shape, f32), pltpu.SemaphoreType.DMA((2,))],
+        light=True,
+        name="first_message",
+    )
     attn_direct = spread(attn_send)
-    attn_cross = [swap_core(n_dp, piece) for piece in attn_direct]
-    widths = MLP_CUT
-    attn_low, mlp_low, *mlp_halves = call(
+    attn_low, mlp_low, mlp_early, mlp_late = call(
         functools.partial(cast_weights, plan),
-        [shaped((own, 4 * D), bf16), shaped((own, 2 * FF), bf16)] + [shaped((own, w), bf16) for w in widths],
+        [
+            shaped((own, 4 * D), bf16),
+            shaped((own, 2 * FF), bf16),
+            shaped((own, WIDE + EARLY), bf16),
+            shaped((own, WIDE - EARLY), bf16),
+        ],
         [vmem] * 2,
         [w_attn, after(w_mlp, attn_send)],
         name="cast_weights",
         room=20,
     )
-    mlp_direct = [spread(half) for k, half in enumerate(mlp_halves)]
+    early, late = spread(mlp_early), spread(mlp_late)
+    attn_y = [swap_dp(plan, piece, 2) for piece in attn_direct]
+    attn_pieces = attn_direct + [swap_core(n_dp, x) for x in attn_direct] + attn_y + [swap_core(n_dp, x) for x in attn_y]
     size = math.gcd(length, D)
-    full, qkv, mixed, lse, resid, vec8, bup = call(
-        functools.partial(attn_forward, plan, length),
+    heads = 2
+    full, qkv, mixed, lse, bias, vec8, bup = call(
+        functools.partial(attn_enter, plan, length, heads),
         [
-            shaped((n_opt, 2, own, width), bf16),
+            shaped((n_opt, 2, own, 2 * D), bf16),
             shaped((3, D, TOK), bf16),
-            shaped((D, TOK), bf16),
-            shaped((HEADS, 1, TOK), f32),
-            shaped((TOK, D), f32),
+            shaped((heads * HEAD_DIM, TOK), bf16),
+            shaped((heads, 1, TOK), f32),
+            shaped((TOK, TOK), f32),
             shaped((8, D), f32),
             shaped((2, 1, FF // 2), f32),
         ],
-        [vmem] * (4 + 2 * (n_opt - 1)),
-        [tokens, seg, attn_low, attn_send, *attn_direct, *attn_cross],
-        [pltpu.VMEM((TOK, TOK), f32), pltpu.VMEM((n_opt * length // size, 1, size), f32)],
+        [vmem] * (4 + 4 * (n_opt - 1)),
+        [tokens, seg, attn_low, attn_send, *attn_pieces],
+        [pltpu.VMEM((n_opt * length // size, 1, size), f32)],
         flops=2 * TOK * D * 4 * D + 8 * TOK * TOK * D,
-        name="attn_forward",
-    )
-    mlp_cross = [[swap_core(n_dp, after(piece, resid)) for piece in pieces] for pieces in mlp_direct]
+        light=True,
+        name="attn_enter",
+    )
+    early += [swap_core(n_dp, after(piece, vec8)) for piece in early]
+    mixed, lse, resid = call(
+        functools.partial(attn_leave, heads),
+        [shaped((D, TOK), bf16), shaped((HEADS, 1, TOK), f32), shaped((TOK, D), f32)],
+        [vmem] * 7,
+        [tokens, full, qkv, mixed, lse, bias, vec8],
+        light=True,
+        name="attn_leave",
+    )
     stream = plan.mlp
-    mlp_keep, *rest = call(
-        functools.partial(mlp_step, plan, len(widths)),
-        [
-            shaped((stream.total, stream.unit, D), f32),
-            *[shaped((stream.piece, stream.unit, D), bf16)] * stream.places,
-            shaped((TOK, D), bf16),
-            shaped((TOK, D), f32),
-            shaped((8, D), f32),
-            shaped((2, 1, FF // 2), f32),
-        ],
-        [vmem] * (6 + 2 * len(widths) * (n_opt - 1)),
-        [resid, cotangent, seg, vec8, bup, mlp_low, *sum(mlp_direct, []), *sum(mlp_cross, [])],
-        [
-            pltpu.VMEM((n_opt, 2, own, FF), bf16),
-            pltpu.VMEM((TOK, D), f32),
-            pltpu.VMEM((TOK, D), f32),
-            pltpu.VMEM((stream.total, stream.unit, D), bf16),
-        ],
-        flops=12 * TOK * D * FF,
+    half_units = stream.total // 2
+    half_outs = [
+        shaped((half_units, stream.unit, D), f32),
+        *[shaped((stream.piece, stream.unit, D), bf16)] * n_opt,
+        shaped((1, WIDE), f32),
+    ]
+    half_scratch = [pltpu.VMEM((n_opt, 2, own, WIDE), bf16), pltpu.VMEM((half_units, stream.unit, D), bf16)]
+    common = [resid, cotangent, seg, vec8, bup, mlp_low, *early]
+    far_keep, *far_sends, gbup1, out_part, db_part = call(
+        functools.partial(mlp_block, plan, 1),
+        half_outs + [shaped((TOK, D), f32)] * 2,
+        [vmem] * (6 + 2 * (n_opt - 1)),
+        common,
+        half_scratch,
+        flops=6 * TOK * D * FF,
         room=20,
-        name="mlp_step",
-    )
-    mlp_sends, (activations, dres, gvec, gbup) = rest[: stream.places], rest[stream.places :]
-    mlp_got, finish = reduce_core(plan, stream, mlp_keep, mlp_sends)
+        light=True,
+        name="mlp_far",
+    )
+    far_got = [swap_core(n_dp, send) for send in far_sends]
+    late += [swap_core(n_dp, after(piece, out_part)) for piece in late]
+    near_keep, *near_sends, gbup0, activations, dres, gvec = call(
+        functools.partial(mlp_block, plan, 0),
+        half_outs + [shaped((TOK, D), bf16), shaped((TOK, D), f32), shaped((8, D), f32)],
+        [vmem] * (8 + 4 * (n_opt - 1)),
+        common + late + [out_part, db_part],
+        half_scratch,
+        flops=6 * TOK * D * FF,
+        room=20,
+        name="mlp_near",
+    )
+    near_got = [swap_core(n_dp, send) for send in near_sends]
+    far_got[0] = after(far_got[0], dres)
+    far_parts = reduce_core(stream, far_keep, far_got, False, n_opt)
+    dres_in = after(dres, *far_parts)
 
     head_flops = 14 * TOK * TOK * HEAD_DIM
-    head_scratch = [pltpu.VMEM((TOK, TOK), f32), pltpu.VMEM((2, HEAD_DIM, TOK), f32)]
+    head_scratch = [pltpu.VMEM((2, HEAD_DIM, TOK), f32)]
     cuts = (0, 2, 6)
-    dmix, gout, gbo, part = call(
+    head_scratch.append(pltpu.SemaphoreType.DMA((3,)))
+
+    def state_args(arrays):
+        return [pltpu.with_memory_space_constraint(x, pltpu.HBM) for x in arrays], [shaped(x.shape, f32) for x in arrays]
+
+    sources, shapes = state_args([w_attn, m_attn, v_attn])
+    dmix, gout, gbo, part, *attn_states = call(
         functools.partial(attn_back_first, cuts[1]),
         [
             shaped((D, TOK), bf16),
             shaped((D, D), f32),
             shaped((8, D), f32),
             shaped((3, cuts[1] * HEAD_DIM, TOK), bf16),
+            *shapes,
         ],
-        [vmem] * 6,
-        [seg, dres, full, mixed, qkv, lse],
+        [vmem] * 6 + [any_spec] * 3,
+        [bias, dres_in, full, mixed, qkv, lse, *sources],
         head_scratch,
+        light=True,
         flops=4 * TOK * D * D + cuts[1] * head_flops,
         name="attn_back_first",
     )
-    mlp_got[0] = after(mlp_got[0], dmix)
-    mlp_parts = finish(mlp_got)
+    near_got[0] = after(near_got[0], dmix)
+    mlp_parts = reduce_core(plan.mlp, near_keep, near_got, True, n_opt)
     dmix = after(dmix, *mlp_parts)
-    states = [w_mlp, m_mlp, v_mlp, w_attn, m_attn, v_attn]
-    next_part, *states = call(
+    sources, shapes = state_args([w_mlp, m_mlp, v_mlp])
+    next_part, *mlp_states = call(
         functools.partial(attn_back_next, cuts[1], cuts[2]),
-        [shaped((3, (cuts[2] - cuts[1]) * HEAD_DIM, TOK), bf16)] + [shaped(x.shape, f32) for x in states],
-        [vmem] * 4 + [pl.BlockSpec(memory_space=pl.ANY)] * 6,
-        [seg, dmix, qkv, lse] + [pltpu.with_memory_space_constraint(x, pltpu.HBM) for x in states],
-        head_scratch + [pltpu.SemaphoreType.DMA((6,))],
+        [shaped((3, (cuts[2] - cuts[1]) * HEAD_DIM, TOK), bf16), *shapes],
+        [vmem] * 4 + [any_spec] * 3,
+        [bias, dmix, qkv, lse, *sources],
+        head_scratch,
         light=True,
-        room=24,
+        room=20,
         name="attn_back_next",
     )
     parts = [part, next_part]
@@ -649,12 +726,12 @@
         functools.partial(attn_back_last, plan, len(parts)),
         [
             shaped((stream.total + stream.tail, stream.unit, D), f32),
-            *[shaped((stream.piece, stream.unit, D), bf16)] * stream.places,
-            shaped((stream.tail, stream.unit, D), bf16),
+            *[shaped((stream.piece, stream.unit, D), bf16)] * (stream.places - 1),
+            shaped((stream.piece + stream.tail, stream.unit, D), bf16),
             shaped((TOK, D), f32),
         ],
-        [vmem] * (8 + len(parts)),
-        [tokens, dres, full, vec8, gout, gbo, gvec, gbup, *parts],
+        [vmem] * (9 + len(parts)),
+        [tokens, dres, full, vec8, gout, gbo, gvec, gbup0, gbup1, *parts],
         [pltpu.VMEM((stream.total, stream.unit, D), bf16)],
         light=True,
         flops=12 * TOK * D * D,
@@ -662,11 +739,11 @@
     )
     mlp, attn = plan.mlp, plan.attn
     zbits = [4 << k for k in range(plan.n_z.bit_length() - 1)]
-    attn_got, finish = reduce_core(plan, attn, attn_keep, attn_sends)
-    mlp_got = send_plane(plan, mlp_parts)
+    attn_got = [swap_core(n_dp, send) for send in attn_sends]
+    mlp_got = send_plane(plan, mlp_parts + far_parts)
     mlp_keep, mlp_send = reduce_plane(mlp, mlp_parts[0], mlp_got)
     attn_got[0] = after(attn_got[0], mlp_send)
-    attn_parts = finish(attn_got)
+    attn_parts = reduce_core(attn, attn_keep, attn_got, True, attn.places)
     mlp_got = swap_dp(plan, mlp_send, zbits[0])
     attn_got = send_plane(plan, attn_parts)
     mlp_got = after(mlp_got, attn_parts[1])
@@ -707,10 +784,10 @@
         new_vec, first_vec, second_vec = adamw(vectors, m_vec, v_vec, own_vec, vector_rate, 0.0)
     attn_y = swap_dp(plan, attn_own, 2)
     mlp_grads[0] = after(mlp_grads[0], attn_own)
-    new_mlp, first_mlp, second_mlp = adam_matrix(plan, mlp, mlp_grads, *states[:3])
+    new_mlp, first_mlp, second_mlp = adam_matrix(plan, mlp, mlp_grads, *mlp_states)
     attn_y = after(attn_y, new_mlp)
     attn_grads = [attn_own, swap_core(n_dp, attn_own), attn_y, swap_core(n_dp, attn_y)]
-    new_attn, first_attn, second_attn = adam_matrix(plan, attn, attn_grads, *states[3:])
+    new_attn, first_attn, second_attn = adam_matrix(plan, attn, attn_grads, *attn_states)
     return (
         activations,
         input_grad,

time: 96.2 us -> 88.8 us (0.923)
  waiting for transfers between devices: 36.9 us -> 26.1 us
  starting transfers between devices: 23.5 us -> 28.5 us
  local copies, waits for them, and re-layouts: 2.85 us -> 1.69 us
    ppermute x2 -> x3, waiting for transfers between devices: 11.7 us -> 2.37 us  [spread(): lax.ppermute(send, 'opt', [(o, o ^ m) for o in range(n_opt)])]
    ppermute x8 -> x9, waiting for transfers between devices: 10.7 us -> 14.4 us  [swap_dp(): return lax.ppermute(value, 'dp', [(i, i ^ mask) for i in range(plan.n_dp)])]
    ppermute x6, waiting for transfers between devices: 8.88 us -> 5.77 us  [send_plane(): got.append(lax.ppermute(parts[number], ('dp', 'opt'), perm))]
    ppermute x2 -> x3, starting transfers between devices: 3.09 us -> 5.74 us  [spread(): lax.ppermute(send, 'opt', [(o, o ^ m) for o in range(n_opt)])]
    ppermute x17 -> x18, waiting for transfers between devices: 5.68 us -> 3.5 us  [swap_core(): return lax.ppermute(value, 'dp', [(i, i ^ 1) for i in range(n_dp)])]
    ppermute x8 -> x9, starting transfers between devices: 10.5 us -> 12.4 us  [swap_dp(): return lax.ppermute(value, 'dp', [(i, i ^ mask) for i in range(plan.n_dp)])]
    convert_element_type x1 -> x0, local copies, waits for them, and re-layouts: 1.1 us -> none  [body(): lax.dynamic_slice(w_attn, (0, core * width), (own, width)).astype(bf16)]
    pallas_call x14 -> x18, Pallas kernels: 24.3 us -> 24.8 us  [call(): pl.pallas_call(kernel, out_shape=list(outs), in_specs=list(ins), out_spec...]
  transfers between devices with their start and end apart: 33 -> 36, of which waited for: 15 -> 16; matrix products, arithmetic and copies ran while one was open for 0% -> 0% of each run, Pallas kernels for 23% -> 32%
where the time goes in v3:
time: 88.8 us; the launch traced here: 88.6 us
  Pallas kernels  31.5 us (35%)
  starting transfers between devices  28.5 us (32%)
  waiting for transfers between devices  26.1 us (29%)
  local copies, waits for them, and re-layouts  1.69 us (2%)
    pallas_call x18, Pallas kernels, call(): pl.pallas_call(kernel, out_shape=list(outs), in_specs=list(ins), out_spec...  24.8 us
    ppermute x9, waiting for transfers between devices, swap_dp(): return lax.ppermute(value, 'dp', [(i, i ^ mask) for i in range(plan.n_dp)])  14.4 us
    ppermute x9, starting transfers between devices, swap_dp(): return lax.ppermute(value, 'dp', [(i, i ^ mask) for i in range(plan.n_dp)])  12.4 us
    ppermute x6, starting transfers between devices, send_plane(): got.append(lax.ppermute(parts[number], ('dp', 'opt'), perm))  7.17 us
    pallas_call x2, Pallas kernels, adam_matrix(): pl.pallas_call(functools.partial(adam_kernel, stream, rows), grid=(stream...  6.65 us
    ppermute x6, waiting for transfers between devices, send_plane(): got.append(lax.ppermute(parts[number], ('dp', 'opt'), perm))  5.77 us
    ppermute x3, starting transfers between devices, spread(): lax.ppermute(send, 'opt', [(o, o ^ m) for o in range(n_opt)])  5.74 us
    ppermute x18, waiting for transfers between devices, swap_core(): return lax.ppermute(value, 'dp', [(i, i ^ 1) for i in range(n_dp)])  3.5 us
  transfers between devices with their start and end apart: 36, of which 16 were waited for; matrix products, arithmetic and copies ran while one was open for 0% of the time, Pallas kernels for 32%

profile of v3, /device:TPU:0, one launch (start us, length us, event | category | flops | bytes accessed | tf_op | source)
XLA Modules:
  0.0 88.6 jit_solution(7325651165874640986)
XLA Ops:
  0.6 0.0 copy-start
  0.7 1.1 %first_message.1.refs_3_ = bf16[208,384]{1,0:T(8,128)(2,1)S(1)} custom-call(f32[192,1536]{1,0:T(8,128)} %refs_0_.5, f32[2304]{0:T(1024)} %w_ref.3), custom_call_target="tpu_custom_call" | custom-call | tf_op jit(solution)/shard_map/first_message/pallas_call | solution.py:79
  1.8 3.0 %collective-permute-start = (bf16[208,384]{1,0:T(8,128)(2,1)S(1)}, bf16[208,384]{1,0:T(8,128)(2,1)S(1)}, u32[]{:S(2)}, u32[]{:S(2)}) collective-permute-start(bf16[208,384]{1,0:T(8,128)(2,1)S(1)} %first_message.1.refs_3_), channel_id=1, source_target_pairs={{0,1},{1,0},{2,3},{3,2},{4,5},{5,4},{6,7},{7,6},{8,9},{9,8},{10,11... | collective-permute-start | bytes 479240 | tf_op jit(solution)/shard_map/ppermute | solution.py:587
  4.8 1.7 %copy-done.1 = f32[192,3072]{1,0:T(8,128)S(1)} copy-done((f32[192,3072]{1,0:T(8,128)S(1)}, f32[192,3072]{1,0:T(8,128)}, u32[]{:S(2)}) %copy-start.1) | copy-done | bytes 2359320
  6.4 0.2 cast_weights.1
  6.7 0.3 collective-permute-start.4
  6.9 2.4 %collective-permute-done.refs_4_ = bf16[208,384]{1,0:T(8,128)(2,1)S(1)} collective-permute-done((bf16[208,384]{1,0:T(8,128)(2,1)S(1)}, bf16[208,384]{1,0:T(8,128)(2,1)S(1)}, u32[]{:S(2)}, u32[]{:S(2)}) %collective-permute-start) | collective-permute-done | bytes 159776 | tf_op jit(solution)/shard_map/ppermute | solution.py:587
  9.3 1.5 %collective-permute-start.2 = (bf16[208,384]{1,0:T(8,128)(2,1)S(1)}, bf16[208,384]{1,0:T(8,128)(2,1)S(1)}, u32[]{:S(2)}, u32[]{:S(2)}) collective-permute-start(bf16[208,384]{1,0:T(8,128)(2,1)S(1)} %collective-permute-done.refs_4_), channel_id=1, source_target_pairs={{0,4},{2,6},{4,0},{6,2},{8,12},{10,14},{12,8},{14,10},{16,20},{18,... | collective-permute-start | bytes 479240 | tf_op jit(solution)/shard_map/ppermute | solution.py:480
  10.8 3.7 %collective-permute-done.2.refs_6_ = bf16[208,384]{1,0:T(8,128)(2,1)S(1)} collective-permute-done((bf16[208,384]{1,0:T(8,128)(2,1)S(1)}, bf16[208,384]{1,0:T(8,128)(2,1)S(1)}, u32[]{:S(2)}, u32[]{:S(2)}) %collective-permute-start.2) | collective-permute-done | bytes 159776 | tf_op jit(solution)/shard_map/ppermute | solution.py:480
  14.6 0.0 collective-permute-start.3
  14.6 0.0 collective-permute-done.1.refs_5_
  14.6 1.4 %collective-permute-done.3.refs_7_ = bf16[208,384]{1,0:T(8,128)(2,1)S(1)} collective-permute-done((bf16[208,384]{1,0:T(8,128)(2,1)S(1)}, bf16[208,384]{1,0:T(8,128)(2,1)S(1)}, u32[]{:S(2)}, u32[]{:S(2)}) %collective-permute-start.3) | collective-permute-done | bytes 159776 | tf_op jit(solution)/shard_map/ppermute | solution.py:476
  16.0 2.5 %attn_enter.1 = (bf16[2,2,192,768]{3,2,1,0:T(8,128)(2,1)S(1)}, bf16[3,384,512]{2,1,0:T(8,128)(2,1)S(1)}, bf16[128,512]{1,0:T(8,128)(2,1)S(1)}, f32[2,1,512]{2,1,...) custom-call(bf16[512,384]{1,0:T(8,128)(2,1)S(1)} %copy-done.2, ...), custom_call_target="tpu_custom_call" | custom-call | tf_op jit(solution)/shard_map/attn_enter/pallas_call | solution.py:79
  18.5 0.2 collective-permute-start.5
  18.7 2.5 %collective-permute-start.6 = (bf16[192,384]{1,0:T(8,128)(2,1)S(1)}, bf16[192,384]{1,0:T(8,128)(2,1)S(1)}, u32[]{:S(2)}, u32[]{:S(2)}) collective-permute-start(bf16[192,384]{1,0:T(8,128)(2,1)S(1)} %get-tuple-element.103), channel_id=1, source_target_pairs={{0,1},{1,0},{2,3},{3,2},{4,5},{5,4},{6,7},{7,6},{8,9},{9,8},{10,11... | collective-permute-start | bytes 442376 | tf_op jit(solution)/shard_map/ppermute | solution.py:587
  21.1 3.2 %attn_leave.1 = (bf16[384,512]{1,0:T(8,128)(2,1)S(1)}, f32[6,1,512]{2,1,0:T(1,128)S(1)}, f32[512,384]{1,0:T(8,128)S(1)}) custom-call(bf16[512,384]{1,0:T(8,128)(2,1)S(1)} %copy-done.2, bf16[2,2,192,768]{3,2,1,0:T(8,128)(2,1)S(1)} %get-tuple-element.92.full_ref.refs_2_, bf16[3,384,512]{2,1,0:T(8,128)(2,1)S(1)} %get-tuple-element.93.qkv_ref, ...), custom_call_target="tpu_custom_call" | custom-call | tf_op jit(solution)/shard_map/attn_leave/pallas_call | solution.py:79
  24.3 3.4 %mlp_far.1 = (f32[48,16,384]{2,1,0:T(8,128)S(1)}, bf16[24,16,384]{2,1,0:T(8,128)(2,1)S(1)}, bf16[24,16,384]{2,1,0:T(8,128)(2,1)S(1)}, f32[1,768]{1,0:T(1,128)S(1...) custom-call(f32[512,384]{1,0:T(8,128)S(1)} %get-tuple-element.98.refs_0_, bf16[512,384]{1,0:T(8,128)(2,1)S(1)} %copy-done.3, ...), custom_call_target="tpu_custom_call" | custom-call | tf_op jit(solution)/shard_map/mlp_far/pallas_call | solution.py:79
  27.7 0.2 collective-permute-start.7
  27.9 0.4 collective-permute-start.8
  28.3 0.1 collective-permute-start.9
  28.4 0.7 collective-permute-done.7.refs_9_
  29.1 3.8 %mlp_near.1 = (f32[48,16,384]{2,1,0:T(8,128)S(1)}, bf16[24,16,384]{2,1,0:T(8,128)(2,1)S(1)}, bf16[24,16,384]{2,1,0:T(8,128)(2,1)S(1)}, f32[1,768]{1,0:T(1,128)S(...) custom-call(f32[512,384]{1,0:T(8,128)S(1)} %get-tuple-element.98.refs_0_, ...), custom_call_target="tpu_custom_call" | custom-call | flops 1811939328 | bytes 8096768 | tf_op jit(solution)/shard_map/mlp_near/pallas_call | solution.py:79
  32.9 0.2 collective-permute-start.10
  33.1 0.4 collective-permute-start.11
  33.5 0.1 add_core_mlp.2
  33.6 1.6 %collective-permute-start.14 = (bf16[24,16,384]{2,1,0:T(8,128)(2,1)S(1)}, bf16[24,16,384]{2,1,0:T(8,128)(2,1)S(1)}, u32[]{:S(2)}, u32[]{:S(2)}) collective-permute-start(bf16[24,16,384]{2,1,0:T(8,128)(2,1)S(1)} %get-tuple-element.113), channel_id=1, source_target_pairs={{0,4},{1,5},{2,6},{3,7},{4,0},{5,1},{6,2},{7,3},{8,12},{9,13},{10,... | collective-permute-start | bytes 884744 | tf_op jit(solution)/shard_map/ppermute | solution.py:503
  35.2 2.4 %attn_back_first.1 = (bf16[384,512]{1,0:T(8,128)(2,1)S(1)}, f32[384,384]{1,0:T(8,128)S(1)}, f32[8,384]{1,0:T(8,128)S(1)}, bf16[3,128,512]{2,1,0:T(8,128)(2,1)S(1...) custom-call(f32[512,512]{1,0:T(8,128)S(1)} %get-tuple-element.96.bias_ref, ...), custom_call_target="tpu_custom_call" | custom-call | tf_op jit(solution)/shard_map/attn_back_first/pallas_call | solution.py:79
  37.7 0.2 add_core_mlp.3
  37.9 2.0 %collective-permute-start.13 = (bf16[24,16,384]{2,1,0:T(8,128)(2,1)S(1)}, bf16[24,16,384]{2,1,0:T(8,128)(2,1)S(1)}, u32[]{:S(2)}, u32[]{:S(2)}) collective-permute-start(bf16[24,16,384]{2,1,0:T(8,128)(2,1)S(1)} %get-tuple-element.130), channel_id=1, source_target_pairs={{0,1},{1,0},{2,3},{3,2},{4,5},{5,4},{6,7},{7,6},{8,9},{9,8},{10,11... | collective-permute-start | bytes 884744 | tf_op jit(solution)/shard_map/ppermute | solution.py:503
  39.9 3.8 %attn_back_next.1 = (bf16[3,256,512]{2,1,0:T(8,128)(2,1)S(1)}, f32[192,3072]{1,0:T(8,128)S(1)}, f32[192,3072]{1,0:T(8,128)S(1)}, f32[192,3072]{1,0:T(8,128)S(1)}) custom-call(f32[512,512]{1,0:T(8,128)S(1)} %get-tuple-element.96.bias_ref, bf16[384,512]{1,0:T(8,128)(2,1)S(1)} %get-tuple-element.131.dmix_ref, ...), custom_call_target="tpu_custom_call" | custom-call | tf_op jit(solution)/shard_map/attn_back_next/pallas_call | solution.py:79
  43.6 3.1 %attn_back_last.1 = (f32[49,16,384]{2,1,0:T(8,128)S(1)}, bf16[12,16,384]{2,1,0:T(8,128)(2,1)S(1)}, bf16[12,16,384]{2,1,0:T(8,128)(2,1)S(1)}, bf16[12,16,384]{2,1...) custom-call(bf16[512,384]{1,0:T(8,128)(2,1)S(1)} %copy-done.2, ...), custom_call_target="tpu_custom_call" | custom-call | tf_op jit(solution)/shard_map/attn_back_last/pallas_call | solution.py:79
  46.7 0.5 collective-permute-start.12
  47.2 1.9 %collective-permute-done.14.refs_1_ = bf16[24,16,384]{2,1,0:T(8,128)(2,1)S(1)} collective-permute-done((bf16[24,16,384]{2,1,0:T(8,128)(2,1)S(1)}, bf16[24,16,384]{2,1,0:T(8,128)(2,1)S(1)}, u32[]{:S(2)}, u32[]{:S(2)}) %collective-permute-start.14) | collective-permute-done | bytes 294944 | tf_op jit(solution)/shard_map/ppermute | solution.py:503
  49.1 0.5 collective-permute-start.17
  49.6 0.7 collective-permute-done.13.refs_0_
  50.3 0.1 add_plane_mlp.1
  50.4 1.7 %collective-permute-start.20 = (bf16[12,16,384]{2,1,0:T(8,128)(2,1)S(1)}, bf16[12,16,384]{2,1,0:T(8,128)(2,1)S(1)}, u32[]{:S(2)}, u32[]{:S(2)}) collective-permute-start(bf16[12,16,384]{2,1,0:T(8,128)(2,1)S(1)} %get-tuple-element.136), channel_id=1, source_target_pairs={{0,8},{2,10},{4,12},{6,14},{8,0},{10,2},{12,4},{14,6},{16,24},{18,... | collective-permute-start | bytes 442376 | tf_op jit(solution)/shard_map/ppermute | solution.py:480
  52.1 0.1 add_core_attn.1
  52.2 0.4 collective-permute-start.19
  52.6 1.4 %collective-permute-start.21 = (bf16[13,16,384]{2,1,0:T(8,128)(2,1)S(1)}, bf16[13,16,384]{2,1,0:T(8,128)(2,1)S(1)}, u32[]{:S(2)}, u32[]{:S(2)}) collective-permute-start(bf16[13,16,384]{2,1,0:T(8,128)(2,1)S(1)} %get-tuple-element.146), channel_id=1, source_target_pairs={{0,4},{1,5},{2,6},{3,7},{4,0},{5,1},{6,2},{7,3},{8,12},{9,13},{10,... | collective-permute-start | bytes 479240 | tf_op jit(solution)/shard_map/ppermute | solution.py:503
  54.1 1.7 %collective-permute-start.22 = (bf16[13,16,384]{2,1,0:T(8,128)(2,1)S(1)}, bf16[13,16,384]{2,1,0:T(8,128)(2,1)S(1)}, u32[]{:S(2)}, u32[]{:S(2)}) collective-permute-start(bf16[13,16,384]{2,1,0:T(8,128)(2,1)S(1)} %get-tuple-element.147), channel_id=1, source_target_pairs={{0,5},{1,4},{2,7},{3,6},{4,1},{5,0},{6,3},{7,2},{8,13},{9,12},{10,... | collective-permute-start | bytes 479240 | tf_op jit(solution)/shard_map/ppermute | solution.py:503
  55.9 2.7 %collective-permute-start.24 = (bf16[12,16,384]{2,1,0:T(8,128)(2,1)S(1)}, bf16[12,16,384]{2,1,0:T(8,128)(2,1)S(1)}, u32[]{:S(2)}, u32[]{:S(2)}) collective-permute-start(bf16[12,16,384]{2,1,0:T(8,128)(2,1)S(1)} %add_two_mlp.2.left_ref), channel_id=1, source_target_pairs={{0,16},{2,18},{4,20},{6,22},{8,24},{10,26},{12,28},{14,30},{16,0},... | collective-permute-start | bytes 442376 | tf_op jit(solution)/shard_map/ppermute | solution.py:480
  58.5 0.5 collective-permute-done.19.refs_0_
  59.1 0.5 collective-permute-done.21.refs_1_
  59.5 2.2 %collective-permute-done.22.refs_2_ = bf16[13,16,384]{2,1,0:T(8,128)(2,1)S(1)} collective-permute-done((bf16[13,16,384]{2,1,0:T(8,128)(2,1)S(1)}, bf16[13,16,384]{2,1,0:T(8,128)(2,1)S(1)}, u32[]{:S(2)}, u32[]{:S(2)}) %collective-permute-start.22) | collective-permute-done | bytes 159776 | tf_op jit(solution)/shard_map/ppermute | solution.py:503
  61.7 0.1 add_plane_attn.1.left_ref
  61.8 1.5 %collective-permute-start.23 = (bf16[13,16,384]{2,1,0:T(8,128)(2,1)S(1)}, bf16[13,16,384]{2,1,0:T(8,128)(2,1)S(1)}, u32[]{:S(2)}, u32[]{:S(2)}) collective-permute-start(bf16[13,16,384]{2,1,0:T(8,128)(2,1)S(1)} %add_plane_attn.1.left_ref), channel_id=1, source_target_pairs={{0,8},{2,10},{4,12},{6,14},{8,0},{10,2},{12,4},{14,6},{16,24},{18,... | collective-permute-start | bytes 479240 | tf_op jit(solution)/shard_map/ppermute | solution.py:480
  63.3 0.7 collective-permute-done.24.right_ref
  64.0 0.6 collective-permute-start.31
  64.6 4.3 %collective-permute-done.23.right_ref = bf16[13,16,384]{2,1,0:T(8,128)(2,1)S(1)} collective-permute-done((bf16[13,16,384]{2,1,0:T(8,128)(2,1)S(1)}, bf16[13,16,384]{2,1,0:T(8,128)(2,1)S(1)}, u32[]{:S(2)}, u32[]{:S(2)}) %collective-permute-start.23) | collective-permute-done | bytes 159776 | tf_op jit(solution)/shard_map/ppermute | solution.py:480
  69.0 2.3 %collective-permute-start.25 = (bf16[13,16,384]{2,1,0:T(8,128)(2,1)S(1)}, bf16[13,16,384]{2,1,0:T(8,128)(2,1)S(1)}, u32[]{:S(2)}, u32[]{:S(2)}) collective-permute-start(bf16[13,16,384]{2,1,0:T(8,128)(2,1)S(1)} %add_two_attn.1.left_ref), channel_id=1, source_target_pairs={{0,16},{2,18},{4,20},{6,22},{8,24},{10,26},{12,28},{14,30},{16,0},... | collective-permute-start | bytes 479240 | tf_op jit(solution)/shard_map/ppermute | solution.py:480
  71.3 0.5 collective-permute-start.29
  71.7 0.5 collective-permute-done.31.refs_4_
  72.2 1.1 %collective-permute-start.33 = (bf16[12,16,384]{2,1,0:T(8,128)(2,1)S(1)}, bf16[12,16,384]{2,1,0:T(8,128)(2,1)S(1)}, u32[]{:S(2)}, u32[]{:S(2)}) collective-permute-start(bf16[12,16,384]{2,1,0:T(8,128)(2,1)S(1)} %collective-permute-done.31.refs_4_), channel_id=1, source_target_pairs={{0,4},{2,6},{4,0},{6,2},{8,12},{10,14},{12,8},{14,10},{16,20},{18,... | collective-permute-start | bytes 442376 | tf_op jit(solution)/shard_map/ppermute | solution.py:480
  73.3 0.5 collective-permute-start.32
  73.8 2.6 %collective-permute-done.29.refs_2_ = bf16[12,16,384]{2,1,0:T(8,128)(2,1)S(1)} collective-permute-done((bf16[12,16,384]{2,1,0:T(8,128)(2,1)S(1)}, bf16[12,16,384]{2,1,0:T(8,128)(2,1)S(1)}, u32[]{:S(2)}, u32[]{:S(2)}) %collective-permute-start.29) | collective-permute-done | bytes 147488 | tf_op jit(solution)/shard_map/ppermute | solution.py:480
  76.4 1.6 %collective-permute-done.33.refs_6_ = bf16[12,16,384]{2,1,0:T(8,128)(2,1)S(1)} collective-permute-done((bf16[12,16,384]{2,1,0:T(8,128)(2,1)S(1)}, bf16[12,16,384]{2,1,0:T(8,128)(2,1)S(1)}, u32[]{:S(2)}, u32[]{:S(2)}) %collective-permute-start.33) | collective-permute-done | bytes 147488 | tf_op jit(solution)/shard_map/ppermute | solution.py:480
  78.0 0.7 add_last.1
  78.7 0.5 collective-permute-start.27
  79.3 0.2 collective-permute-start.26
  79.5 4.4 %adam_mlp.1 = (f32[192,3072]{1,0:T(8,128)}, f32[192,3072]{1,0:T(8,128)}, f32[192,3072]{1,0:T(8,128)}) custom-call(bf16[12,16,384]{2,1,0:T(8,128)(2,1)S(1)} %add_two_mlp.3.refs_0_, bf16[12,16,384]{2,1,0:T(8,128)(2,1)S(1)} %collective-permute-done.28.refs_1_, bf16[12,16,384]{2,1,0:T(8,128)(2,1)S(1)} %collective-permute-done.29.refs_2_, ...), custom_call_target="tpu_custom_call" | custom-call | flops 9437184 | bytes 14155776 | tf_op jit(solution)/shard_map/adam_mlp/pallas_call | solution.py:568
  83.9 1.1 %collective-permute-done.27.refs_2_ = bf16[12,16,384]{2,1,0:T(8,128)(2,1)S(1)} collective-permute-done((bf16[12,16,384]{2,1,0:T(8,128)(2,1)S(1)}, bf16[12,16,384]{2,1,0:T(8,128)(2,1)S(1)}, u32[]{:S(2)}, u32[]{:S(2)}) %collective-permute-start.27) | collective-permute-done | bytes 147488 | tf_op jit(solution)/shard_map/ppermute | solution.py:480
  85.0 1.4 %collective-permute-done.35.refs_3_ = bf16[12,16,384]{2,1,0:T(8,128)(2,1)S(1)} collective-permute-done((bf16[12,16,384]{2,1,0:T(8,128)(2,1)S(1)}, bf16[12,16,384]{2,1,0:T(8,128)(2,1)S(1)}, u32[]{:S(2)}, u32[]{:S(2)}) %collective-permute-start.35) | collective-permute-done | bytes 147488 | tf_op jit(solution)/shard_map/ppermute | solution.py:476
  86.3 2.3 %adam_attn.1 = (f32[192,1536]{1,0:T(8,128)}, f32[192,1536]{1,0:T(8,128)}, f32[192,1536]{1,0:T(8,128)}) custom-call(bf16[12,16,384]{2,1,0:T(8,128)(2,1)S(1)} %get-tuple-element.150.refs_0_, bf16[12,16,384]{2,1,0:T(8,128)(2,1)S(1)} %collective-permute-done.26.refs_1_, bf16[12,16,384]{2,1,0:T(8,128)(2,1)S(1)} %collective-permute-done.27.refs_2_, ...), custom_call_target="tpu_custom_call" | custom-call | flops 4718592 | bytes 7077888 | tf_op jit(solution)/shard_map/adam_attn/pallas_call | solution.py:568
  (44 shorter events, 0.2 us)
Async XLA Ops:
  0.6 4.1 %copy-start = (f32[192,1536]{1,0:T(8,128)S(1)}, f32[192,1536]{1,0:T(8,128)}, u32[]{:S(2)}) copy-start(f32[192,1536]{1,0:T(8,128)} %refs_0_.5) | copy-start | bytes 3538948
  1.8 7.5 %collective-permute-start = (bf16[208,384]{1,0:T(8,128)(2,1)S(1)}, bf16[208,384]{1,0:T(8,128)(2,1)S(1)}, u32[]{:S(2)}, u32[]{:S(2)}) collective-permute-start(bf16[208,384]{1,0:T(8,128)(2,1)S(1)} %first_message.1.refs_3_), channel_id=1, source_target_pairs={{0,1},{1,0},{2,3},{3,2},{4,5},{5,4},{6,7},{7,6},{8,9},{9,8},{10,11... | collective-permute-start | bytes 479240 | tf_op jit(solution)/shard_map/ppermute | solution.py:587
  4.8 1.7 %copy-start.1 = (f32[192,3072]{1,0:T(8,128)S(1)}, f32[192,3072]{1,0:T(8,128)}, u32[]{:S(2)}) copy-start(f32[192,3072]{1,0:T(8,128)} %refs_0_.6) | copy-start | bytes 7077892
  6.4 9.5 %copy-start.2 = (bf16[512,384]{1,0:T(8,128)(2,1)S(1)}, bf16[512,384]{1,0:T(8,128)(2,1)}, u32[]{:S(2)}) copy-start(bf16[512,384]{1,0:T(8,128)(2,1)} %refs_0_.7) | copy-start | bytes 1179652
  6.4 9.5 %copy-start.7 = (s32[512]{0:T(512)S(1)}, s32[512]{0:T(512)}, u32[]{:S(2)}) copy-start(s32[512]{0:T(512)} %param.13) | copy-start | bytes 6148
  6.7 11.8 %collective-permute-start.4 = (bf16[192,1152]{1,0:T(8,128)(2,1)S(1)}, bf16[192,1152]{1,0:T(8,128)(2,1)S(1)}, u32[]{:S(2)}, u32[]{:S(2)}) collective-permute-start(bf16[192,1152]{1,0:T(8,128)(2,1)S(1)} %get-tuple-element.101), channel_id=1, source_target_pairs={{0,1},{1,0},{2,3},{3,2},{4,5},{5,4},{6,7},{7,6},{8,9},{9,8},{10,11... | collective-permute-start | bytes 1327112 | tf_op jit(solution)/shard_map/ppermute | solution.py:587
  9.3 5.3 %collective-permute-start.2 = (bf16[208,384]{1,0:T(8,128)(2,1)S(1)}, bf16[208,384]{1,0:T(8,128)(2,1)S(1)}, u32[]{:S(2)}, u32[]{:S(2)}) collective-permute-start(bf16[208,384]{1,0:T(8,128)(2,1)S(1)} %collective-permute-done.refs_4_), channel_id=1, source_target_pairs={{0,4},{2,6},{4,0},{6,2},{8,12},{10,14},{12,8},{14,10},{16,20},{18,... | collective-permute-start | bytes 479240 | tf_op jit(solution)/shard_map/ppermute | solution.py:480
  10.8 3.7 %collective-permute-start.1 = (bf16[208,384]{1,0:T(8,128)(2,1)S(1)}, bf16[208,384]{1,0:T(8,128)(2,1)S(1)}, u32[]{:S(2)}, u32[]{:S(2)}) collective-permute-start(bf16[208,384]{1,0:T(8,128)(2,1)S(1)} %collective-permute-done.refs_4_), channel_id=1, source_target_pairs={{0,2},{2,0},{4,6},{6,4},{8,10},{10,8},{12,14},{14,12},{16,18},{18,... | collective-permute-start | bytes 479240 | tf_op jit(solution)/shard_map/ppermute | solution.py:476
  14.6 1.4 %collective-permute-start.3 = (bf16[208,384]{1,0:T(8,128)(2,1)S(1)}, bf16[208,384]{1,0:T(8,128)(2,1)S(1)}, u32[]{:S(2)}, u32[]{:S(2)}) collective-permute-start(bf16[208,384]{1,0:T(8,128)(2,1)S(1)} %collective-permute-done.2.refs_6_), channel_id=1, source_target_pairs={{0,2},{2,0},{4,6},{6,4},{8,10},{10,8},{12,14},{14,12},{16,18},{18,... | collective-permute-start | bytes 479240 | tf_op jit(solution)/shard_map/ppermute | solution.py:476
  18.5 5.8 %collective-permute-start.5 = (bf16[192,1152]{1,0:T(8,128)(2,1)S(1)}, bf16[192,1152]{1,0:T(8,128)(2,1)S(1)}, u32[]{:S(2)}, u32[]{:S(2)}) collective-permute-start(bf16[192,1152]{1,0:T(8,128)(2,1)S(1)} %collective-permute-done.4.refs_6_), channel_id=1, source_target_pairs={{0,2},{2,0},{4,6},{6,4},{8,10},{10,8},{12,14},{14,12},{16,18},{18,... | collective-permute-start | bytes 1327112 | tf_op jit(solution)/shard_map/ppermute | solution.py:476
  18.7 9.0 %collective-permute-start.6 = (bf16[192,384]{1,0:T(8,128)(2,1)S(1)}, bf16[192,384]{1,0:T(8,128)(2,1)S(1)}, u32[]{:S(2)}, u32[]{:S(2)}) collective-permute-start(bf16[192,384]{1,0:T(8,128)(2,1)S(1)} %get-tuple-element.103), channel_id=1, source_target_pairs={{0,1},{1,0},{2,3},{3,2},{4,5},{5,4},{6,7},{7,6},{8,9},{9,8},{10,11... | collective-permute-start | bytes 442376 | tf_op jit(solution)/shard_map/ppermute | solution.py:587
  21.1 3.2 %copy-start.3 = (bf16[512,384]{1,0:T(8,128)(2,1)S(1)}, bf16[512,384]{1,0:T(8,128)(2,1)}, u32[]{:S(2)}) copy-start(bf16[512,384]{1,0:T(8,128)(2,1)} %refs_1_.5) | copy-start | bytes 1179652
  27.7 1.4 %collective-permute-start.7 = (bf16[192,384]{1,0:T(8,128)(2,1)S(1)}, bf16[192,384]{1,0:T(8,128)(2,1)S(1)}, u32[]{:S(2)}, u32[]{:S(2)}) collective-permute-start(bf16[192,384]{1,0:T(8,128)(2,1)S(1)} %collective-permute-done.6.refs_8_), channel_id=1, source_target_pairs={{0,2},{2,0},{4,6},{6,4},{8,10},{10,8},{12,14},{14,12},{16,18},{18,... | collective-permute-start | bytes 442376 | tf_op jit(solution)/shard_map/ppermute | solution.py:476
  27.9 5.6 %collective-permute-start.8 = (bf16[24,16,384]{2,1,0:T(8,128)(2,1)S(1)}, bf16[24,16,384]{2,1,0:T(8,128)(2,1)S(1)}, u32[]{:S(2)}, u32[]{:S(2)}) collective-permute-start(bf16[24,16,384]{2,1,0:T(8,128)(2,1)S(1)} %get-tuple-element.110), channel_id=1, source_target_pairs={{0,2},{2,0},{4,6},{6,4},{8,10},{10,8},{12,14},{14,12},{16,18},{18,... | collective-permute-start | bytes 884744 | tf_op jit(solution)/shard_map/ppermute | solution.py:476
  28.3 5.2 %collective-permute-start.9 = (bf16[24,16,384]{2,1,0:T(8,128)(2,1)S(1)}, bf16[24,16,384]{2,1,0:T(8,128)(2,1)S(1)}, u32[]{:S(2)}, u32[]{:S(2)}) collective-permute-start(bf16[24,16,384]{2,1,0:T(8,128)(2,1)S(1)} %get-tuple-element.112), channel_id=1, source_target_pairs={{0,2},{2,0},{4,6},{6,4},{8,10},{10,8},{12,14},{14,12},{16,18},{18,... | collective-permute-start | bytes 884744 | tf_op jit(solution)/shard_map/ppermute | solution.py:476
  32.9 4.8 %collective-permute-start.10 = (bf16[24,16,384]{2,1,0:T(8,128)(2,1)S(1)}, bf16[24,16,384]{2,1,0:T(8,128)(2,1)S(1)}, u32[]{:S(2)}, u32[]{:S(2)}) collective-permute-start(bf16[24,16,384]{2,1,0:T(8,128)(2,1)S(1)} %get-tuple-element.126), channel_id=1, source_target_pairs={{0,2},{2,0},{4,6},{6,4},{8,10},{10,8},{12,14},{14,12},{16,18},{18,... | collective-permute-start | bytes 884744 | tf_op jit(solution)/shard_map/ppermute | solution.py:476
  33.1 4.6 %collective-permute-start.11 = (bf16[24,16,384]{2,1,0:T(8,128)(2,1)S(1)}, bf16[24,16,384]{2,1,0:T(8,128)(2,1)S(1)}, u32[]{:S(2)}, u32[]{:S(2)}) collective-permute-start(bf16[24,16,384]{2,1,0:T(8,128)(2,1)S(1)} %get-tuple-element.128), channel_id=1, source_target_pairs={{0,2},{2,0},{4,6},{6,4},{8,10},{10,8},{12,14},{14,12},{16,18},{18,... | collective-permute-start | bytes 884744 | tf_op jit(solution)/shard_map/ppermute | solution.py:476
  33.6 15.4 %collective-permute-start.14 = (bf16[24,16,384]{2,1,0:T(8,128)(2,1)S(1)}, bf16[24,16,384]{2,1,0:T(8,128)(2,1)S(1)}, u32[]{:S(2)}, u32[]{:S(2)}) collective-permute-start(bf16[24,16,384]{2,1,0:T(8,128)(2,1)S(1)} %get-tuple-element.113), channel_id=1, source_target_pairs={{0,4},{1,5},{2,6},{3,7},{4,0},{5,1},{6,2},{7,3},{8,12},{9,13},{10,... | collective-permute-start | bytes 884744 | tf_op jit(solution)/shard_map/ppermute | solution.py:503
  35.2 13.8 %collective-permute-start.15 = (bf16[24,16,384]{2,1,0:T(8,128)(2,1)S(1)}, bf16[24,16,384]{2,1,0:T(8,128)(2,1)S(1)}, u32[]{:S(2)}, u32[]{:S(2)}) collective-permute-start(bf16[24,16,384]{2,1,0:T(8,128)(2,1)S(1)} %get-tuple-element.114), channel_id=1, source_target_pairs={{0,5},{1,4},{2,7},{3,6},{4,1},{5,0},{6,3},{7,2},{8,13},{9,12},{10,... | collective-permute-start | bytes 884744 | tf_op jit(solution)/shard_map/ppermute | solution.py:503
  37.9 12.4 %collective-permute-start.13 = (bf16[24,16,384]{2,1,0:T(8,128)(2,1)S(1)}, bf16[24,16,384]{2,1,0:T(8,128)(2,1)S(1)}, u32[]{:S(2)}, u32[]{:S(2)}) collective-permute-start(bf16[24,16,384]{2,1,0:T(8,128)(2,1)S(1)} %get-tuple-element.130), channel_id=1, source_target_pairs={{0,1},{1,0},{2,3},{3,2},{4,5},{5,4},{6,7},{7,6},{8,9},{9,8},{10,11... | collective-permute-start | bytes 884744 | tf_op jit(solution)/shard_map/ppermute | solution.py:503
  46.7 5.4 %collective-permute-start.18 = (bf16[13,16,384]{2,1,0:T(8,128)(2,1)S(1)}, bf16[13,16,384]{2,1,0:T(8,128)(2,1)S(1)}, u32[]{:S(2)}, u32[]{:S(2)}) collective-permute-start(bf16[13,16,384]{2,1,0:T(8,128)(2,1)S(1)} %get-tuple-element.140), channel_id=1, source_target_pairs={{0,2},{2,0},{4,6},{6,4},{8,10},{10,8},{12,14},{14,12},{16,18},{18,... | collective-permute-start | bytes 479240 | tf_op jit(solution)/shard_map/ppermute | solution.py:476
  46.7 5.4 %collective-permute-start.12 = (bf16[12,16,384]{2,1,0:T(8,128)(2,1)S(1)}, bf16[12,16,384]{2,1,0:T(8,128)(2,1)S(1)}, u32[]{:S(2)}, u32[]{:S(2)}) collective-permute-start(bf16[12,16,384]{2,1,0:T(8,128)(2,1)S(1)} %get-tuple-element.135), channel_id=1, source_target_pairs={{0,2},{2,0},{4,6},{6,4},{8,10},{10,8},{12,14},{14,12},{16,18},{18,... | collective-permute-start | bytes 442376 | tf_op jit(solution)/shard_map/ppermute | solution.py:476
  49.0 3.0 %collective-permute-start.16 = (bf16[12,16,384]{2,1,0:T(8,128)(2,1)S(1)}, bf16[12,16,384]{2,1,0:T(8,128)(2,1)S(1)}, u32[]{:S(2)}, u32[]{:S(2)}) collective-permute-start(bf16[12,16,384]{2,1,0:T(8,128)(2,1)S(1)} %get-tuple-element.138), channel_id=1, source_target_pairs={{0,2},{2,0},{4,6},{6,4},{8,10},{10,8},{12,14},{14,12},{16,18},{18,... | collective-permute-start | bytes 442376 | tf_op jit(solution)/shard_map/ppermute | solution.py:476
  49.1 3.0 %collective-permute-start.17 = (bf16[12,16,384]{2,1,0:T(8,128)(2,1)S(1)}, bf16[12,16,384]{2,1,0:T(8,128)(2,1)S(1)}, u32[]{:S(2)}, u32[]{:S(2)}) collective-permute-start(bf16[12,16,384]{2,1,0:T(8,128)(2,1)S(1)} %get-tuple-element.139), channel_id=1, source_target_pairs={{0,2},{2,0},{4,6},{6,4},{8,10},{10,8},{12,14},{14,12},{16,18},{18,... | collective-permute-start | bytes 442376 | tf_op jit(solution)/shard_map/ppermute | solution.py:476
  50.4 5.4 %collective-permute-start.20 = (bf16[12,16,384]{2,1,0:T(8,128)(2,1)S(1)}, bf16[12,16,384]{2,1,0:T(8,128)(2,1)S(1)}, u32[]{:S(2)}, u32[]{:S(2)}) collective-permute-start(bf16[12,16,384]{2,1,0:T(8,128)(2,1)S(1)} %get-tuple-element.136), channel_id=1, source_target_pairs={{0,8},{2,10},{4,12},{6,14},{8,0},{10,2},{12,4},{14,6},{16,24},{18,... | collective-permute-start | bytes 442376 | tf_op jit(solution)/shard_map/ppermute | solution.py:480
  52.2 6.8 %collective-permute-start.19 = (bf16[13,16,384]{2,1,0:T(8,128)(2,1)S(1)}, bf16[13,16,384]{2,1,0:T(8,128)(2,1)S(1)}, u32[]{:S(2)}, u32[]{:S(2)}) collective-permute-start(bf16[13,16,384]{2,1,0:T(8,128)(2,1)S(1)} %get-tuple-element.142), channel_id=1, source_target_pairs={{0,1},{1,0},{2,3},{3,2},{4,5},{5,4},{6,7},{7,6},{8,9},{9,8},{10,11... | collective-permute-start | bytes 479240 | tf_op jit(solution)/shard_map/ppermute | solution.py:503
  52.6 6.9 %collective-permute-start.21 = (bf16[13,16,384]{2,1,0:T(8,128)(2,1)S(1)}, bf16[13,16,384]{2,1,0:T(8,128)(2,1)S(1)}, u32[]{:S(2)}, u32[]{:S(2)}) collective-permute-start(bf16[13,16,384]{2,1,0:T(8,128)(2,1)S(1)} %get-tuple-element.146), channel_id=1, source_target_pairs={{0,4},{1,5},{2,6},{3,7},{4,0},{5,1},{6,2},{7,3},{8,12},{9,13},{10,... | collective-permute-start | bytes 479240 | tf_op jit(solution)/shard_map/ppermute | solution.py:503
  54.1 7.7 %collective-permute-start.22 = (bf16[13,16,384]{2,1,0:T(8,128)(2,1)S(1)}, bf16[13,16,384]{2,1,0:T(8,128)(2,1)S(1)}, u32[]{:S(2)}, u32[]{:S(2)}) collective-permute-start(bf16[13,16,384]{2,1,0:T(8,128)(2,1)S(1)} %get-tuple-element.147), channel_id=1, source_target_pairs={{0,5},{1,4},{2,7},{3,6},{4,1},{5,0},{6,3},{7,2},{8,13},{9,12},{10,... | collective-permute-start | bytes 479240 | tf_op jit(solution)/shard_map/ppermute | solution.py:503
  55.8 22.2 %copy-start.4 = (f32[2304]{0:T(1024)S(1)}, f32[2304]{0:T(1024)}, u32[]{:S(2)}) copy-start(f32[2304]{0:T(1024)} %w_ref.3) | copy-start | bytes 27652
  55.8 22.2 %copy-start.5 = (f32[2304]{0:T(1024)S(1)}, f32[2304]{0:T(1024)}, u32[]{:S(2)}) copy-start(f32[2304]{0:T(1024)} %m_ref.1) | copy-start | bytes 27652
  55.8 22.2 %copy-start.6 = (f32[2304]{0:T(1024)S(1)}, f32[2304]{0:T(1024)}, u32[]{:S(2)}) copy-start(f32[2304]{0:T(1024)} %v_ref.1) | copy-start | bytes 27652
  55.9 8.1 %collective-permute-start.24 = (bf16[12,16,384]{2,1,0:T(8,128)(2,1)S(1)}, bf16[12,16,384]{2,1,0:T(8,128)(2,1)S(1)}, u32[]{:S(2)}, u32[]{:S(2)}) collective-permute-start(bf16[12,16,384]{2,1,0:T(8,128)(2,1)S(1)} %add_two_mlp.2.left_ref), channel_id=1, source_target_pairs={{0,16},{2,18},{4,20},{6,22},{8,24},{10,26},{12,28},{14,30},{16,0},... | collective-permute-start | bytes 442376 | tf_op jit(solution)/shard_map/ppermute | solution.py:480
  61.8 7.1 %collective-permute-start.23 = (bf16[13,16,384]{2,1,0:T(8,128)(2,1)S(1)}, bf16[13,16,384]{2,1,0:T(8,128)(2,1)S(1)}, u32[]{:S(2)}, u32[]{:S(2)}) collective-permute-start(bf16[13,16,384]{2,1,0:T(8,128)(2,1)S(1)} %add_plane_attn.1.left_ref), channel_id=1, source_target_pairs={{0,8},{2,10},{4,12},{6,14},{8,0},{10,2},{12,4},{14,6},{16,24},{18,... | collective-permute-start | bytes 479240 | tf_op jit(solution)/shard_map/ppermute | solution.py:480
  64.0 8.2 %collective-permute-start.31 = (bf16[12,16,384]{2,1,0:T(8,128)(2,1)S(1)}, bf16[12,16,384]{2,1,0:T(8,128)(2,1)S(1)}, u32[]{:S(2)}, u32[]{:S(2)}) collective-permute-start(bf16[12,16,384]{2,1,0:T(8,128)(2,1)S(1)} %add_two_mlp.3.refs_0_), channel_id=1, source_target_pairs={{0,8},{2,10},{4,12},{6,14},{8,0},{10,2},{12,4},{14,6},{16,24},{18,... | collective-permute-start | bytes 442376 | tf_op jit(solution)/shard_map/ppermute | solution.py:480
  69.0 9.0 %collective-permute-start.25 = (bf16[13,16,384]{2,1,0:T(8,128)(2,1)S(1)}, bf16[13,16,384]{2,1,0:T(8,128)(2,1)S(1)}, u32[]{:S(2)}, u32[]{:S(2)}) collective-permute-start(bf16[13,16,384]{2,1,0:T(8,128)(2,1)S(1)} %add_two_attn.1.left_ref), channel_id=1, source_target_pairs={{0,16},{2,18},{4,20},{6,22},{8,24},{10,26},{12,28},{14,30},{16,0},... | collective-permute-start | bytes 479240 | tf_op jit(solution)/shard_map/ppermute | solution.py:480
  71.3 5.1 %collective-permute-start.29 = (bf16[12,16,384]{2,1,0:T(8,128)(2,1)S(1)}, bf16[12,16,384]{2,1,0:T(8,128)(2,1)S(1)}, u32[]{:S(2)}, u32[]{:S(2)}) collective-permute-start(bf16[12,16,384]{2,1,0:T(8,128)(2,1)S(1)} %add_two_mlp.3.refs_0_), channel_id=1, source_target_pairs={{0,4},{2,6},{4,0},{6,2},{8,12},{10,14},{12,8},{14,10},{16,20},{18,... | collective-permute-start | bytes 442376 | tf_op jit(solution)/shard_map/ppermute | solution.py:480
  72.2 5.8 %collective-permute-start.33 = (bf16[12,16,384]{2,1,0:T(8,128)(2,1)S(1)}, bf16[12,16,384]{2,1,0:T(8,128)(2,1)S(1)}, u32[]{:S(2)}, u32[]{:S(2)}) collective-permute-start(bf16[12,16,384]{2,1,0:T(8,128)(2,1)S(1)} %collective-permute-done.31.refs_4_), channel_id=1, source_target_pairs={{0,4},{2,6},{4,0},{6,2},{8,12},{10,14},{12,8},{14,10},{16,20},{18,... | collective-permute-start | bytes 442376 | tf_op jit(solution)/shard_map/ppermute | solution.py:480
  73.3 6.0 %collective-permute-start.28 = (bf16[12,16,384]{2,1,0:T(8,128)(2,1)S(1)}, bf16[12,16,384]{2,1,0:T(8,128)(2,1)S(1)}, u32[]{:S(2)}, u32[]{:S(2)}) collective-permute-start(bf16[12,16,384]{2,1,0:T(8,128)(2,1)S(1)} %add_two_mlp.3.refs_0_), channel_id=1, source_target_pairs={{0,2},{2,0},{4,6},{6,4},{8,10},{10,8},{12,14},{14,12},{16,18},{18,... | collective-permute-start | bytes 442376 | tf_op jit(solution)/shard_map/ppermute | solution.py:476
  73.3 6.2 %collective-permute-start.32 = (bf16[12,16,384]{2,1,0:T(8,128)(2,1)S(1)}, bf16[12,16,384]{2,1,0:T(8,128)(2,1)S(1)}, u32[]{:S(2)}, u32[]{:S(2)}) collective-permute-start(bf16[12,16,384]{2,1,0:T(8,128)(2,1)S(1)} %collective-permute-done.31.refs_4_), channel_id=1, source_target_pairs={{0,2},{2,0},{4,6},{6,4},{8,10},{10,8},{12,14},{14,12},{16,18},{18,... | collective-permute-start | bytes 442376 | tf_op jit(solution)/shard_map/ppermute | solution.py:476
  76.4 3.1 %collective-permute-start.30 = (bf16[12,16,384]{2,1,0:T(8,128)(2,1)S(1)}, bf16[12,16,384]{2,1,0:T(8,128)(2,1)S(1)}, u32[]{:S(2)}, u32[]{:S(2)}) collective-permute-start(bf16[12,16,384]{2,1,0:T(8,128)(2,1)S(1)} %collective-permute-done.29.refs_2_), channel_id=1, source_target_pairs={{0,2},{2,0},{4,6},{6,4},{8,10},{10,8},{12,14},{14,12},{16,18},{18,... | collective-permute-start | bytes 442376 | tf_op jit(solution)/shard_map/ppermute | solution.py:476
  78.0 1.5 %collective-permute-start.34 = (bf16[12,16,384]{2,1,0:T(8,128)(2,1)S(1)}, bf16[12,16,384]{2,1,0:T(8,128)(2,1)S(1)}, u32[]{:S(2)}, u32[]{:S(2)}) collective-permute-start(bf16[12,16,384]{2,1,0:T(8,128)(2,1)S(1)} %collective-permute-done.33.refs_6_), channel_id=1, source_target_pairs={{0,2},{2,0},{4,6},{6,4},{8,10},{10,8},{12,14},{14,12},{16,18},{18,... | collective-permute-start | bytes 442376 | tf_op jit(solution)/shard_map/ppermute | solution.py:476
  78.7 6.3 %collective-permute-start.27 = (bf16[12,16,384]{2,1,0:T(8,128)(2,1)S(1)}, bf16[12,16,384]{2,1,0:T(8,128)(2,1)S(1)}, u32[]{:S(2)}, u32[]{:S(2)}) collective-permute-start(bf16[12,16,384]{2,1,0:T(8,128)(2,1)S(1)} %get-tuple-element.150.refs_0_), channel_id=1, source_target_pairs={{0,4},{2,6},{4,0},{6,2},{8,12},{10,14},{12,8},{14,10},{16,20},{18,... | collective-permute-start | bytes 442376 | tf_op jit(solution)/shard_map/ppermute | solution.py:480
  79.3 5.7 %collective-permute-start.26 = (bf16[12,16,384]{2,1,0:T(8,128)(2,1)S(1)}, bf16[12,16,384]{2,1,0:T(8,128)(2,1)S(1)}, u32[]{:S(2)}, u32[]{:S(2)}) collective-permute-start(bf16[12,16,384]{2,1,0:T(8,128)(2,1)S(1)} %get-tuple-element.150.refs_0_), channel_id=1, source_target_pairs={{0,2},{2,0},{4,6},{6,4},{8,10},{10,8},{12,14},{14,12},{16,18},{18,... | collective-permute-start | bytes 442376 | tf_op jit(solution)/shard_map/ppermute | solution.py:476
  85.0 1.4 %collective-permute-start.35 = (bf16[12,16,384]{2,1,0:T(8,128)(2,1)S(1)}, bf16[12,16,384]{2,1,0:T(8,128)(2,1)S(1)}, u32[]{:S(2)}, u32[]{:S(2)}) collective-permute-start(bf16[12,16,384]{2,1,0:T(8,128)(2,1)S(1)} %collective-permute-done.27.refs_2_), channel_id=1, source_target_pairs={{0,2},{2,0},{4,6},{6,4},{8,10},{10,8},{12,14},{14,12},{16,18},{18,... | collective-permute-start | bytes 442376 | tf_op jit(solution)/shard_map/ppermute | solution.py:476

commit v4 on v3

--- a/solution.py
+++ b/solution.py
@@ -14,6 +14,7 @@
 FF = 1536
 TOK = 512
 QBLK = 256
+FORWARD_BLK = 512
 STEP = 10
 VEC_ROWS = 16
 
@@ -225,9 +226,9 @@
 def forward_heads(first, last, qkv_ref, bias_ref, mixed_ref, lse_ref):
     for head in range(first, last):
         rows = slice(head * HEAD_DIM, (head + 1) * HEAD_DIM)
-        for blk in range(TOK // QBLK):
-            cols = slice(blk * QBLK, (blk + 1) * QBLK)
-            keys = (blk + 1) * QBLK
+        for blk in range(TOK // FORWARD_BLK):
+            cols = slice(blk * FORWARD_BLK, (blk + 1) * FORWARD_BLK)
+            keys = (blk + 1) * FORWARD_BLK
             query = qkv_ref[0, rows, cols] * bf16(HEAD_DIM**-0.5)
             scores = mm_tn(qkv_ref[1, rows, :keys], query) + bias_ref[:keys, cols]
             top = jnp.max(scores, axis=0, keepdims=True)
@@ -579,6 +580,40 @@
     )(*grads, *states)
 
 
+def adam_half_kernel(stream, rel, *refs):
+    grads, states, outs = refs[:2], refs[2:5], refs[-7:-4]
+    bufs, sems = refs[-4:-1], refs[-1]
+    core, ybit, _, _ = position()
+    copies = []
+    for number, ref in enumerate(grads):
+        cols = pl.ds(pl.multiple_of(((number + 2 * rel) ^ (core + 2 * ybit)) * D, D), D)
+        grad = ref[...].reshape(ref.shape[0] * ref.shape[1], D).astype(f32)
+        values = adamw(*[state[:, cols] for state in states], grad, matrix_rate, matrix_decay)
+        for k in range(3):
+            bufs[k][number] = values[k]
+            copy = pltpu.make_async_copy(bufs[k].at[number], outs[k].at[:, cols], sems.at[number, k])
+            copy.start()
+            copies.append(copy)
+    for copy in copies:
+        copy.wait()
+
+
+def adam_half(plan, stream, rel, grads, states, before=()):
+    any_spec = pl.BlockSpec(memory_space=pl.ANY)
+    shape = shaped(states[0].shape, f32)
+    return pl.pallas_call(
+        functools.partial(adam_half_kernel, stream, rel),
+        out_shape=[shape] * 3,
+        in_specs=[vmem] * 5 + [any_spec] * len(before),
+        out_specs=[any_spec] * 3,
+        scratch_shapes=[pltpu.VMEM((2, plan.own, D), f32)] * 3 + [pltpu.SemaphoreType.DMA((2, 3))],
+        input_output_aliases={5 + k: k for k in range(len(before))},
+        compiler_params=pltpu.CompilerParams(vmem_limit_bytes=16 * MIB),
+        cost_estimate=pl.CostEstimate(flops=0, bytes_accessed=0, transcendentals=0),
+        name="adam_half_" + str(rel),
+    )(*grads, *states, *before)
+
+
 def body(plan, tokens, segment, cotangent, w_attn, m_attn, v_attn, w_mlp, m_mlp, v_mlp, vectors, m_vec, v_vec):
     n_dp, n_opt, own = plan.n_dp, plan.n_opt, plan.own
     seg = segment.reshape(1, TOK)
@@ -783,11 +818,12 @@
         own_vec = lax.dynamic_slice(vec_grad.reshape(-1), (lax.axis_index("opt") * length,), (length,))
         new_vec, first_vec, second_vec = adamw(vectors, m_vec, v_vec, own_vec, vector_rate, 0.0)
     attn_y = swap_dp(plan, attn_own, 2)
-    mlp_grads[0] = after(mlp_grads[0], attn_own)
     new_mlp, first_mlp, second_mlp = adam_matrix(plan, mlp, mlp_grads, *mlp_states)
+    near_grads = [after(attn_own, new_mlp), swap_core(n_dp, attn_own)]
+    near_done = adam_half(plan, attn, 0, near_grads, attn_states)
     attn_y = after(attn_y, new_mlp)
-    attn_grads = [attn_own, swap_core(n_dp, attn_own), attn_y, swap_core(n_dp, attn_y)]
-    new_attn, first_attn, second_attn = adam_matrix(plan, attn, attn_grads, *attn_states)
+    cross_y = after(swap_core(n_dp, attn_y), near_done[0])
+    new_attn, first_attn, second_attn = adam_half(plan, attn, 1, [attn_y, cross_y], attn_states, near_done)
     return (
         activations,
         input_grad,

time: 88.8 us -> 87.9 us (0.990)
  waiting for transfers between devices: 26.1 us -> 24.7 us
    pallas_call x0 -> x2, Pallas kernels: none -> 2.93 us  [adam_half(): pl.pallas_call(functools.partial(adam_half_kernel, stream, rel), out_shap...]
    pallas_call x2 -> x1, Pallas kernels: 6.65 us -> 4.38 us  [adam_matrix(): pl.pallas_call(functools.partial(adam_kernel, stream, rows), grid=(stream...]
    ppermute x18, waiting for transfers between devices: 3.5 us -> 2.21 us  [swap_core(): return lax.ppermute(value, 'dp', [(i, i ^ 1) for i in range(n_dp)])]
  transfers between devices with their start and end apart: 36 -> 36, of which waited for: 16 -> 15; matrix products, arithmetic and copies ran while one was open for 0% -> 0% of each run, Pallas kernels for 32% -> 33%
where the time goes in v4:
time: 87.9 us; the launch traced here: 87.7 us
  Pallas kernels  31.7 us (36%)
  starting transfers between devices  28.5 us (32%)
  waiting for transfers between devices  24.7 us (28%)
  local copies, waits for them, and re-layouts  1.69 us (2%)
  between operations  1.04 us (1%)
    pallas_call x18, Pallas kernels, call(): pl.pallas_call(kernel, out_shape=list(outs), in_specs=list(ins), out_spec...  24.4 us
    ppermute x9, waiting for transfers between devices, swap_dp(): return lax.ppermute(value, 'dp', [(i, i ^ mask) for i in range(plan.n_dp)])  14.3 us
    ppermute x9, starting transfers between devices, swap_dp(): return lax.ppermute(value, 'dp', [(i, i ^ mask) for i in range(plan.n_dp)])  12.4 us
    ppermute x6, starting transfers between devices, send_plane(): got.append(lax.ppermute(parts[number], ('dp', 'opt'), perm))  7.17 us
    ppermute x6, waiting for transfers between devices, send_plane(): got.append(lax.ppermute(parts[number], ('dp', 'opt'), perm))  5.79 us
    ppermute x3, starting transfers between devices, spread(): lax.ppermute(send, 'opt', [(o, o ^ m) for o in range(n_opt)])  5.75 us
    pallas_call x1, Pallas kernels, adam_matrix(): pl.pallas_call(functools.partial(adam_kernel, stream, rows), grid=(stream...  4.38 us
    ppermute x18, starting transfers between devices, swap_core(): return lax.ppermute(value, 'dp', [(i, i ^ 1) for i in range(n_dp)])  3.2 us
  transfers between devices with their start and end apart: 36, of which 15 were waited for; matrix products, arithmetic and copies ran while one was open for 0% of the time, Pallas kernels for 33%

profile of v4, /device:TPU:0, one launch (start us, length us, event | category | flops | bytes accessed | tf_op | source)
XLA Modules:
  0.0 87.7 jit_solution(11046999652784311603)
XLA Ops:
  0.6 0.0 copy-start
  0.7 1.1 %first_message.1.refs_3_ = bf16[208,384]{1,0:T(8,128)(2,1)S(1)} custom-call(f32[192,1536]{1,0:T(8,128)} %refs_0_.5, f32[2304]{0:T(1024)} %w_ref.3), custom_call_target="tpu_custom_call" | custom-call | tf_op jit(solution)/shard_map/first_message/pallas_call | solution.py:80
  1.8 3.0 %collective-permute-start = (bf16[208,384]{1,0:T(8,128)(2,1)S(1)}, bf16[208,384]{1,0:T(8,128)(2,1)S(1)}, u32[]{:S(2)}, u32[]{:S(2)}) collective-permute-start(bf16[208,384]{1,0:T(8,128)(2,1)S(1)} %first_message.1.refs_3_), channel_id=1, source_target_pairs={{0,1},{1,0},{2,3},{3,2},{4,5},{5,4},{6,7},{7,6},{8,9},{9,8},{10,11... | collective-permute-start | bytes 479240 | tf_op jit(solution)/shard_map/ppermute | solution.py:622
  4.8 1.7 %copy-done.1 = f32[192,3072]{1,0:T(8,128)S(1)} copy-done((f32[192,3072]{1,0:T(8,128)S(1)}, f32[192,3072]{1,0:T(8,128)}, u32[]{:S(2)}) %copy-start.1) | copy-done | bytes 2359320
  6.4 0.2 cast_weights.1
  6.7 0.3 collective-permute-start.4
  6.9 2.4 %collective-permute-done.refs_4_ = bf16[208,384]{1,0:T(8,128)(2,1)S(1)} collective-permute-done((bf16[208,384]{1,0:T(8,128)(2,1)S(1)}, bf16[208,384]{1,0:T(8,128)(2,1)S(1)}, u32[]{:S(2)}, u32[]{:S(2)}) %collective-permute-start) | collective-permute-done | bytes 159776 | tf_op jit(solution)/shard_map/ppermute | solution.py:622
  9.3 1.5 %collective-permute-start.2 = (bf16[208,384]{1,0:T(8,128)(2,1)S(1)}, bf16[208,384]{1,0:T(8,128)(2,1)S(1)}, u32[]{:S(2)}, u32[]{:S(2)}) collective-permute-start(bf16[208,384]{1,0:T(8,128)(2,1)S(1)} %collective-permute-done.refs_4_), channel_id=1, source_target_pairs={{0,4},{2,6},{4,0},{6,2},{8,12},{10,14},{12,8},{14,10},{16,20},{18,... | collective-permute-start | bytes 479240 | tf_op jit(solution)/shard_map/ppermute | solution.py:481
  10.8 0.0 collective-permute-start.1
  10.8 3.7 %collective-permute-done.2.refs_6_ = bf16[208,384]{1,0:T(8,128)(2,1)S(1)} collective-permute-done((bf16[208,384]{1,0:T(8,128)(2,1)S(1)}, bf16[208,384]{1,0:T(8,128)(2,1)S(1)}, u32[]{:S(2)}, u32[]{:S(2)}) %collective-permute-start.2) | collective-permute-done | bytes 159776 | tf_op jit(solution)/shard_map/ppermute | solution.py:481
  14.6 0.0 collective-permute-start.3
  14.6 1.4 %collective-permute-done.3.refs_7_ = bf16[208,384]{1,0:T(8,128)(2,1)S(1)} collective-permute-done((bf16[208,384]{1,0:T(8,128)(2,1)S(1)}, bf16[208,384]{1,0:T(8,128)(2,1)S(1)}, u32[]{:S(2)}, u32[]{:S(2)}) %collective-permute-start.3) | collective-permute-done | bytes 159776 | tf_op jit(solution)/shard_map/ppermute | solution.py:477
  16.0 2.4 %attn_enter.1 = (bf16[2,2,192,768]{3,2,1,0:T(8,128)(2,1)S(1)}, bf16[3,384,512]{2,1,0:T(8,128)(2,1)S(1)}, bf16[128,512]{1,0:T(8,128)(2,1)S(1)}, f32[2,1,512]{2,1,...) custom-call(bf16[512,384]{1,0:T(8,128)(2,1)S(1)} %copy-done.2, ...), custom_call_target="tpu_custom_call" | custom-call | tf_op jit(solution)/shard_map/attn_enter/pallas_call | solution.py:80
  18.4 0.2 collective-permute-start.5
  18.6 2.5 %collective-permute-start.6 = (bf16[192,384]{1,0:T(8,128)(2,1)S(1)}, bf16[192,384]{1,0:T(8,128)(2,1)S(1)}, u32[]{:S(2)}, u32[]{:S(2)}) collective-permute-start(bf16[192,384]{1,0:T(8,128)(2,1)S(1)} %get-tuple-element.107), channel_id=1, source_target_pairs={{0,1},{1,0},{2,3},{3,2},{4,5},{5,4},{6,7},{7,6},{8,9},{9,8},{10,11... | collective-permute-start | bytes 442376 | tf_op jit(solution)/shard_map/ppermute | solution.py:622
  21.1 2.8 %attn_leave.1 = (bf16[384,512]{1,0:T(8,128)(2,1)S(1)}, f32[6,1,512]{2,1,0:T(1,128)S(1)}, f32[512,384]{1,0:T(8,128)S(1)}) custom-call(bf16[512,384]{1,0:T(8,128)(2,1)S(1)} %copy-done.2, bf16[2,2,192,768]{3,2,1,0:T(8,128)(2,1)S(1)} %get-tuple-element.96.full_ref.refs_2_, bf16[3,384,512]{2,1,0:T(8,128)(2,1)S(1)} %get-tuple-element.97.qkv_ref, ...), custom_call_target="tpu_custom_call" | custom-call | tf_op jit(solution)/shard_map/attn_leave/pallas_call | solution.py:80
  24.0 3.4 %mlp_far.1 = (f32[48,16,384]{2,1,0:T(8,128)S(1)}, bf16[24,16,384]{2,1,0:T(8,128)(2,1)S(1)}, bf16[24,16,384]{2,1,0:T(8,128)(2,1)S(1)}, f32[1,768]{1,0:T(1,128)S(1...) custom-call(f32[512,384]{1,0:T(8,128)S(1)} %get-tuple-element.102.refs_0_, bf16[512,384]{1,0:T(8,128)(2,1)S(1)} %copy-done.3, ...), custom_call_target="tpu_custom_call" | custom-call | tf_op jit(solution)/shard_map/mlp_far/pallas_call | solution.py:80
  27.3 0.1 collective-permute-start.7
  27.5 0.4 collective-permute-start.8
  27.9 0.1 collective-permute-start.9
  28.0 0.8 collective-permute-done.7.refs_9_
  28.8 3.8 %mlp_near.1 = (f32[48,16,384]{2,1,0:T(8,128)S(1)}, bf16[24,16,384]{2,1,0:T(8,128)(2,1)S(1)}, bf16[24,16,384]{2,1,0:T(8,128)(2,1)S(1)}, f32[1,768]{1,0:T(1,128)S(...) custom-call(f32[512,384]{1,0:T(8,128)S(1)} %get-tuple-element.102.refs_0_, ...), custom_call_target="tpu_custom_call" | custom-call | flops 1811939328 | bytes 8096768 | tf_op jit(solution)/shard_map/mlp_near/pallas_call | solution.py:80
  32.6 0.2 collective-permute-start.10
  32.8 0.4 collective-permute-start.11
  33.2 0.1 add_core_mlp.2
  33.3 1.6 %collective-permute-start.14 = (bf16[24,16,384]{2,1,0:T(8,128)(2,1)S(1)}, bf16[24,16,384]{2,1,0:T(8,128)(2,1)S(1)}, u32[]{:S(2)}, u32[]{:S(2)}) collective-permute-start(bf16[24,16,384]{2,1,0:T(8,128)(2,1)S(1)} %get-tuple-element.117), channel_id=1, source_target_pairs={{0,4},{1,5},{2,6},{3,7},{4,0},{5,1},{6,2},{7,3},{8,12},{9,13},{10,... | collective-permute-start | bytes 884744 | tf_op jit(solution)/shard_map/ppermute | solution.py:504
  34.9 2.4 %attn_back_first.1 = (bf16[384,512]{1,0:T(8,128)(2,1)S(1)}, f32[384,384]{1,0:T(8,128)S(1)}, f32[8,384]{1,0:T(8,128)S(1)}, bf16[3,128,512]{2,1,0:T(8,128)(2,1)S(1...) custom-call(f32[512,512]{1,0:T(8,128)S(1)} %get-tuple-element.100.bias_ref, ...), custom_call_target="tpu_custom_call" | custom-call | tf_op jit(solution)/shard_map/attn_back_first/pallas_call | solution.py:80
  37.4 0.1 add_core_mlp.3
  37.5 2.0 %collective-permute-start.13 = (bf16[24,16,384]{2,1,0:T(8,128)(2,1)S(1)}, bf16[24,16,384]{2,1,0:T(8,128)(2,1)S(1)}, u32[]{:S(2)}, u32[]{:S(2)}) collective-permute-start(bf16[24,16,384]{2,1,0:T(8,128)(2,1)S(1)} %get-tuple-element.134), channel_id=1, source_target_pairs={{0,1},{1,0},{2,3},{3,2},{4,5},{5,4},{6,7},{7,6},{8,9},{9,8},{10,11... | collective-permute-start | bytes 884744 | tf_op jit(solution)/shard_map/ppermute | solution.py:504
  39.5 3.8 %attn_back_next.1 = (bf16[3,256,512]{2,1,0:T(8,128)(2,1)S(1)}, f32[192,3072]{1,0:T(8,128)S(1)}, f32[192,3072]{1,0:T(8,128)S(1)}, f32[192,3072]{1,0:T(8,128)S(1)}) custom-call(f32[512,512]{1,0:T(8,128)S(1)} %get-tuple-element.100.bias_ref, bf16[384,512]{1,0:T(8,128)(2,1)S(1)} %get-tuple-element.135.dmix_ref, ...), custom_call_target="tpu_custom_call" | custom-call | tf_op jit(solution)/shard_map/attn_back_next/pallas_call | solution.py:80
  43.3 3.1 %attn_back_last.1 = (f32[49,16,384]{2,1,0:T(8,128)S(1)}, bf16[12,16,384]{2,1,0:T(8,128)(2,1)S(1)}, bf16[12,16,384]{2,1,0:T(8,128)(2,1)S(1)}, bf16[12,16,384]{2,1...) custom-call(bf16[512,384]{1,0:T(8,128)(2,1)S(1)} %copy-done.2, ...), custom_call_target="tpu_custom_call" | custom-call | tf_op jit(solution)/shard_map/attn_back_last/pallas_call | solution.py:80
  46.4 0.5 collective-permute-start.12
  46.9 1.8 %collective-permute-done.14.refs_1_ = bf16[24,16,384]{2,1,0:T(8,128)(2,1)S(1)} collective-permute-done((bf16[24,16,384]{2,1,0:T(8,128)(2,1)S(1)}, bf16[24,16,384]{2,1,0:T(8,128)(2,1)S(1)}, u32[]{:S(2)}, u32[]{:S(2)}) %collective-permute-start.14) | collective-permute-done | bytes 294944 | tf_op jit(solution)/shard_map/ppermute | solution.py:504
  48.7 0.5 collective-permute-start.17
  49.2 0.7 collective-permute-done.13.refs_0_
  50.0 0.1 add_plane_mlp.1
  50.1 1.6 %collective-permute-start.20 = (bf16[12,16,384]{2,1,0:T(8,128)(2,1)S(1)}, bf16[12,16,384]{2,1,0:T(8,128)(2,1)S(1)}, u32[]{:S(2)}, u32[]{:S(2)}) collective-permute-start(bf16[12,16,384]{2,1,0:T(8,128)(2,1)S(1)} %get-tuple-element.140), channel_id=1, source_target_pairs={{0,8},{2,10},{4,12},{6,14},{8,0},{10,2},{12,4},{14,6},{16,24},{18,... | collective-permute-start | bytes 442376 | tf_op jit(solution)/shard_map/ppermute | solution.py:481
  51.8 0.1 add_core_attn.1
  51.9 0.4 collective-permute-start.19
  52.3 1.4 %collective-permute-start.21 = (bf16[13,16,384]{2,1,0:T(8,128)(2,1)S(1)}, bf16[13,16,384]{2,1,0:T(8,128)(2,1)S(1)}, u32[]{:S(2)}, u32[]{:S(2)}) collective-permute-start(bf16[13,16,384]{2,1,0:T(8,128)(2,1)S(1)} %get-tuple-element.150), channel_id=1, source_target_pairs={{0,4},{1,5},{2,6},{3,7},{4,0},{5,1},{6,2},{7,3},{8,12},{9,13},{10,... | collective-permute-start | bytes 479240 | tf_op jit(solution)/shard_map/ppermute | solution.py:504
  53.7 1.8 %collective-permute-start.22 = (bf16[13,16,384]{2,1,0:T(8,128)(2,1)S(1)}, bf16[13,16,384]{2,1,0:T(8,128)(2,1)S(1)}, u32[]{:S(2)}, u32[]{:S(2)}) collective-permute-start(bf16[13,16,384]{2,1,0:T(8,128)(2,1)S(1)} %get-tuple-element.151), channel_id=1, source_target_pairs={{0,5},{1,4},{2,7},{3,6},{4,1},{5,0},{6,3},{7,2},{8,13},{9,12},{10,... | collective-permute-start | bytes 479240 | tf_op jit(solution)/shard_map/ppermute | solution.py:504
  55.5 2.7 %collective-permute-start.24 = (bf16[12,16,384]{2,1,0:T(8,128)(2,1)S(1)}, bf16[12,16,384]{2,1,0:T(8,128)(2,1)S(1)}, u32[]{:S(2)}, u32[]{:S(2)}) collective-permute-start(bf16[12,16,384]{2,1,0:T(8,128)(2,1)S(1)} %add_two_mlp.2.left_ref), channel_id=1, source_target_pairs={{0,16},{2,18},{4,20},{6,22},{8,24},{10,26},{12,28},{14,30},{16,0},... | collective-permute-start | bytes 442376 | tf_op jit(solution)/shard_map/ppermute | solution.py:481
  58.2 0.5 collective-permute-done.19.refs_0_
  58.7 0.5 collective-permute-done.21.refs_1_
  59.2 2.1 %collective-permute-done.22.refs_2_ = bf16[13,16,384]{2,1,0:T(8,128)(2,1)S(1)} collective-permute-done((bf16[13,16,384]{2,1,0:T(8,128)(2,1)S(1)}, bf16[13,16,384]{2,1,0:T(8,128)(2,1)S(1)}, u32[]{:S(2)}, u32[]{:S(2)}) %collective-permute-start.22) | collective-permute-done | bytes 159776 | tf_op jit(solution)/shard_map/ppermute | solution.py:504
  61.4 0.1 add_plane_attn.1.left_ref
  61.5 1.5 %collective-permute-start.23 = (bf16[13,16,384]{2,1,0:T(8,128)(2,1)S(1)}, bf16[13,16,384]{2,1,0:T(8,128)(2,1)S(1)}, u32[]{:S(2)}, u32[]{:S(2)}) collective-permute-start(bf16[13,16,384]{2,1,0:T(8,128)(2,1)S(1)} %add_plane_attn.1.left_ref), channel_id=1, source_target_pairs={{0,8},{2,10},{4,12},{6,14},{8,0},{10,2},{12,4},{14,6},{16,24},{18,... | collective-permute-start | bytes 479240 | tf_op jit(solution)/shard_map/ppermute | solution.py:481
  62.9 0.7 collective-permute-done.24.right_ref
  63.7 0.6 collective-permute-start.30
  64.3 4.3 %collective-permute-done.23.right_ref = bf16[13,16,384]{2,1,0:T(8,128)(2,1)S(1)} collective-permute-done((bf16[13,16,384]{2,1,0:T(8,128)(2,1)S(1)}, bf16[13,16,384]{2,1,0:T(8,128)(2,1)S(1)}, u32[]{:S(2)}, u32[]{:S(2)}) %collective-permute-start.23) | collective-permute-done | bytes 159776 | tf_op jit(solution)/shard_map/ppermute | solution.py:481
  68.6 2.2 %collective-permute-start.25 = (bf16[13,16,384]{2,1,0:T(8,128)(2,1)S(1)}, bf16[13,16,384]{2,1,0:T(8,128)(2,1)S(1)}, u32[]{:S(2)}, u32[]{:S(2)}) collective-permute-start(bf16[13,16,384]{2,1,0:T(8,128)(2,1)S(1)} %add_two_attn.1.left_ref), channel_id=1, source_target_pairs={{0,16},{2,18},{4,20},{6,22},{8,24},{10,26},{12,28},{14,30},{16,0},... | collective-permute-start | bytes 479240 | tf_op jit(solution)/shard_map/ppermute | solution.py:481
  70.8 0.6 collective-permute-start.28
  71.4 0.4 collective-permute-done.30.refs_4_
  71.8 1.0 %collective-permute-start.32 = (bf16[12,16,384]{2,1,0:T(8,128)(2,1)S(1)}, bf16[12,16,384]{2,1,0:T(8,128)(2,1)S(1)}, u32[]{:S(2)}, u32[]{:S(2)}) collective-permute-start(bf16[12,16,384]{2,1,0:T(8,128)(2,1)S(1)} %collective-permute-done.30.refs_4_), channel_id=1, source_target_pairs={{0,4},{2,6},{4,0},{6,2},{8,12},{10,14},{12,8},{14,10},{16,20},{18,... | collective-permute-start | bytes 442376 | tf_op jit(solution)/shard_map/ppermute | solution.py:481
  72.9 0.5 collective-permute-start.31
  73.4 2.6 %collective-permute-done.28.refs_2_ = bf16[12,16,384]{2,1,0:T(8,128)(2,1)S(1)} collective-permute-done((bf16[12,16,384]{2,1,0:T(8,128)(2,1)S(1)}, bf16[12,16,384]{2,1,0:T(8,128)(2,1)S(1)}, u32[]{:S(2)}, u32[]{:S(2)}) %collective-permute-start.28) | collective-permute-done | bytes 147488 | tf_op jit(solution)/shard_map/ppermute | solution.py:481
  76.0 1.6 %collective-permute-done.32.refs_6_ = bf16[12,16,384]{2,1,0:T(8,128)(2,1)S(1)} collective-permute-done((bf16[12,16,384]{2,1,0:T(8,128)(2,1)S(1)}, bf16[12,16,384]{2,1,0:T(8,128)(2,1)S(1)}, u32[]{:S(2)}, u32[]{:S(2)}) %collective-permute-start.32) | collective-permute-done | bytes 147488 | tf_op jit(solution)/shard_map/ppermute | solution.py:481
  77.6 0.7 add_last.1
  78.3 0.6 collective-permute-start.26
  78.9 0.2 collective-permute-start.35
  79.1 4.4 %adam_mlp.1 = (f32[192,3072]{1,0:T(8,128)}, f32[192,3072]{1,0:T(8,128)}, f32[192,3072]{1,0:T(8,128)}) custom-call(bf16[12,16,384]{2,1,0:T(8,128)(2,1)S(1)} %add_two_mlp.3.refs_0_, bf16[12,16,384]{2,1,0:T(8,128)(2,1)S(1)} %collective-permute-done.27.refs_1_, bf16[12,16,384]{2,1,0:T(8,128)(2,1)S(1)} %collective-permute-done.28.refs_2_, ...), custom_call_target="tpu_custom_call" | custom-call | flops 9437184 | bytes 14155776 | tf_op jit(solution)/shard_map/adam_mlp/pallas_call | solution.py:569
  83.5 1.0 %collective-permute-done.26.refs_0_ = bf16[12,16,384]{2,1,0:T(8,128)(2,1)S(1)} collective-permute-done((bf16[12,16,384]{2,1,0:T(8,128)(2,1)S(1)}, bf16[12,16,384]{2,1,0:T(8,128)(2,1)S(1)}, u32[]{:S(2)}, u32[]{:S(2)}) %collective-permute-start.26) | collective-permute-done | bytes 147488 | tf_op jit(solution)/shard_map/ppermute | solution.py:481
  84.5 1.5 %adam_half_0.1 = (f32[192,1536]{1,0:T(8,128)}, f32[192,1536]{1,0:T(8,128)}, f32[192,1536]{1,0:T(8,128)}) custom-call(bf16[12,16,384]{2,1,0:T(8,128)(2,1)S(1)} %get-tuple-element.161.refs_0_, bf16[12,16,384]{2,1,0:T(8,128)(2,1)S(1)} %collective-permute-done.35.refs_1_, f32[192,1536]{1,0:T(8,128)S(1)} %get-tuple-element.162.refs_2_, ...), custom_call_target="tpu_custom_call" | custom-call | tf_op jit(solution)/shard_map/adam_half_0/pallas_call | solution.py:604
  86.0 1.5 %adam_half_1.1 = (f32[192,1536]{1,0:T(8,128)}, f32[192,1536]{1,0:T(8,128)}, f32[192,1536]{1,0:T(8,128)}) custom-call(bf16[12,16,384]{2,1,0:T(8,128)(2,1)S(1)} %collective-permute-done.26.refs_0_, bf16[12,16,384]{2,1,0:T(8,128)(2,1)S(1)} %collective-permute-done.34.refs_1_, ...), custom_call_target="tpu_custom_call", output_to_operand_aliasing={{0}: (5, {}), {1}: (6, {}), {2}: (7, {})} | custom-call | tf_op jit(solution)/shard_map/adam_half_1/pallas_call | solution.py:604
  (45 shorter events, 0.2 us)
Async XLA Ops:
  0.6 4.1 %copy-start = (f32[192,1536]{1,0:T(8,128)S(1)}, f32[192,1536]{1,0:T(8,128)}, u32[]{:S(2)}) copy-start(f32[192,1536]{1,0:T(8,128)} %refs_0_.5) | copy-start | bytes 3538948
  1.8 7.5 %collective-permute-start = (bf16[208,384]{1,0:T(8,128)(2,1)S(1)}, bf16[208,384]{1,0:T(8,128)(2,1)S(1)}, u32[]{:S(2)}, u32[]{:S(2)}) collective-permute-start(bf16[208,384]{1,0:T(8,128)(2,1)S(1)} %first_message.1.refs_3_), channel_id=1, source_target_pairs={{0,1},{1,0},{2,3},{3,2},{4,5},{5,4},{6,7},{7,6},{8,9},{9,8},{10,11... | collective-permute-start | bytes 479240 | tf_op jit(solution)/shard_map/ppermute | solution.py:622
  4.8 1.7 %copy-start.1 = (f32[192,3072]{1,0:T(8,128)S(1)}, f32[192,3072]{1,0:T(8,128)}, u32[]{:S(2)}) copy-start(f32[192,3072]{1,0:T(8,128)} %refs_0_.6) | copy-start | bytes 7077892
  6.4 9.5 %copy-start.2 = (bf16[512,384]{1,0:T(8,128)(2,1)S(1)}, bf16[512,384]{1,0:T(8,128)(2,1)}, u32[]{:S(2)}) copy-start(bf16[512,384]{1,0:T(8,128)(2,1)} %refs_0_.7) | copy-start | bytes 1179652
  6.4 9.5 %copy-start.7 = (s32[512]{0:T(512)S(1)}, s32[512]{0:T(512)}, u32[]{:S(2)}) copy-start(s32[512]{0:T(512)} %param.13) | copy-start | bytes 6148
  6.7 11.7 %collective-permute-start.4 = (bf16[192,1152]{1,0:T(8,128)(2,1)S(1)}, bf16[192,1152]{1,0:T(8,128)(2,1)S(1)}, u32[]{:S(2)}, u32[]{:S(2)}) collective-permute-start(bf16[192,1152]{1,0:T(8,128)(2,1)S(1)} %get-tuple-element.105), channel_id=1, source_target_pairs={{0,1},{1,0},{2,3},{3,2},{4,5},{5,4},{6,7},{7,6},{8,9},{9,8},{10,11... | collective-permute-start | bytes 1327112 | tf_op jit(solution)/shard_map/ppermute | solution.py:622
  9.3 5.3 %collective-permute-start.2 = (bf16[208,384]{1,0:T(8,128)(2,1)S(1)}, bf16[208,384]{1,0:T(8,128)(2,1)S(1)}, u32[]{:S(2)}, u32[]{:S(2)}) collective-permute-start(bf16[208,384]{1,0:T(8,128)(2,1)S(1)} %collective-permute-done.refs_4_), channel_id=1, source_target_pairs={{0,4},{2,6},{4,0},{6,2},{8,12},{10,14},{12,8},{14,10},{16,20},{18,... | collective-permute-start | bytes 479240 | tf_op jit(solution)/shard_map/ppermute | solution.py:481
  10.8 3.7 %collective-permute-start.1 = (bf16[208,384]{1,0:T(8,128)(2,1)S(1)}, bf16[208,384]{1,0:T(8,128)(2,1)S(1)}, u32[]{:S(2)}, u32[]{:S(2)}) collective-permute-start(bf16[208,384]{1,0:T(8,128)(2,1)S(1)} %collective-permute-done.refs_4_), channel_id=1, source_target_pairs={{0,2},{2,0},{4,6},{6,4},{8,10},{10,8},{12,14},{14,12},{16,18},{18,... | collective-permute-start | bytes 479240 | tf_op jit(solution)/shard_map/ppermute | solution.py:477
  14.6 1.4 %collective-permute-start.3 = (bf16[208,384]{1,0:T(8,128)(2,1)S(1)}, bf16[208,384]{1,0:T(8,128)(2,1)S(1)}, u32[]{:S(2)}, u32[]{:S(2)}) collective-permute-start(bf16[208,384]{1,0:T(8,128)(2,1)S(1)} %collective-permute-done.2.refs_6_), channel_id=1, source_target_pairs={{0,2},{2,0},{4,6},{6,4},{8,10},{10,8},{12,14},{14,12},{16,18},{18,... | collective-permute-start | bytes 479240 | tf_op jit(solution)/shard_map/ppermute | solution.py:477
  18.4 5.5 %collective-permute-start.5 = (bf16[192,1152]{1,0:T(8,128)(2,1)S(1)}, bf16[192,1152]{1,0:T(8,128)(2,1)S(1)}, u32[]{:S(2)}, u32[]{:S(2)}) collective-permute-start(bf16[192,1152]{1,0:T(8,128)(2,1)S(1)} %collective-permute-done.4.refs_6_), channel_id=1, source_target_pairs={{0,2},{2,0},{4,6},{6,4},{8,10},{10,8},{12,14},{14,12},{16,18},{18,... | collective-permute-start | bytes 1327112 | tf_op jit(solution)/shard_map/ppermute | solution.py:477
  18.6 8.7 %collective-permute-start.6 = (bf16[192,384]{1,0:T(8,128)(2,1)S(1)}, bf16[192,384]{1,0:T(8,128)(2,1)S(1)}, u32[]{:S(2)}, u32[]{:S(2)}) collective-permute-start(bf16[192,384]{1,0:T(8,128)(2,1)S(1)} %get-tuple-element.107), channel_id=1, source_target_pairs={{0,1},{1,0},{2,3},{3,2},{4,5},{5,4},{6,7},{7,6},{8,9},{9,8},{10,11... | collective-permute-start | bytes 442376 | tf_op jit(solution)/shard_map/ppermute | solution.py:622
  21.1 2.8 %copy-start.3 = (bf16[512,384]{1,0:T(8,128)(2,1)S(1)}, bf16[512,384]{1,0:T(8,128)(2,1)}, u32[]{:S(2)}) copy-start(bf16[512,384]{1,0:T(8,128)(2,1)} %refs_1_.5) | copy-start | bytes 1179652
  27.3 1.4 %collective-permute-start.7 = (bf16[192,384]{1,0:T(8,128)(2,1)S(1)}, bf16[192,384]{1,0:T(8,128)(2,1)S(1)}, u32[]{:S(2)}, u32[]{:S(2)}) collective-permute-start(bf16[192,384]{1,0:T(8,128)(2,1)S(1)} %collective-permute-done.6.refs_8_), channel_id=1, source_target_pairs={{0,2},{2,0},{4,6},{6,4},{8,10},{10,8},{12,14},{14,12},{16,18},{18,... | collective-permute-start | bytes 442376 | tf_op jit(solution)/shard_map/ppermute | solution.py:477
  27.5 5.7 %collective-permute-start.8 = (bf16[24,16,384]{2,1,0:T(8,128)(2,1)S(1)}, bf16[24,16,384]{2,1,0:T(8,128)(2,1)S(1)}, u32[]{:S(2)}, u32[]{:S(2)}) collective-permute-start(bf16[24,16,384]{2,1,0:T(8,128)(2,1)S(1)} %get-tuple-element.114), channel_id=1, source_target_pairs={{0,2},{2,0},{4,6},{6,4},{8,10},{10,8},{12,14},{14,12},{16,18},{18,... | collective-permute-start | bytes 884744 | tf_op jit(solution)/shard_map/ppermute | solution.py:477
  27.9 5.2 %collective-permute-start.9 = (bf16[24,16,384]{2,1,0:T(8,128)(2,1)S(1)}, bf16[24,16,384]{2,1,0:T(8,128)(2,1)S(1)}, u32[]{:S(2)}, u32[]{:S(2)}) collective-permute-start(bf16[24,16,384]{2,1,0:T(8,128)(2,1)S(1)} %get-tuple-element.116), channel_id=1, source_target_pairs={{0,2},{2,0},{4,6},{6,4},{8,10},{10,8},{12,14},{14,12},{16,18},{18,... | collective-permute-start | bytes 884744 | tf_op jit(solution)/shard_map/ppermute | solution.py:477
  32.6 4.8 %collective-permute-start.10 = (bf16[24,16,384]{2,1,0:T(8,128)(2,1)S(1)}, bf16[24,16,384]{2,1,0:T(8,128)(2,1)S(1)}, u32[]{:S(2)}, u32[]{:S(2)}) collective-permute-start(bf16[24,16,384]{2,1,0:T(8,128)(2,1)S(1)} %get-tuple-element.130), channel_id=1, source_target_pairs={{0,2},{2,0},{4,6},{6,4},{8,10},{10,8},{12,14},{14,12},{16,18},{18,... | collective-permute-start | bytes 884744 | tf_op jit(solution)/shard_map/ppermute | solution.py:477
  32.8 4.6 %collective-permute-start.11 = (bf16[24,16,384]{2,1,0:T(8,128)(2,1)S(1)}, bf16[24,16,384]{2,1,0:T(8,128)(2,1)S(1)}, u32[]{:S(2)}, u32[]{:S(2)}) collective-permute-start(bf16[24,16,384]{2,1,0:T(8,128)(2,1)S(1)} %get-tuple-element.132), channel_id=1, source_target_pairs={{0,2},{2,0},{4,6},{6,4},{8,10},{10,8},{12,14},{14,12},{16,18},{18,... | collective-permute-start | bytes 884744 | tf_op jit(solution)/shard_map/ppermute | solution.py:477
  33.3 15.4 %collective-permute-start.14 = (bf16[24,16,384]{2,1,0:T(8,128)(2,1)S(1)}, bf16[24,16,384]{2,1,0:T(8,128)(2,1)S(1)}, u32[]{:S(2)}, u32[]{:S(2)}) collective-permute-start(bf16[24,16,384]{2,1,0:T(8,128)(2,1)S(1)} %get-tuple-element.117), channel_id=1, source_target_pairs={{0,4},{1,5},{2,6},{3,7},{4,0},{5,1},{6,2},{7,3},{8,12},{9,13},{10,... | collective-permute-start | bytes 884744 | tf_op jit(solution)/shard_map/ppermute | solution.py:504
  34.9 13.8 %collective-permute-start.15 = (bf16[24,16,384]{2,1,0:T(8,128)(2,1)S(1)}, bf16[24,16,384]{2,1,0:T(8,128)(2,1)S(1)}, u32[]{:S(2)}, u32[]{:S(2)}) collective-permute-start(bf16[24,16,384]{2,1,0:T(8,128)(2,1)S(1)} %get-tuple-element.118), channel_id=1, source_target_pairs={{0,5},{1,4},{2,7},{3,6},{4,1},{5,0},{6,3},{7,2},{8,13},{9,12},{10,... | collective-permute-start | bytes 884744 | tf_op jit(solution)/shard_map/ppermute | solution.py:504
  37.5 12.5 %collective-permute-start.13 = (bf16[24,16,384]{2,1,0:T(8,128)(2,1)S(1)}, bf16[24,16,384]{2,1,0:T(8,128)(2,1)S(1)}, u32[]{:S(2)}, u32[]{:S(2)}) collective-permute-start(bf16[24,16,384]{2,1,0:T(8,128)(2,1)S(1)} %get-tuple-element.134), channel_id=1, source_target_pairs={{0,1},{1,0},{2,3},{3,2},{4,5},{5,4},{6,7},{7,6},{8,9},{9,8},{10,11... | collective-permute-start | bytes 884744 | tf_op jit(solution)/shard_map/ppermute | solution.py:504
  46.4 5.4 %collective-permute-start.18 = (bf16[13,16,384]{2,1,0:T(8,128)(2,1)S(1)}, bf16[13,16,384]{2,1,0:T(8,128)(2,1)S(1)}, u32[]{:S(2)}, u32[]{:S(2)}) collective-permute-start(bf16[13,16,384]{2,1,0:T(8,128)(2,1)S(1)} %get-tuple-element.144), channel_id=1, source_target_pairs={{0,2},{2,0},{4,6},{6,4},{8,10},{10,8},{12,14},{14,12},{16,18},{18,... | collective-permute-start | bytes 479240 | tf_op jit(solution)/shard_map/ppermute | solution.py:477
  46.4 5.4 %collective-permute-start.12 = (bf16[12,16,384]{2,1,0:T(8,128)(2,1)S(1)}, bf16[12,16,384]{2,1,0:T(8,128)(2,1)S(1)}, u32[]{:S(2)}, u32[]{:S(2)}) collective-permute-start(bf16[12,16,384]{2,1,0:T(8,128)(2,1)S(1)} %get-tuple-element.139), channel_id=1, source_target_pairs={{0,2},{2,0},{4,6},{6,4},{8,10},{10,8},{12,14},{14,12},{16,18},{18,... | collective-permute-start | bytes 442376 | tf_op jit(solution)/shard_map/ppermute | solution.py:477
  48.7 3.0 %collective-permute-start.16 = (bf16[12,16,384]{2,1,0:T(8,128)(2,1)S(1)}, bf16[12,16,384]{2,1,0:T(8,128)(2,1)S(1)}, u32[]{:S(2)}, u32[]{:S(2)}) collective-permute-start(bf16[12,16,384]{2,1,0:T(8,128)(2,1)S(1)} %get-tuple-element.142), channel_id=1, source_target_pairs={{0,2},{2,0},{4,6},{6,4},{8,10},{10,8},{12,14},{14,12},{16,18},{18,... | collective-permute-start | bytes 442376 | tf_op jit(solution)/shard_map/ppermute | solution.py:477
  48.7 3.0 %collective-permute-start.17 = (bf16[12,16,384]{2,1,0:T(8,128)(2,1)S(1)}, bf16[12,16,384]{2,1,0:T(8,128)(2,1)S(1)}, u32[]{:S(2)}, u32[]{:S(2)}) collective-permute-start(bf16[12,16,384]{2,1,0:T(8,128)(2,1)S(1)} %get-tuple-element.143), channel_id=1, source_target_pairs={{0,2},{2,0},{4,6},{6,4},{8,10},{10,8},{12,14},{14,12},{16,18},{18,... | collective-permute-start | bytes 442376 | tf_op jit(solution)/shard_map/ppermute | solution.py:477
  50.1 5.3 %collective-permute-start.20 = (bf16[12,16,384]{2,1,0:T(8,128)(2,1)S(1)}, bf16[12,16,384]{2,1,0:T(8,128)(2,1)S(1)}, u32[]{:S(2)}, u32[]{:S(2)}) collective-permute-start(bf16[12,16,384]{2,1,0:T(8,128)(2,1)S(1)} %get-tuple-element.140), channel_id=1, source_target_pairs={{0,8},{2,10},{4,12},{6,14},{8,0},{10,2},{12,4},{14,6},{16,24},{18,... | collective-permute-start | bytes 442376 | tf_op jit(solution)/shard_map/ppermute | solution.py:481
  51.9 6.8 %collective-permute-start.19 = (bf16[13,16,384]{2,1,0:T(8,128)(2,1)S(1)}, bf16[13,16,384]{2,1,0:T(8,128)(2,1)S(1)}, u32[]{:S(2)}, u32[]{:S(2)}) collective-permute-start(bf16[13,16,384]{2,1,0:T(8,128)(2,1)S(1)} %get-tuple-element.146), channel_id=1, source_target_pairs={{0,1},{1,0},{2,3},{3,2},{4,5},{5,4},{6,7},{7,6},{8,9},{9,8},{10,11... | collective-permute-start | bytes 479240 | tf_op jit(solution)/shard_map/ppermute | solution.py:504
  52.3 6.9 %collective-permute-start.21 = (bf16[13,16,384]{2,1,0:T(8,128)(2,1)S(1)}, bf16[13,16,384]{2,1,0:T(8,128)(2,1)S(1)}, u32[]{:S(2)}, u32[]{:S(2)}) collective-permute-start(bf16[13,16,384]{2,1,0:T(8,128)(2,1)S(1)} %get-tuple-element.150), channel_id=1, source_target_pairs={{0,4},{1,5},{2,6},{3,7},{4,0},{5,1},{6,2},{7,3},{8,12},{9,13},{10,... | collective-permute-start | bytes 479240 | tf_op jit(solution)/shard_map/ppermute | solution.py:504
  53.7 7.7 %collective-permute-start.22 = (bf16[13,16,384]{2,1,0:T(8,128)(2,1)S(1)}, bf16[13,16,384]{2,1,0:T(8,128)(2,1)S(1)}, u32[]{:S(2)}, u32[]{:S(2)}) collective-permute-start(bf16[13,16,384]{2,1,0:T(8,128)(2,1)S(1)} %get-tuple-element.151), channel_id=1, source_target_pairs={{0,5},{1,4},{2,7},{3,6},{4,1},{5,0},{6,3},{7,2},{8,13},{9,12},{10,... | collective-permute-start | bytes 479240 | tf_op jit(solution)/shard_map/ppermute | solution.py:504
  55.4 22.1 %copy-start.4 = (f32[2304]{0:T(1024)S(1)}, f32[2304]{0:T(1024)}, u32[]{:S(2)}) copy-start(f32[2304]{0:T(1024)} %w_ref.3) | copy-start | bytes 27652
  55.4 22.1 %copy-start.5 = (f32[2304]{0:T(1024)S(1)}, f32[2304]{0:T(1024)}, u32[]{:S(2)}) copy-start(f32[2304]{0:T(1024)} %m_ref.1) | copy-start | bytes 27652
  55.4 22.1 %copy-start.6 = (f32[2304]{0:T(1024)S(1)}, f32[2304]{0:T(1024)}, u32[]{:S(2)}) copy-start(f32[2304]{0:T(1024)} %v_ref.1) | copy-start | bytes 27652
  55.5 8.1 %collective-permute-start.24 = (bf16[12,16,384]{2,1,0:T(8,128)(2,1)S(1)}, bf16[12,16,384]{2,1,0:T(8,128)(2,1)S(1)}, u32[]{:S(2)}, u32[]{:S(2)}) collective-permute-start(bf16[12,16,384]{2,1,0:T(8,128)(2,1)S(1)} %add_two_mlp.2.left_ref), channel_id=1, source_target_pairs={{0,16},{2,18},{4,20},{6,22},{8,24},{10,26},{12,28},{14,30},{16,0},... | collective-permute-start | bytes 442376 | tf_op jit(solution)/shard_map/ppermute | solution.py:481
  61.5 7.1 %collective-permute-start.23 = (bf16[13,16,384]{2,1,0:T(8,128)(2,1)S(1)}, bf16[13,16,384]{2,1,0:T(8,128)(2,1)S(1)}, u32[]{:S(2)}, u32[]{:S(2)}) collective-permute-start(bf16[13,16,384]{2,1,0:T(8,128)(2,1)S(1)} %add_plane_attn.1.left_ref), channel_id=1, source_target_pairs={{0,8},{2,10},{4,12},{6,14},{8,0},{10,2},{12,4},{14,6},{16,24},{18,... | collective-permute-start | bytes 479240 | tf_op jit(solution)/shard_map/ppermute | solution.py:481
  63.7 8.2 %collective-permute-start.30 = (bf16[12,16,384]{2,1,0:T(8,128)(2,1)S(1)}, bf16[12,16,384]{2,1,0:T(8,128)(2,1)S(1)}, u32[]{:S(2)}, u32[]{:S(2)}) collective-permute-start(bf16[12,16,384]{2,1,0:T(8,128)(2,1)S(1)} %add_two_mlp.3.refs_0_), channel_id=1, source_target_pairs={{0,8},{2,10},{4,12},{6,14},{8,0},{10,2},{12,4},{14,6},{16,24},{18,... | collective-permute-start | bytes 442376 | tf_op jit(solution)/shard_map/ppermute | solution.py:481
  68.6 9.0 %collective-permute-start.25 = (bf16[13,16,384]{2,1,0:T(8,128)(2,1)S(1)}, bf16[13,16,384]{2,1,0:T(8,128)(2,1)S(1)}, u32[]{:S(2)}, u32[]{:S(2)}) collective-permute-start(bf16[13,16,384]{2,1,0:T(8,128)(2,1)S(1)} %add_two_attn.1.left_ref), channel_id=1, source_target_pairs={{0,16},{2,18},{4,20},{6,22},{8,24},{10,26},{12,28},{14,30},{16,0},... | collective-permute-start | bytes 479240 | tf_op jit(solution)/shard_map/ppermute | solution.py:481
  70.8 5.1 %collective-permute-start.28 = (bf16[12,16,384]{2,1,0:T(8,128)(2,1)S(1)}, bf16[12,16,384]{2,1,0:T(8,128)(2,1)S(1)}, u32[]{:S(2)}, u32[]{:S(2)}) collective-permute-start(bf16[12,16,384]{2,1,0:T(8,128)(2,1)S(1)} %add_two_mlp.3.refs_0_), channel_id=1, source_target_pairs={{0,4},{2,6},{4,0},{6,2},{8,12},{10,14},{12,8},{14,10},{16,20},{18,... | collective-permute-start | bytes 442376 | tf_op jit(solution)/shard_map/ppermute | solution.py:481
  71.8 5.7 %collective-permute-start.32 = (bf16[12,16,384]{2,1,0:T(8,128)(2,1)S(1)}, bf16[12,16,384]{2,1,0:T(8,128)(2,1)S(1)}, u32[]{:S(2)}, u32[]{:S(2)}) collective-permute-start(bf16[12,16,384]{2,1,0:T(8,128)(2,1)S(1)} %collective-permute-done.30.refs_4_), channel_id=1, source_target_pairs={{0,4},{2,6},{4,0},{6,2},{8,12},{10,14},{12,8},{14,10},{16,20},{18,... | collective-permute-start | bytes 442376 | tf_op jit(solution)/shard_map/ppermute | solution.py:481
  72.9 6.0 %collective-permute-start.27 = (bf16[12,16,384]{2,1,0:T(8,128)(2,1)S(1)}, bf16[12,16,384]{2,1,0:T(8,128)(2,1)S(1)}, u32[]{:S(2)}, u32[]{:S(2)}) collective-permute-start(bf16[12,16,384]{2,1,0:T(8,128)(2,1)S(1)} %add_two_mlp.3.refs_0_), channel_id=1, source_target_pairs={{0,2},{2,0},{4,6},{6,4},{8,10},{10,8},{12,14},{14,12},{16,18},{18,... | collective-permute-start | bytes 442376 | tf_op jit(solution)/shard_map/ppermute | solution.py:477
  72.9 6.3 %collective-permute-start.31 = (bf16[12,16,384]{2,1,0:T(8,128)(2,1)S(1)}, bf16[12,16,384]{2,1,0:T(8,128)(2,1)S(1)}, u32[]{:S(2)}, u32[]{:S(2)}) collective-permute-start(bf16[12,16,384]{2,1,0:T(8,128)(2,1)S(1)} %collective-permute-done.30.refs_4_), channel_id=1, source_target_pairs={{0,2},{2,0},{4,6},{6,4},{8,10},{10,8},{12,14},{14,12},{16,18},{18,... | collective-permute-start | bytes 442376 | tf_op jit(solution)/shard_map/ppermute | solution.py:477
  76.0 3.2 %collective-permute-start.29 = (bf16[12,16,384]{2,1,0:T(8,128)(2,1)S(1)}, bf16[12,16,384]{2,1,0:T(8,128)(2,1)S(1)}, u32[]{:S(2)}, u32[]{:S(2)}) collective-permute-start(bf16[12,16,384]{2,1,0:T(8,128)(2,1)S(1)} %collective-permute-done.28.refs_2_), channel_id=1, source_target_pairs={{0,2},{2,0},{4,6},{6,4},{8,10},{10,8},{12,14},{14,12},{16,18},{18,... | collective-permute-start | bytes 442376 | tf_op jit(solution)/shard_map/ppermute | solution.py:477
  77.6 1.6 %collective-permute-start.33 = (bf16[12,16,384]{2,1,0:T(8,128)(2,1)S(1)}, bf16[12,16,384]{2,1,0:T(8,128)(2,1)S(1)}, u32[]{:S(2)}, u32[]{:S(2)}) collective-permute-start(bf16[12,16,384]{2,1,0:T(8,128)(2,1)S(1)} %collective-permute-done.32.refs_6_), channel_id=1, source_target_pairs={{0,2},{2,0},{4,6},{6,4},{8,10},{10,8},{12,14},{14,12},{16,18},{18,... | collective-permute-start | bytes 442376 | tf_op jit(solution)/shard_map/ppermute | solution.py:477
  78.3 6.3 %collective-permute-start.26 = (bf16[12,16,384]{2,1,0:T(8,128)(2,1)S(1)}, bf16[12,16,384]{2,1,0:T(8,128)(2,1)S(1)}, u32[]{:S(2)}, u32[]{:S(2)}) collective-permute-start(bf16[12,16,384]{2,1,0:T(8,128)(2,1)S(1)} %get-tuple-element.161.refs_0_), channel_id=1, source_target_pairs={{0,4},{2,6},{4,0},{6,2},{8,12},{10,14},{12,8},{14,10},{16,20},{18,... | collective-permute-start | bytes 442376 | tf_op jit(solution)/shard_map/ppermute | solution.py:481
  78.9 5.6 %collective-permute-start.35 = (bf16[12,16,384]{2,1,0:T(8,128)(2,1)S(1)}, bf16[12,16,384]{2,1,0:T(8,128)(2,1)S(1)}, u32[]{:S(2)}, u32[]{:S(2)}) collective-permute-start(bf16[12,16,384]{2,1,0:T(8,128)(2,1)S(1)} %get-tuple-element.161.refs_0_), channel_id=1, source_target_pairs={{0,2},{2,0},{4,6},{6,4},{8,10},{10,8},{12,14},{14,12},{16,18},{18,... | collective-permute-start | bytes 442376 | tf_op jit(solution)/shard_map/ppermute | solution.py:477
  84.5 1.5 %collective-permute-start.34 = (bf16[12,16,384]{2,1,0:T(8,128)(2,1)S(1)}, bf16[12,16,384]{2,1,0:T(8,128)(2,1)S(1)}, u32[]{:S(2)}, u32[]{:S(2)}) collective-permute-start(bf16[12,16,384]{2,1,0:T(8,128)(2,1)S(1)} %collective-permute-done.26.refs_0_), channel_id=1, source_target_pairs={{0,2},{2,0},{4,6},{6,4},{8,10},{10,8},{12,14},{14,12},{16,18},{18,... | collective-permute-start | bytes 442376 | tf_op jit(solution)/shard_map/ppermute | solution.py:477
